TPU v7x, 32 devices: a whole 2x2x4 slice. The times are simulated.
32 devices in a mesh: grp: 8 (over z, x), nar: 4 (over y, core).
Axes of the slice: x: 2, y: 2, z: 4, core: 2. Of those that a mesh axis runs over, the one named last changes fastest.
Arguments:
- run_desc: bfloat16 [131072, 256], P(('grp', 'nar')), may hold values from -48 to 48
- ref_desc: bfloat16 [4096, 256], P('nar'), may hold values from -6 to 6
- candidates: int32 [1024, 8], P(('grp', 'nar')), may hold values from 0 to 31, as said below
- live_slots: int32 [1024], P(('grp', 'nar')), may hold values from 1 to 8, as said below
- run_mass: float32 [131072], P(('grp', 'nar')), may hold values from 0.1 to 2
- ref_mass: float32 [4096], P('nar'), may hold values from 0.1 to 2
- ref_start: float32 [4096], P('nar'), may hold values from -62 to 42
Outputs:
- run_potential: float32 [131072], P(('grp', 'nar'))
- ref_potential: float32 [4096], P('nar')
Inputs may be any that keep to these rules, and one draw needn't show every extreme that they name: `candidates`: each row holds 8 different reference block numbers; every reference block is the first entry of some row. `live_slots`: the first run block of each device has all 8 slots live.
All inputs are finite; a program needn't handle non-finite values.
Results may differ from a plain program's by a relative error of at most 0.0003.
Values may be sent and summed in bfloat16 or wider, within the bound.
No kernel may reach another device: no remote copies, remote signals or barrier semaphores. Data moves between devices by JAX's collectives and lax.ppermute only.
A program may use at most 128 MiB of HBM per device.

v0:
```python
import math

import jax
import jax.numpy as jnp
from jax import lax
from jax.sharding import PartitionSpec as P

BLK = 128
TOPC = 8
ITERS = 3


entropic = 0.5
floor_value = -1e30


def combined_all(value, axis, join):
    pieces = jax.tree.map(lambda part: lax.all_gather(part, axis), value)
    head = jax.tree.map(lambda part: part[0], pieces)
    tail = jax.tree.map(lambda part: part[1:], pieces)
    total, _ = lax.scan(lambda total, share: (join(total, share), None), head, tail)
    return total


def merge_pair(earlier, later):
    joined_peak = jnp.maximum(earlier[0], later[0])
    joined_total = earlier[1] * jnp.exp(earlier[0] - joined_peak) + later[1] * jnp.exp(
        later[0] - joined_peak
    )
    return (joined_peak, joined_total)


def shards(run_desc, ref_desc, candidates, live_slots, run_mass, ref_mass, ref_start):
    run_blocks = candidates.shape[0]
    feature_width = run_desc.shape[1]
    run_tiles = run_desc.reshape(run_blocks, BLK, feature_width)
    ref_all = lax.all_gather(ref_desc, "nar", axis=0, tiled=True)
    mass_all, start_all = (
        lax.all_gather(ref_mass, "nar", axis=0, tiled=True),
        lax.all_gather(ref_start, "nar", axis=0, tiled=True),
    )
    ref_blocks = ref_all.shape[0] // BLK
    ref_tiles = ref_all.reshape(ref_blocks, BLK, feature_width)
    log_ref = jnp.log(mass_all).reshape(ref_blocks, BLK)
    log_run = jnp.log(run_mass).reshape(run_blocks, BLK)
    live_mask = jnp.arange(TOPC, dtype=jnp.int32)[None, :] < live_slots[:, None]
    ref_index = jnp.arange(ref_blocks, dtype=jnp.int32)
    nar_index = lax.axis_index("nar")
    own_blocks = ref_blocks // lax.axis_size("nar")

    def slot_cost(slot_index):
        picked = ref_tiles[candidates[:, slot_index]]
        products = jnp.einsum("rid,rjd->rij", run_tiles, picked, preferred_element_type=jnp.float32)
        return -products / math.sqrt(feature_width)

    potential_ref = start_all.reshape(ref_blocks, BLK)
    potential_run = jnp.zeros((run_blocks, BLK), jnp.float32)
    own_ref = jnp.zeros((own_blocks, BLK), jnp.float32)
    for iteration in range(ITERS):
        row_peak = jnp.full((run_blocks, BLK), floor_value, jnp.float32)
        row_total = jnp.zeros((run_blocks, BLK), jnp.float32)
        for row_slot_index in range(TOPC):
            shifted = potential_ref[candidates[:, row_slot_index]]
            row_scores = (shifted[:, None, :] - slot_cost(row_slot_index)) / entropic
            row_slot_peak = jnp.max(row_scores, axis=2)
            row_slot_total = jnp.sum(jnp.exp(row_scores - row_slot_peak[:, :, None]), axis=2)
            row_active = live_mask[:, row_slot_index][:, None]
            row_slot_peak = jnp.where(row_active, row_slot_peak, floor_value)
            row_slot_total = jnp.where(row_active, row_slot_total, 0.0)
            row_peak, row_total = merge_pair((row_peak, row_total), (row_slot_peak, row_slot_total))
        potential_run = entropic * log_run - entropic * (row_peak + jnp.log(row_total))
        slot_peaks = []
        slot_totals = []
        onehots = []
        for column_slot_index in range(TOPC):
            scores = (potential_run[:, :, None] - slot_cost(column_slot_index)) / entropic
            slot_peak = jnp.max(scores, axis=1)
            slot_total = jnp.sum(jnp.exp(scores - slot_peak[:, None, :]), axis=1)
            active = live_mask[:, column_slot_index][:, None]
            slot_peaks.append(jnp.where(active, slot_peak, floor_value))
            slot_totals.append(jnp.where(active, slot_total, 0.0))
            onehots.append(candidates[:, column_slot_index][:, None] == ref_index[None, :])
        dense_peak = jnp.full((ref_blocks, BLK), floor_value, jnp.float32)
        for column_slot_index in range(TOPC):
            spread = jnp.where(
                onehots[column_slot_index][:, :, None],
                slot_peaks[column_slot_index][:, None, :],
                floor_value,
            )
            dense_peak = jnp.maximum(dense_peak, jnp.max(spread, axis=0))
        dense_total = jnp.zeros((ref_blocks, BLK), jnp.float32)
        for column_slot_index in range(TOPC):
            lifted = dense_peak[candidates[:, column_slot_index]]
            scaled = slot_totals[column_slot_index] * jnp.exp(
                slot_peaks[column_slot_index] - lifted
            )
            dense_total = dense_total + jnp.einsum(
                "rb,rj->bj",
                onehots[column_slot_index].astype(jnp.float32),
                scaled,
                precision=lax.Precision.HIGHEST,
            )
        dense_peak, dense_total = (dense_peak, dense_total)
        global_peak, global_total = combined_all(
            (dense_peak, dense_total), ("grp", "nar"), merge_pair
        )
        potential_ref = entropic * log_ref - entropic * (global_peak + jnp.log(global_total))
        own_ref = lax.dynamic_slice_in_dim(potential_ref, nar_index * own_blocks, own_blocks, 0)
    return (potential_run.reshape(-1), own_ref.reshape(-1))


def solution(mesh):
    return jax.shard_map(
        shards,
        mesh=mesh,
        in_specs=(
            P(("grp", "nar"), None),
            P("nar", None),
            P(("grp", "nar"), None),
            P(("grp", "nar")),
            P(("grp", "nar")),
            P("nar"),
            P("nar"),
        ),
        out_specs=(P(("grp", "nar")), P("nar")),
        check_vma=False,
    )
```

profile of v0, /device:TPU:0, one launch (start us, length us, event | category | flops | bytes accessed | tf_op | source)
XLA Modules:
  0.0 447.4 jit_solution(2617935637955885576)
XLA Ops:
  7.9 6.4 %all_gather.40 = f32[4096]{0:T(1024)S(1)} all-gather(f32[1024]{0:T(1024)} %param.19), channel_id=1, replica_groups=mesh['grp'=8,'nar'=4] {'nar'}, dimensions={0}, use_global_device_ids=true | all-gather | bytes 20480 | tf_op jit(solution)/shard_map/all_gather | solution.py:40
  19.9 5.5 %all_gather.39 = f32[4096]{0:T(1024)S(1)} all-gather(f32[1024]{0:T(1024)} %param.18), channel_id=1, replica_groups=mesh['grp'=8,'nar'=4] {'nar'}, dimensions={0}, use_global_device_ids=true | all-gather | bytes 20480 | tf_op jit(solution)/shard_map/all_gather | solution.py:39
  26.5 8.5 %all-gather.8.cloned.1.call-done = bf16[4096,256]{1,0:T(8,128)(2,1)} async-done(((bf16[1024,256]{1,0:T(8,128)(2,1)}), bf16[4096,256]{1,0:T(8,128)(2,1)}) %all-gather.8.cloned.1.call-update) | async-done | bytes 2097168 | tf_op jit(solution)/shard_map/all_gather | solution.py:37
  35.0 3.6 gather_fusion.1
  38.6 3.6 gather_fusion.13
  42.2 3.6 gather_fusion.11
  45.8 3.6 gather_fusion.9
  49.3 3.6 gather_fusion.7
  52.9 3.6 gather_fusion.5
  56.6 3.7 gather_fusion.3
  60.2 3.6 gather_fusion.15
  63.8 2.3 bitcast_reduce_fusion.47
  66.9 1.6 copy-done.31
  70.3 1.6 copy-done.30
  73.6 1.6 copy-done.29
  76.9 1.6 copy-done.28
  80.2 1.6 copy-done.27
  83.5 1.6 copy-done.26
  91.5 5.9 %fusion.71 = (f32[32,128]{1,0:T(8,128)S(1)}, f32[32,128]{1,0:T(8,128)S(1)}, f32[32,128]{1,0:T(8,128)S(1)}, f32[32,128]{1,0:T(8,128)S(1)}, f32[32,128]{1,0:T(8,12...) fusion(f32[32,128,128]{2,1,0:T(8,128)S(1)} %get-tuple-element.201, ...), kind=kLoop, calls=%fused_computation.202 | loop fusion | flops 13598720 | bytes 16957440 | tf_op jit(solution)/shard_map/reduce_sum | solution.py:78
  97.8 7.5 %fusion.73 = (f32[32,128]{1,0:T(8,128)S(1)}, f32[32,128]{1,0:T(8,128)S(1)}, f32[32,128]{1,0:T(8,128)S(1)}, f32[32,128]{1,0:T(8,128)S(1)}, f32[32,128]{1,0:T(8,128)S(1)}, /*index=5*/f32[32,128]{1,0:T(8,128)S(1)}) fusion(f32[32,128,128]{2,1,0:T(8,128)S(1)} %get-tuple-element.203, f32[32,128]{1,0:T(8,128)S(1)} %get-tuple-element.130, ...), kind=kLoop, calls=%fused_computation.206 | loop fusion | flops 12558336 | bytes 12795904 | tf_op jit(solution)/shard_map/reduce_sum | solution.py:78
  114.0 42.3 %all-gather.1 = f32[1024,128]{1,0:T(8,128)S(1)} all-gather(f32[32,128]{1,0:T(8,128)S(1)} %convolution_add_fusion.14), channel_id=3, replica_groups=mesh['grp'=8,'nar'=4] {'grp','nar'}, dimensions={0}, use_global_device_ids=true | all-gather | bytes 540672 | tf_op jit(solution)/shard_map/all_gather | solution.py:18
  156.4 38.1 %all-gather = f32[1024,128]{1,0:T(8,128)S(1)} all-gather(f32[32,128]{1,0:T(8,128)S(1)} %maximum_maximum_fusion.6), channel_id=2, replica_groups=mesh['grp'=8,'nar'=4] {'grp','nar'}, dimensions={0}, use_global_device_ids=true | all-gather | bytes 540672 | tf_op jit(solution)/shard_map/all_gather | solution.py:18
  200.6 2.1 bitcast_reduce_fusion.31
  215.9 5.9 %fusion.39 = (f32[32,128]{1,0:T(8,128)S(1)}, f32[32,128]{1,0:T(8,128)S(1)}, f32[32,128]{1,0:T(8,128)S(1)}, f32[32,128]{1,0:T(8,128)S(1)}, f32[32,128]{1,0:T(8,12...) fusion(f32[32,128,128]{2,1,0:T(8,128)S(1)} %copy-done.23, ...), kind=kLoop, calls=%fused_computation.138 | loop fusion | flops 13598720 | bytes 16957440 | tf_op jit(solution)/shard_map/reduce_sum | solution.py:78
  222.1 7.5 %fusion.41 = (f32[32,128]{1,0:T(8,128)S(1)}, f32[32,128]{1,0:T(8,128)S(1)}, f32[32,128]{1,0:T(8,128)S(1)}, f32[32,128]{1,0:T(8,128)S(1)}, f32[32,128]{1,0:T(8,128)S(1)}, /*index=5*/f32[32,128]{1,0:T(8,128)S(1)}) fusion(f32[32,128,128]{2,1,0:T(8,128)S(1)} %copy-done.2, f32[32,128]{1,0:T(8,128)S(1)} %get-tuple-element.114, ...), kind=kLoop, calls=%fused_computation.142 | loop fusion | flops 12558336 | bytes 12795904 | tf_op jit(solution)/shard_map/reduce_sum | solution.py:78
  238.4 39.6 %all-gather.3 = f32[1024,128]{1,0:T(8,128)S(1)} all-gather(f32[32,128]{1,0:T(8,128)S(1)} %convolution_add_fusion.7), channel_id=5, replica_groups=mesh['grp'=8,'nar'=4] {'grp','nar'}, dimensions={0}, use_global_device_ids=true | all-gather | bytes 540672 | tf_op jit(solution)/shard_map/all_gather | solution.py:18
  278.0 38.1 %all-gather.2 = f32[1024,128]{1,0:T(8,128)S(1)} all-gather(f32[32,128]{1,0:T(8,128)S(1)} %maximum_maximum_fusion.5), channel_id=4, replica_groups=mesh['grp'=8,'nar'=4] {'grp','nar'}, dimensions={0}, use_global_device_ids=true | all-gather | bytes 540672 | tf_op jit(solution)/shard_map/all_gather | solution.py:18
  322.2 2.1 bitcast_reduce_fusion.15
  337.5 5.9 %fusion.7 = (f32[32,128]{1,0:T(8,128)S(1)}, f32[32,128]{1,0:T(8,128)S(1)}, f32[32,128]{1,0:T(8,128)S(1)}, f32[32,128]{1,0:T(8,128)S(1)}, f32[32,128]{1,0:T(8,128...) fusion(f32[32,128,128]{2,1,0:T(8,128)S(1)} %copy-done.24, ...), kind=kLoop, calls=%fused_computation.74 | loop fusion | flops 13598720 | bytes 16957440 | tf_op jit(solution)/shard_map/reduce_sum | solution.py:78
  343.7 7.5 %fusion.9 = (f32[32,128]{1,0:T(8,128)S(1)}, f32[32,128]{1,0:T(8,128)S(1)}, f32[32,128]{1,0:T(8,128)S(1)}, f32[32,128]{1,0:T(8,128)S(1)}, f32[32,128]{1,0:T(8,128)S(1)}, /*index=5*/f32[32,128]{1,0:T(8,128)S(1)}) fusion(f32[32,128,128]{2,1,0:T(8,128)S(1)} %copy-done.3, f32[32,128]{1,0:T(8,128)S(1)} %get-tuple-element.98, ...), kind=kLoop, calls=%fused_computation.78 | loop fusion | flops 12558336 | bytes 12795904 | tf_op jit(solution)/shard_map/reduce_sum | solution.py:78
  360.0 39.4 %all-gather.5 = f32[1024,128]{1,0:T(8,128)S(1)} all-gather(f32[32,128]{1,0:T(8,128)S(1)} %convolution_add_fusion), channel_id=7, replica_groups=mesh['grp'=8,'nar'=4] {'grp','nar'}, dimensions={0}, use_global_device_ids=true | all-gather | bytes 540672 | tf_op jit(solution)/shard_map/all_gather | solution.py:18
  399.5 38.1 %all-gather.4 = f32[1024,128]{1,0:T(8,128)S(1)} all-gather(f32[32,128]{1,0:T(8,128)S(1)} %maximum_maximum_fusion.4), channel_id=6, replica_groups=mesh['grp'=8,'nar'=4] {'grp','nar'}, dimensions={0}, use_global_device_ids=true | all-gather | bytes 540672 | tf_op jit(solution)/shard_map/all_gather | solution.py:18
  (384 shorter events, 93.1 us)
Async XLA Ops:
  7.2 56.7 %copy-start = (bf16[4096,256]{1,0:T(8,128)(2,1)S(1)}, bf16[4096,256]{1,0:T(8,128)(2,1)}, u32[]{:S(2)}) copy-start(bf16[4096,256]{1,0:T(8,128)(2,1)} %param.13) | copy-start | bytes 6291460
  7.2 27.8 %all-gather.8.cloned.1.call-start = ((), (), s32[]{:S(2)}) async-start(), calls=%async_computation | async-start | bytes 2621440 | tf_op jit(solution)/shard_map/all_gather | solution.py:37
  15.3 96.6 %copy-start.42 = (s32[32]{0:T(128)}, s32[32]{0:T(128)S(1)}, u32[]{:S(2)}) copy-start(s32[32]{0:T(128)S(1)} %get-tuple-element.176) | copy-start | bytes 388
  15.3 96.8 %copy-start.39 = (s32[32]{0:T(128)}, s32[32]{0:T(128)S(1)}, u32[]{:S(2)}) copy-start(s32[32]{0:T(128)S(1)} %get-tuple-element.189) | copy-start | bytes 388
  15.3 97.1 %copy-start.36 = (s32[32]{0:T(128)}, s32[32]{0:T(128)S(1)}, u32[]{:S(2)}) copy-start(s32[32]{0:T(128)S(1)} %get-tuple-element.188) | copy-start | bytes 388
  15.3 97.4 %copy-start.33 = (s32[32]{0:T(128)}, s32[32]{0:T(128)S(1)}, u32[]{:S(2)}) copy-start(s32[32]{0:T(128)S(1)} %get-tuple-element.187) | copy-start | bytes 388
  66.2 25.3 %copy-start.7 = (f32[32,128,128]{2,1,0:T(8,128)}, f32[32,128,128]{2,1,0:T(8,128)S(1)}, u32[]{:S(2)}) copy-start(f32[32,128,128]{2,1,0:T(8,128)S(1)} %get-tuple-element.215) | copy-start | bytes 6291460
  66.2 2.3 copy-start.31
  69.5 28.2 %copy-start.1 = (f32[32,128,128]{2,1,0:T(8,128)}, f32[32,128,128]{2,1,0:T(8,128)S(1)}, u32[]{:S(2)}) copy-start(f32[32,128,128]{2,1,0:T(8,128)S(1)} %get-tuple-element.203) | copy-start | bytes 6291460
  69.5 2.3 copy-start.30
  72.8 24.9 %copy-start.4 = (f32[32,128,128]{2,1,0:T(8,128)}, f32[32,128,128]{2,1,0:T(8,128)S(1)}, u32[]{:S(2)}) copy-start(f32[32,128,128]{2,1,0:T(8,128)S(1)} %get-tuple-element.205) | copy-start | bytes 6291460
  72.8 2.3 copy-start.29
  76.1 21.6 %copy-start.10 = (f32[32,128,128]{2,1,0:T(8,128)}, f32[32,128,128]{2,1,0:T(8,128)S(1)}, u32[]{:S(2)}) copy-start(f32[32,128,128]{2,1,0:T(8,128)S(1)} %get-tuple-element.207) | copy-start | bytes 6291460
  76.1 2.3 copy-start.28
  79.4 18.3 %copy-start.13 = (f32[32,128,128]{2,1,0:T(8,128)}, f32[32,128,128]{2,1,0:T(8,128)S(1)}, u32[]{:S(2)}) copy-start(f32[32,128,128]{2,1,0:T(8,128)S(1)} %get-tuple-element.209) | copy-start | bytes 6291460
  79.4 2.3 copy-start.27
  82.7 15.0 %copy-start.16 = (f32[32,128,128]{2,1,0:T(8,128)}, f32[32,128,128]{2,1,0:T(8,128)S(1)}, u32[]{:S(2)}) copy-start(f32[32,128,128]{2,1,0:T(8,128)S(1)} %get-tuple-element.211) | copy-start | bytes 6291460
  82.7 2.3 copy-start.26
  86.0 11.7 %copy-start.19 = (f32[32,128,128]{2,1,0:T(8,128)}, f32[32,128,128]{2,1,0:T(8,128)S(1)}, u32[]{:S(2)}) copy-start(f32[32,128,128]{2,1,0:T(8,128)S(1)} %get-tuple-element.213) | copy-start | bytes 6291460
  86.0 2.3 copy-start.25
  200.6 2.2 copy-start.8
  200.6 2.9 copy-start.20
  222.1 14.1 %copy-start.43 = (s32[32]{0:T(128)S(1)}, s32[32]{0:T(128)}, u32[]{:S(2)}) copy-start(s32[32]{0:T(128)} %copy-done.42) | copy-start | bytes 388
  222.1 14.4 %copy-start.40 = (s32[32]{0:T(128)S(1)}, s32[32]{0:T(128)}, u32[]{:S(2)}) copy-start(s32[32]{0:T(128)} %copy-done.39) | copy-start | bytes 388
  222.1 14.6 %copy-start.37 = (s32[32]{0:T(128)S(1)}, s32[32]{0:T(128)}, u32[]{:S(2)}) copy-start(s32[32]{0:T(128)} %copy-done.36) | copy-start | bytes 388
  229.7 7.4 %copy-start.34 = (s32[32]{0:T(128)S(1)}, s32[32]{0:T(128)}, u32[]{:S(2)}) copy-start(s32[32]{0:T(128)} %copy-done.33) | copy-start | bytes 388
  322.2 2.2 copy-start.9
  322.2 2.9 copy-start.21
  343.7 14.1 %copy-start.44 = (s32[32]{0:T(128)S(1)}, s32[32]{0:T(128)}, u32[]{:S(2)}) copy-start(s32[32]{0:T(128)} %copy-done.42) | copy-start | bytes 388
  343.7 14.4 %copy-start.41 = (s32[32]{0:T(128)S(1)}, s32[32]{0:T(128)}, u32[]{:S(2)}) copy-start(s32[32]{0:T(128)} %copy-done.39) | copy-start | bytes 388
  343.7 14.6 %copy-start.38 = (s32[32]{0:T(128)S(1)}, s32[32]{0:T(128)}, u32[]{:S(2)}) copy-start(s32[32]{0:T(128)} %copy-done.36) | copy-start | bytes 388
  351.3 7.4 %copy-start.35 = (s32[32]{0:T(128)S(1)}, s32[32]{0:T(128)}, u32[]{:S(2)}) copy-start(s32[32]{0:T(128)} %copy-done.33) | copy-start | bytes 388
  (14 other events, 22.0 us)
Sparse Core Ops, SparseCore 0:
  9.6 25.3 all-gather.7
where the time goes:
time: 451 us; the launch traced here: 447 us
  blocking collectives  247 us (55%)
  other arithmetic  88.1 us (20%)
  local copies, waits for them, and re-layouts  69.7 us (15%)
  matrix products  15.5 us (3%)
  between operations  15.5 us (3%)
  waiting for transfers between devices  9.18 us (2%)
    all_gather x6, blocking collectives, combined_all(): pieces = jax.tree.map(lambda part: lax.all_gather(part, axis), value)  236 us
    reduce_sum x6, other arithmetic, shards(): slot_total = jnp.sum(jnp.exp(scores - slot_peak[:, None, :]), axis=1)  40.3 us
    gather x8, local copies, waits for them, and re-layouts, slot_cost(): picked = ref_tiles[candidates[:, slot_index]]  28.9 us
    reduce_sum x24, other arithmetic, shards(): jnp.sum(jnp.exp(row_scores - row_slot_peak[:, :, None]), axis=2)  17.7 us
    reduce_max x16, other arithmetic, shards(): row_slot_peak = jnp.max(row_scores, axis=2)  14 us
    gather x24, local copies, waits for them, and re-layouts, shards(): shifted = potential_ref[candidates[:, row_slot_index]]  13.7 us
    gather x24, local copies, waits for them, and re-layouts, shards(): lifted = dense_peak[candidates[:, column_slot_index]]  13.7 us
    unnamed x90, local copies, waits for them, and re-layouts  13.2 us
  transfers between devices with their start and end apart: 1, of which 1 were waited for; matrix products, arithmetic and copies ran while one was open for 1% of the time, Pallas kernels for 0%

commit v1 on v0

v1 whole, which is shorter than its diff:
```python
import functools
import math

import jax
import jax.numpy as jnp
from jax import lax
from jax.experimental import pallas as pl
from jax.experimental.pallas import tpu as pltpu
from jax.sharding import PartitionSpec as P

BLK = 128
TOPC = 8
PAIRS = TOPC // 2
LOG2E = math.log2(math.e)
FLOOR = -1e30
VMEM_LIMIT = 56 * 1024 * 1024

vmem = pl.BlockSpec(memory_space=pltpu.VMEM)
smem = pl.BlockSpec(memory_space=pltpu.SMEM)


def group_size(run_blocks):
    for size in (4, 2):
        if run_blocks % size == 0:
            return size
    return 1


def by_groups(group_pairs, run_blocks, body):
    size = group_size(run_blocks)

    def step(group, carry):
        pairs = group_pairs[group]
        for count in range(1, PAIRS + 1):

            @pl.when(pairs == count)
            def _():
                body(count, [group * size + k for k in range(size)])

        return carry

    lax.fori_loop(0, run_blocks // size, step, 0)


def rows_of(block):
    return pl.ds(pl.multiple_of(block * BLK, BLK), BLK)


def pair_row(table, eff, place, pair):
    left = table[pl.ds(eff[place, 2 * pair], 1), :]
    right = table[pl.ds(eff[place, 2 * pair + 1], 1), :]
    return jnp.concatenate([left, right], axis=1)


def halves(join, tile):
    return join(tile[:, :BLK], tile[:, BLK:])


def first_kernel(group_pairs, order, cand, eff, run, ref, pot, log_mass, slot_ref, scores, lse, rows):
    run_blocks = order.shape[0]
    ref_blocks = lse.shape[0]
    scale = 2.0 * LOG2E / math.sqrt(run.shape[1])

    def body(pairs, places):
        for place in places:
            block = order[place]
            own = run[rows_of(block), :]
            peak = None
            for pair in range(pairs):
                both = jnp.concatenate(
                    [ref[rows_of(cand[place, 2 * pair + half]), :] for half in range(2)], axis=0
                )
                tile = lax.dot_general(
                    own, both, (((1,), (1,)), ((), ())), preferred_element_type=jnp.float32
                )
                tile = tile * scale
                scores[place, :, 2 * BLK * pair : 2 * BLK * (pair + 1)] = tile
                top = halves(jnp.maximum, tile + pair_row(pot, eff, place, pair))
                peak = top if peak is None else jnp.maximum(peak, top)
            peak = jnp.max(peak, axis=1, keepdims=True)
            total = None
            for pair in range(pairs):
                tile = scores[place, :, 2 * BLK * pair : 2 * BLK * (pair + 1)]
                part = halves(
                    jnp.add, jnp.exp2(tile + (pair_row(pot, eff, place, pair) - peak))
                )
                total = part if total is None else total + part
            total = jnp.sum(total, axis=1, keepdims=True)
            potential = log_mass[rows_of(block), :1] - (peak + jnp.log2(total))
            for pair in range(pairs):
                tile = scores[place, :, 2 * BLK * pair : 2 * BLK * (pair + 1)] + potential
                top = jnp.max(tile, axis=0, keepdims=True)
                row = top + jnp.log2(jnp.sum(jnp.exp2(tile - top), axis=0, keepdims=True))
                rows[pl.ds(place * TOPC + 2 * pair, 1), :] = row[:, :BLK]
                rows[pl.ds(place * TOPC + 2 * pair + 1, 1), :] = row[:, BLK:]

    by_groups(group_pairs, run_blocks, body)

    def join(block, carry):
        picked = jnp.where(slot_ref[...] == block, rows[...], FLOOR)
        top = jnp.max(picked, axis=0, keepdims=True)
        total = jnp.sum(jnp.exp2(picked - top), axis=0, keepdims=True)
        lse[pl.ds(block, 1), :] = top + jnp.log2(total)
        return carry

    lax.fori_loop(0, ref_blocks, join, 0)


def second_kernel(group_pairs, order, eff, scores, pot, log_mass, onehot, weights, peaks, sums, rows):
    run_blocks = order.shape[0]
    rows[...] = jnp.zeros_like(rows)

    def body(pairs, places):
        for place in places:
            block = order[place]
            peak = None
            for pair in range(pairs):
                tile = scores[place, :, 2 * BLK * pair : 2 * BLK * (pair + 1)]
                top = halves(jnp.maximum, tile + pair_row(pot, eff, place, pair))
                peak = top if peak is None else jnp.maximum(peak, top)
            peak = jnp.max(peak, axis=1, keepdims=True)
            peaks[rows_of(place), :] = jnp.broadcast_to(peak, (BLK, BLK))
            total = None
            for pair in range(pairs):
                tile = scores[place, :, 2 * BLK * pair : 2 * BLK * (pair + 1)]
                weight = jnp.exp2(tile + (pair_row(pot, eff, place, pair) - peak))
                weights[place, :, 2 * BLK * pair : 2 * BLK * (pair + 1)] = weight
                part = halves(jnp.add, weight)
                total = part if total is None else total + part
            total = jnp.sum(total, axis=1, keepdims=True)
            factor = jnp.exp2(log_mass[rows_of(block), :1] - jnp.log2(total))
            for pair in range(pairs):
                weight = weights[place, :, 2 * BLK * pair : 2 * BLK * (pair + 1)]
                row = jnp.sum(weight * factor, axis=0, keepdims=True)
                rows[pl.ds(place * TOPC + 2 * pair, 1), :] = row[:, :BLK]
                rows[pl.ds(place * TOPC + 2 * pair + 1, 1), :] = row[:, BLK:]

    by_groups(group_pairs, run_blocks, body)
    sums[...] = jnp.dot(
        onehot[...],
        rows[...],
        precision=lax.Precision.HIGHEST,
        preferred_element_type=jnp.float32,
    )


def third_kernel(group_pairs, order, eff, weights, peaks, gain, log_mass, onehot, out, sums, rows):
    run_blocks = order.shape[0]
    rows[...] = jnp.zeros_like(rows)
    diagonal = lax.broadcasted_iota(jnp.int32, (BLK, BLK), 0) == lax.broadcasted_iota(
        jnp.int32, (BLK, BLK), 1
    )

    def body(pairs, places):
        for place in places:
            block = order[place]
            total = None
            for pair in range(pairs):
                weight = weights[place, :, 2 * BLK * pair : 2 * BLK * (pair + 1)]
                part = halves(jnp.add, weight * pair_row(gain, eff, place, pair))
                total = part if total is None else total + part
            total = jnp.sum(total, axis=1, keepdims=True)
            log_factor = log_mass[rows_of(block), :1] - jnp.log2(total)
            factor = jnp.exp2(log_factor)
            potential = log_factor - peaks[rows_of(place), :1]
            out[pl.ds(block, 1), :] = jnp.sum(
                jnp.where(diagonal, potential * (0.5 / LOG2E), 0.0), axis=0, keepdims=True
            )
            for pair in range(pairs):
                weight = weights[place, :, 2 * BLK * pair : 2 * BLK * (pair + 1)]
                row = jnp.sum(weight * factor, axis=0, keepdims=True)
                rows[pl.ds(place * TOPC + 2 * pair, 1), :] = row[:, :BLK]
                rows[pl.ds(place * TOPC + 2 * pair + 1, 1), :] = row[:, BLK:]

    by_groups(group_pairs, run_blocks, body)
    sums[...] = jnp.dot(
        onehot[...],
        rows[...],
        precision=lax.Precision.HIGHEST,
        preferred_element_type=jnp.float32,
    )


def call(kernel, ins, outs, scratch):
    return pl.pallas_call(
        kernel,
        in_specs=ins,
        out_specs=[vmem] * len(outs),
        out_shape=outs,
        scratch_shapes=scratch,
        compiler_params=pltpu.CompilerParams(vmem_limit_bytes=VMEM_LIMIT),
    )


def log_sum(parts, axis):
    top = jnp.max(parts, axis=axis, keepdims=True)
    total = jnp.sum(jnp.exp2(parts - top), axis=axis, keepdims=True)
    return jnp.squeeze(top + jnp.log2(total), axis)


class Links:
    def __init__(self, groups, width):
        self.width = width
        self.devices = groups * width
        self.core = lax.axis_index("nar") % 2

    def swap(self, value, mask):
        pairs = [(k, k ^ mask) for k in range(self.devices)]
        return lax.ppermute(value, ("grp", "nar"), pairs)

    def half(self, value, which):
        count = value.shape[0] // 2
        return jnp.where(which == 0, value[:count], value[count:])

    def whole(self, value):
        other = self.swap(value, 1)
        low = jnp.where(self.core == 0, value, other)
        high = jnp.where(self.core == 0, other, value)
        return jnp.concatenate([low, high], axis=0)

    def reduce_half(self, value, join):
        kept = self.half(value, self.core)
        got = self.swap(self.half(value, 1 - self.core), 1)
        kept = join(jnp.stack([kept, got]), 0)
        chips = self.devices // 2
        sent = jnp.broadcast_to(kept[None], (chips,) + kept.shape)
        groups = [list(range(c, self.devices, 2)) for c in range(2)]
        parts = lax.all_to_all(
            sent, ("grp", "nar"), 0, 0, axis_index_groups=groups, tiled=True
        )
        return join(parts, 0)

    def reduce_own(self, value, join):
        own = value.shape[0] // self.width
        pieces = value.reshape(1, self.width, own, BLK)
        sent = jnp.broadcast_to(pieces, (self.devices // self.width,) + pieces.shape[1:])
        parts = lax.all_to_all(
            sent.reshape(self.devices, own, BLK), ("grp", "nar"), 0, 0, tiled=True
        )
        return join(parts, 0)

    def gather(self, value):
        held = {0: value}
        mask = self.width // 2
        while mask:
            held.update({key ^ mask: self.swap(part, mask) for key, part in list(held.items())})
            mask //= 2
        return [held[key] for key in range(self.width)]

    def arrange(self, parts):
        me = lax.axis_index("nar")
        bit = 1
        parts = list(parts)
        while bit < self.width:
            flip = (me & bit) != 0
            parts = [
                jnp.where(flip, parts[key ^ bit], parts[key]) for key in range(self.width)
            ]
            bit *= 2
        return jnp.concatenate(parts, axis=0)


def shards(run_desc, ref_desc, candidates, live_slots, run_mass, ref_mass, ref_start):
    run_blocks = candidates.shape[0]
    links = Links(lax.axis_size("grp"), lax.axis_size("nar"))
    own_blocks = ref_desc.shape[0] // BLK
    ref_blocks = own_blocks * links.width
    depth = run_desc.shape[1]
    f32 = jnp.float32

    small = jnp.concatenate(
        [
            (2.0 * LOG2E) * ref_start.reshape(1, own_blocks, BLK),
            jnp.log2(ref_mass).reshape(1, own_blocks, BLK),
        ]
    )
    small_all = links.gather(small)
    pot = links.arrange([part[0] for part in small_all])
    log_ref = links.arrange([part[1] for part in small_all])
    ref_all = links.arrange(links.gather(ref_desc))

    size = group_size(run_blocks)
    pairs = (live_slots + 1) // 2
    blocks = jnp.arange(run_blocks, dtype=jnp.int32)
    rank_key = pairs * run_blocks - blocks
    place = jnp.sum((rank_key[None, :] > rank_key[:, None]).astype(jnp.int32), axis=1)
    moved = place[None, :] == blocks[:, None]
    order = jnp.sum(jnp.where(moved, blocks[None, :], 0), axis=1)
    cand = jnp.sum(jnp.where(moved[:, :, None], candidates[None], 0), axis=1)
    live = jnp.sum(jnp.where(moved, live_slots[None, :], 0), axis=1)
    group_pairs = ((live + 1) // 2)[::size]
    slots = jnp.arange(TOPC, dtype=jnp.int32)
    eff = jnp.where(slots[None, :] < live[:, None], cand, ref_blocks)
    tiles = run_blocks * TOPC
    slot_ref = jnp.broadcast_to(eff.reshape(tiles, 1), (tiles, BLK))
    onehot = (
        eff.reshape(1, tiles) == jnp.arange(ref_blocks, dtype=jnp.int32)[:, None]
    ).astype(f32)
    log_mass = jnp.broadcast_to(
        jnp.log2(run_mass)[:, None], (run_blocks * BLK, BLK)
    )

    def padded(table):
        return jnp.concatenate([table, jnp.full((8, BLK), FLOOR, f32)], axis=0)

    rows = pltpu.VMEM((tiles, BLK), f32)
    score_shape = jax.ShapeDtypeStruct((run_blocks, BLK, TOPC * BLK), f32)
    table_shape = jax.ShapeDtypeStruct((ref_blocks, BLK), f32)
    rep_shape = jax.ShapeDtypeStruct((run_blocks * BLK, BLK), f32)
    scores, lse = call(
        first_kernel, [smem] * 4 + [vmem] * 5, [score_shape, table_shape], [rows]
    )(group_pairs, order, cand, eff, run_desc, ref_all, padded(pot), log_mass, slot_ref)

    log_half = links.half(log_ref, links.core)
    half = log_half - links.reduce_half(lse, log_sum)
    pot = links.whole(half)

    weights, peaks, sums = call(
        second_kernel, [smem] * 3 + [vmem] * 4, [score_shape, rep_shape, table_shape], [rows]
    )(group_pairs, order, eff, scores, padded(pot), log_mass, onehot)
    log_gain_half = log_half - jnp.log2(links.reduce_half(sums, jnp.sum))
    log_gain = links.whole(log_gain_half)
    pot = pot + log_gain
    gain = jnp.concatenate([jnp.exp2(log_gain), jnp.zeros((8, BLK), f32)], axis=0)

    run_pot, sums = call(
        third_kernel,
        [smem] * 3 + [vmem] * 5,
        [jax.ShapeDtypeStruct((run_blocks, BLK), f32), table_shape],
        [rows],
    )(group_pairs, order, eff, weights, peaks, gain, log_mass, onehot)
    total = links.reduce_own(sums, jnp.sum)
    start = lax.axis_index("nar") * own_blocks

    def mine(table):
        return lax.dynamic_slice_in_dim(table, start, own_blocks, 0)

    own = (mine(log_ref) + mine(pot) - mine(log_gain) - jnp.log2(total)) * (0.5 / LOG2E)
    return run_pot.reshape(-1), own.reshape(-1)


def solution(mesh):
    return jax.shard_map(
        shards,
        mesh=mesh,
        in_specs=(
            P(("grp", "nar"), None),
            P("nar", None),
            P(("grp", "nar"), None),
            P(("grp", "nar")),
            P(("grp", "nar")),
            P("nar"),
            P("nar"),
        ),
        out_specs=(P(("grp", "nar")), P("nar")),
        check_vma=False,
    )
```

time: 451 us -> 124 us (0.27)
  blocking collectives: 247 us -> 23.9 us
  other arithmetic: 88.1 us -> 15.4 us
  local copies, waits for them, and re-layouts: 69.7 us -> 5.43 us
  Pallas kernels: 0 us -> 50.7 us
  matrix products: 15.5 us -> 0 us
  between operations: 15.5 us -> 0.78 us
  waiting for transfers between devices: 9.18 us -> 19.8 us
  starting transfers between devices: 0.04 us -> 6.43 us
    all_gather x8 -> x0, blocking collectives: 247 us -> none  [the longest x6 236 us: combined_all(): pieces = jax.tree.map(lambda part: lax.all_gather(part, axis), value)]
    gather x56 -> x0, local copies, waits for them, and re-layouts: 56.3 us -> none  [the longest x8 28.9 us: slot_cost(): picked = ref_tiles[candidates[:, slot_index]]]
    reduce_sum x30 -> x8, other arithmetic: 57.9 us -> 3.59 us  [the longest x1 1.3 us: shards(): cand = jnp.sum(jnp.where(moved[:, :, None], candidates[None], 0), axis=1)]
    pallas_call x0 -> x3, Pallas kernels: none -> 50.7 us  [the longest x1 21.4 us: shards(): call(first_kernel, [smem] * 4 + [vmem] * 5, [score_shape, table_shape], [...]
    all_to_all x0 -> x2, blocking collectives: none -> 23.9 us  [reduce_half(): lax.all_to_all(sent, ('grp', 'nar'), 0, 0, axis_index_groups=groups, tile...]
    reduce_max x43 -> x1, other arithmetic: 22.3 us -> 0.02 us  [log_sum(): top = jnp.max(parts, axis=axis, keepdims=True)]
    dot_general x32 -> x0, matrix products: 15.5 us -> none  [the longest x8 8.93 us: slot_cost(): jnp.einsum('rid,rjd->rij', run_tiles, picked, preferred_element_type=jnp....]
    unnamed x90 -> x6, local copies, waits for them, and re-layouts: 13.2 us -> 0.01 us
  transfers between devices with their start and end apart: 1 -> 11, of which waited for: 1 -> 7; matrix products, arithmetic and copies ran while one was open for 1% -> 7% of each run, Pallas kernels for 0% -> 0%
where the time goes in v1:
time: 124 us; the launch traced here: 122 us
  Pallas kernels  50.7 us (41%)
  blocking collectives  23.9 us (19%)
  waiting for transfers between devices  19.8 us (16%)
  other arithmetic  15.4 us (12%)
  starting transfers between devices  6.43 us (5%)
  local copies, waits for them, and re-layouts  5.43 us (4%)
    all_to_all x2, blocking collectives, reduce_half(): lax.all_to_all(sent, ('grp', 'nar'), 0, 0, axis_index_groups=groups, tile...  23.9 us
    pallas_call x1, Pallas kernels, shards(): call(first_kernel, [smem] * 4 + [vmem] * 5, [score_shape, table_shape], [...  21.4 us
    pallas_call x1, Pallas kernels, shards(): call(second_kernel, [smem] * 3 + [vmem] * 4, [score_shape, rep_shape, tab...  18.3 us
    ppermute x10, waiting for transfers between devices, swap(): return lax.ppermute(value, ('grp', 'nar'), pairs)  11.6 us
    pallas_call x1, Pallas kernels, shards(): call(third_kernel, [smem] * 3 + [vmem] * 5, [jax.ShapeDtypeStruct((run_bl...  11 us
    all_to_all x1, waiting for transfers between devices, reduce_own(): lax.all_to_all(sent.reshape(self.devices, own, BLK), ('grp', 'nar'), 0, 0...  8.23 us
    ppermute x10, starting transfers between devices, swap(): return lax.ppermute(value, ('grp', 'nar'), pairs)  3.86 us
    all_to_all x1, starting transfers between devices, reduce_own(): lax.all_to_all(sent.reshape(self.devices, own, BLK), ('grp', 'nar'), 0, 0...  2.57 us
  transfers between devices with their start and end apart: 11, of which 7 were waited for; matrix products, arithmetic and copies ran while one was open for 7% of the time, Pallas kernels for 0%

profile of v1, /device:TPU:0, one launch (start us, length us, event | category | flops | bytes accessed | tf_op | source)
XLA Modules:
  0.0 122.4 jit_solution(9442847191150685565)
XLA Ops:
  0.6 0.7 multiply_bitcast_fusion
  1.8 2.6 %collective-permute-start.3 = (f32[2,8,128]{2,1,0:T(8,128)S(1)}, f32[2,8,128]{2,1,0:T(8,128)S(1)}, u32[]{:S(2)}, u32[]{:S(2)}) collective-permute-start(f32[2,8,128]{2,1,0:T(8,128)S(1)} %pad_maximum_fusion.3), channel_id=1, source_target_pairs={{0,2},{1,3},{2,0},{3,1},{4,6},{5,7},{6,4},{7,5},{8,10},{9,11},{10,... | collective-permute-start | bytes 24584 | tf_op jit(solution)/shard_map/ppermute | solution.py:209
  4.6 0.7 iota_subtract_fusion
  5.4 1.3 %select_reduce_fusion.1 = (s32[32]{0:T(128)}, s32[32]{0:T(128)S(1)}) fusion(s32[32]{0:T(128)S(1)} %convert_reduce_fusion, s32[32]{0:T(128)} %param.10), kind=kLoop, calls=%fused_computation.31 | loop fusion | flops 5056 | bytes 512 | tf_op jit(solution)/shard_map/reduce_sum | solution.py:288
  6.7 1.3 %select_reduce_fusion.cand = s32[32,8]{1,0:T(8,128)S(1)} fusion(s32[32,8]{0,1:T(8,128)} %param.9, pred[32,32]{1,0:T(8,128)(4,1)S(1)} %iota_compare_fusion.2), kind=kLoop, calls=%fused_computation.10 | loop fusion | flops 16128 | bytes 3072 | tf_op jit(solution)/shard_map/reduce_sum | solution.py:289
  8.1 0.7 log_multiply_fusion
  9.4 0.7 slice.41.group_pairs
  10.2 0.7 bitcast_select_fusion.5
  10.9 0.7 constant_dynamic-update-slice_fusion.3
  11.6 7.0 %collective-permute-done = bf16[1024,256]{1,0:T(8,128)(2,1)S(1)} collective-permute-done((bf16[1024,256]{1,0:T(8,128)(2,1)}, bf16[1024,256]{1,0:T(8,128)(2,1)S(1)}, u32[]{:S(2)}, u32[]{:S(2)}) %collective-permute-start) | collective-permute-done | bytes 524320 | tf_op jit(solution)/shard_map/ppermute | solution.py:209
  18.6 0.7 constant_dynamic-update-slice_fusion.2
  19.3 0.7 constant_dynamic-update-slice_fusion.1
  20.5 1.2 %broadcast_select_fusion.7 = (bf16[1024,256]{1,0:T(8,128)(2,1)S(1)}, bf16[1024,256]{1,0:T(8,128)(2,1)S(1)}, bf16[1024,256]{1,0:T(8,128)(2,1)S(1)}, bf16[1024,256]{1,0:T(8,128)(2,1)S(1)}) fusion(pred[]{:T(512)S(6)} %ne.40, bf16[1024,256]{1,0:T(8,128)(2,1)S(1)} %collective-permute-done.1, bf16[1024,256]{1,0:T(8,128)(2,1)S(1)} %collective-permute-done, ...), kind=kLoop, calls=%fused_computation.8 | loop fusion | flops 2097152 | bytes 4194306 | tf_op jit(solution)/shard_map/jit(_where)/select_n | solution.py:257
  21.7 1.5 %pad_maximum_fusion.ref = bf16[4096,256]{1,0:T(8,128)(2,1)} fusion(bf16[1024,256]{1,0:T(8,128)(2,1)S(1)} %get-tuple-element.21, bf16[1024,256]{1,0:T(8,128)(2,1)S(1)} %get-tuple-element.20, bf16[1024,256]{1,0:T(8,128)(2,1)S(1)} %get-tuple-element.19, bf16[1024,256]{1,0:T(8,128)(2,1)S(1)} %get-tuple-element.18), kind=kLoop, calls=%fused_computation | loop fusion | flops 8388608 | bytes 4194304 | tf_op jit(solution)/shard_map/concatenate | solution.py:260
  23.2 0.8 broadcast_in_dim.95.slot_ref
  24.0 1.9 %broadcast_in_dim.94.log_mass = f32[4096,128]{1,0:T(8,128)} broadcast(f32[4096]{0:T(1024)S(1)} %log_multiply_fusion), dimensions={0} | broadcast | bytes 2113536 | tf_op jit(solution)/shard_map/broadcast_in_dim | solution.py:299
  25.9 21.4 %shard_map.86 = (f32[32,128,1024]{2,1,0:T(8,128)}, f32[32,128]{1,0:T(8,128)}) custom-call(s32[8]{0:T(128)} %slice.41.group_pairs, s32[32]{0:T(128)} %get-tuple-element.16.order, s32[32,8]{1,0:T(8,128)} %copy-done.1, s32[32,8]{1,0:T(8,128)} %copy-done, bf16[4096,256]{1,0:T(8,128)(2,1)} %run.1, bf16[4096,256]{1,0:T(8,128)(2,1)} %pad_maximum_fusion.ref, ...), custom_call_target="tpu_custom_call" | custom-call | tf_op jit(solution)/shard_map/pallas_call | solution.py:310
  47.3 0.7 slice_select_fusion.1
  48.0 1.2 collective-permute-done.6
  49.2 0.7 fusion.19
  49.9 13.2 %all_to_all.15 = f32[16,16,128]{2,1,0:T(8,128)S(1)} all-to-all(f32[16,16,128]{2,1,0:T(8,128)S(1)} %broadcast_in_dim.96), channel_id=1, replica_groups={{0,2,4,6,8,10,12,14,16,18,20,22,24,26,28,30},{1,3,5,7,9,11,13,15,17,19,..., dimensions={0} | all-to-all | bytes 262144 | tf_op jit(solution)/shard_map/all_to_all | solution.py:228
  65.1 18.3 %shard_map.87 = (f32[32,128,1024]{2,1,0:T(8,128)}, f32[4096,128]{1,0:T(8,128)}, f32[32,128]{1,0:T(8,128)}) custom-call(s32[8]{0:T(128)} %slice.41.group_pairs, s32[32]{0:T(128)} %get-tuple-element.16.order, s32[32,8]{1,0:T(8,128)} %copy-done, f32[32,128,1024]{2,1,0:T(8,128)} %get-tuple-element.9.scores, f32[40,128]{1,0:T(8,128)} %pad_maximum_fusion.1.pot, ...), custom_call_target="tpu_custom_call" | custom-call | tf_op jit(solution)/shard_map/pallas_call | solution.py:318
  83.4 0.7 slice_select_fusion
  84.1 1.2 collective-permute-done.8
  85.3 0.7 select_add_fusion
  86.0 10.7 %all_to_all.16 = f32[16,16,128]{2,1,0:T(8,128)S(1)} all-to-all(f32[16,16,128]{2,1,0:T(8,128)S(1)} %broadcast_in_dim.97), channel_id=1, replica_groups={{0,2,4,6,8,10,12,14,16,18,20,22,24,26,28,30},{1,3,5,7,9,11,13,15,17,19,..., dimensions={0} | all-to-all | bytes 262144 | tf_op jit(solution)/shard_map/all_to_all | solution.py:228
  96.8 1.2 collective-permute-done.9
  98.6 11.0 %shard_map.88 = (f32[32,128]{1,0:T(8,128)}, f32[32,128]{1,0:T(8,128)}) custom-call(s32[8]{0:T(128)} %slice.41.group_pairs, s32[32]{0:T(128)} %get-tuple-element.16.order, s32[32,8]{1,0:T(8,128)} %copy-done, f32[32,128,1024]{2,1,0:T(8,128)} %get-tuple-element.11.weights, f32[4096,128]{1,0:T(8,128)} %get-tuple-element.12.peaks, f32[40,128]{1,0:T(8,128)} %concatenate.38.gain, ...), custom_call_target="tpu_custom_call" | custom-call | tf_op jit(solution)/shard_map/pallas_call | solution.py:326
  109.6 1.4 %broadcast_in_dim.99 = f32[8,4,8,128]{3,2,1,0:T(8,128)} broadcast(f32[4,8,128]{2,1,0:T(8,128)} %bitcast.83), dimensions={1,2,3} | broadcast | bytes 147456 | tf_op jit(solution)/shard_map/broadcast_in_dim | solution.py:236
  111.0 2.6 %all-to-all-start.2 = ((f32[32,8,128]{2,1,0:T(8,128)}), f32[32,8,128]{2,1,0:T(8,128)S(1)}, u32[]{:S(2)}, u32[]{:S(2)}) async-start(f32[32,8,128]{2,1,0:T(8,128)} %bitcast.14), calls=%async_computation.2 | async-start | bytes 262144 | tf_op jit(solution)/shard_map/all_to_all | solution.py:237
  113.6 8.2 %all-to-all-done.2 = f32[32,8,128]{2,1,0:T(8,128)S(1)} async-done(((f32[32,8,128]{2,1,0:T(8,128)}), f32[32,8,128]{2,1,0:T(8,128)S(1)}, u32[]{:S(2)}, u32[]{:S(2)}) %all-to-all-start.2) | async-done | bytes 131104 | tf_op jit(solution)/shard_map/all_to_all | solution.py:237
  121.8 0.6 fusion.13
  (45 shorter events, 4.8 us)
Async XLA Ops:
  1.3 8.8 %collective-permute-start.5 = (f32[2,8,128]{2,1,0:T(8,128)S(1)}, f32[2,8,128]{2,1,0:T(8,128)S(1)}, u32[]{:S(2)}, u32[]{:S(2)}) collective-permute-start(f32[2,8,128]{2,1,0:T(8,128)S(1)} %pad_maximum_fusion.3), channel_id=1, source_target_pairs={{0,1},{1,0},{2,3},{3,2},{4,5},{5,4},{6,7},{7,6},{8,9},{9,8},{10,11... | collective-permute-start | bytes 24584 | tf_op jit(solution)/shard_map/ppermute | solution.py:209
  1.8 7.1 %collective-permute-start.3 = (f32[2,8,128]{2,1,0:T(8,128)S(1)}, f32[2,8,128]{2,1,0:T(8,128)S(1)}, u32[]{:S(2)}, u32[]{:S(2)}) collective-permute-start(f32[2,8,128]{2,1,0:T(8,128)S(1)} %pad_maximum_fusion.3), channel_id=1, source_target_pairs={{0,2},{1,3},{2,0},{3,1},{4,6},{5,7},{6,4},{7,5},{8,10},{9,11},{10,... | collective-permute-start | bytes 24584 | tf_op jit(solution)/shard_map/ppermute | solution.py:209
  4.4 14.2 %collective-permute-start = (bf16[1024,256]{1,0:T(8,128)(2,1)}, bf16[1024,256]{1,0:T(8,128)(2,1)S(1)}, u32[]{:S(2)}, u32[]{:S(2)}) collective-permute-start(bf16[1024,256]{1,0:T(8,128)(2,1)} %param.8), channel_id=1, source_target_pairs={{0,2},{1,3},{2,0},{3,1},{4,6},{5,7},{6,4},{7,5},{8,10},{9,11},{10,... | collective-permute-start | bytes 1572872 | tf_op jit(solution)/shard_map/ppermute | solution.py:209
  4.5 15.5 %collective-permute-start.2 = (bf16[1024,256]{1,0:T(8,128)(2,1)}, bf16[1024,256]{1,0:T(8,128)(2,1)S(1)}, u32[]{:S(2)}, u32[]{:S(2)}) collective-permute-start(bf16[1024,256]{1,0:T(8,128)(2,1)} %param.8), channel_id=1, source_target_pairs={{0,1},{1,0},{2,3},{3,2},{4,5},{5,4},{6,7},{7,6},{8,9},{9,8},{10,11... | collective-permute-start | bytes 1572872 | tf_op jit(solution)/shard_map/ppermute | solution.py:209
  8.0 15.2 %copy-start.1 = (s32[32,8]{1,0:T(8,128)}, s32[32,8]{1,0:T(8,128)S(1)}, u32[]{:S(2)}) copy-start(s32[32,8]{1,0:T(8,128)S(1)} %select_reduce_fusion.cand) | copy-start | bytes 3076
  8.1 15.1 %copy-start = (s32[32,8]{1,0:T(8,128)}, s32[32,8]{1,0:T(8,128)S(1)}, u32[]{:S(2)}) copy-start(s32[32,8]{1,0:T(8,128)S(1)} %fusion.6.eff) | copy-start | bytes 3076
  8.9 1.3 %collective-permute-start.4 = (f32[2,8,128]{2,1,0:T(8,128)S(1)}, f32[2,8,128]{2,1,0:T(8,128)S(1)}, u32[]{:S(2)}, u32[]{:S(2)}) collective-permute-start(f32[2,8,128]{2,1,0:T(8,128)S(1)} %collective-permute-done.3), channel_id=1, source_target_pairs={{0,1},{1,0},{2,3},{3,2},{4,5},{5,4},{6,7},{7,6},{8,9},{9,8},{10,11... | collective-permute-start | bytes 24584 | tf_op jit(solution)/shard_map/ppermute | solution.py:209
  18.6 1.9 %collective-permute-start.1 = (bf16[1024,256]{1,0:T(8,128)(2,1)S(1)}, bf16[1024,256]{1,0:T(8,128)(2,1)S(1)}, u32[]{:S(2)}, u32[]{:S(2)}) collective-permute-start(bf16[1024,256]{1,0:T(8,128)(2,1)S(1)} %collective-permute-done), channel_id=1, source_target_pairs={{0,1},{1,0},{2,3},{3,2},{4,5},{5,4},{6,7},{7,6},{8,9},{9,8},{10,11... | collective-permute-start | bytes 1572872 | tf_op jit(solution)/shard_map/ppermute | solution.py:209
  20.0 3.3 %copy-start.2 = (f32[40,128]{1,0:T(8,128)}, f32[40,128]{1,0:T(8,128)S(1)}, u32[]{:S(2)}) copy-start(f32[40,128]{1,0:T(8,128)S(1)} %constant_dynamic-update-slice_fusion.pot) | copy-start | bytes 61444
  48.0 1.2 collective-permute-start.6
  63.2 1.2 %collective-permute-start.7 = (f32[16,128]{1,0:T(8,128)S(1)}, f32[16,128]{1,0:T(8,128)S(1)}, u32[]{:S(2)}, u32[]{:S(2)}) collective-permute-start(f32[16,128]{1,0:T(8,128)S(1)} %add_subtract_fusion), channel_id=1, source_target_pairs={{0,1},{1,0},{2,3},{3,2},{4,5},{5,4},{6,7},{7,6},{8,9},{9,8},{10,11... | collective-permute-start | bytes 24584 | tf_op jit(solution)/shard_map/ppermute | solution.py:209
  84.1 1.2 collective-permute-start.8
  96.7 1.2 %collective-permute-start.9 = (f32[16,128]{1,0:T(8,128)S(1)}, f32[16,128]{1,0:T(8,128)S(1)}, u32[]{:S(2)}, u32[]{:S(2)}) collective-permute-start(f32[16,128]{1,0:T(8,128)S(1)} %multiply_subtract_fusion), channel_id=1, source_target_pairs={{0,1},{1,0},{2,3},{3,2},{4,5},{5,4},{6,7},{7,6},{8,9},{9,8},{10,11... | collective-permute-start | bytes 24584 | tf_op jit(solution)/shard_map/ppermute | solution.py:209
  111.0 10.8 %all-to-all-start.2 = ((f32[32,8,128]{2,1,0:T(8,128)}), f32[32,8,128]{2,1,0:T(8,128)S(1)}, u32[]{:S(2)}, u32[]{:S(2)}) async-start(f32[32,8,128]{2,1,0:T(8,128)} %bitcast.14), calls=%async_computation.2 | async-start | bytes 262144 | tf_op jit(solution)/shard_map/all_to_all | solution.py:237

commit v2 on v1

--- a/solution.py
+++ b/solution.py
@@ -13,7 +13,7 @@
 PAIRS = TOPC // 2
 LOG2E = math.log2(math.e)
 FLOOR = -1e30
-VMEM_LIMIT = 56 * 1024 * 1024
+VMEM_LIMIT = 8 * 1024 * 1024
 
 vmem = pl.BlockSpec(memory_space=pltpu.VMEM)
 smem = pl.BlockSpec(memory_space=pltpu.SMEM)
@@ -181,54 +181,51 @@
     )
 
 
-def call(kernel, ins, outs, scratch):
+def call(kernel, ins, outs, scratch, aliases={}):
     return pl.pallas_call(
         kernel,
         in_specs=ins,
         out_specs=[vmem] * len(outs),
         out_shape=outs,
         scratch_shapes=scratch,
+        input_output_aliases=aliases,
         compiler_params=pltpu.CompilerParams(vmem_limit_bytes=VMEM_LIMIT),
     )
 
 
-def log_sum(parts, axis):
-    top = jnp.max(parts, axis=axis, keepdims=True)
-    total = jnp.sum(jnp.exp2(parts - top), axis=axis, keepdims=True)
-    return jnp.squeeze(top + jnp.log2(total), axis)
+def by_twos(join, parts):
+    while len(parts) > 1:
+        parts = [join(*parts[k : k + 2]) for k in range(0, len(parts), 2)]
+    return parts[0]
+
+
+def log_sum(parts):
+    top = by_twos(jnp.maximum, parts)
+    return top + jnp.log2(by_twos(jnp.add, [jnp.exp2(part - top) for part in parts]))
+
+
+def plain_sum(parts):
+    return by_twos(jnp.add, parts)
 
 
 class Links:
     def __init__(self, groups, width):
         self.width = width
         self.devices = groups * width
-        self.core = lax.axis_index("nar") % 2
 
     def swap(self, value, mask):
         pairs = [(k, k ^ mask) for k in range(self.devices)]
         return lax.ppermute(value, ("grp", "nar"), pairs)
 
-    def half(self, value, which):
-        count = value.shape[0] // 2
-        return jnp.where(which == 0, value[:count], value[count:])
-
-    def whole(self, value):
-        other = self.swap(value, 1)
-        low = jnp.where(self.core == 0, value, other)
-        high = jnp.where(self.core == 0, other, value)
-        return jnp.concatenate([low, high], axis=0)
-
-    def reduce_half(self, value, join):
-        kept = self.half(value, self.core)
-        got = self.swap(self.half(value, 1 - self.core), 1)
-        kept = join(jnp.stack([kept, got]), 0)
-        chips = self.devices // 2
-        sent = jnp.broadcast_to(kept[None], (chips,) + kept.shape)
-        groups = [list(range(c, self.devices, 2)) for c in range(2)]
-        parts = lax.all_to_all(
-            sent, ("grp", "nar"), 0, 0, axis_index_groups=groups, tiled=True
-        )
-        return join(parts, 0)
+    def reduce_all(self, value, join):
+        masks, bit = [[1]], 2
+        while bit < self.devices:
+            wide = 4 * bit <= self.devices
+            masks.append([bit, 2 * bit, 3 * bit] if wide else [bit])
+            bit *= 4 if wide else 2
+        for stage in masks:
+            value = join([value] + [self.swap(value, mask) for mask in stage])
+        return value
 
     def reduce_own(self, value, join):
         own = value.shape[0] // self.width
@@ -237,7 +234,7 @@
         parts = lax.all_to_all(
             sent.reshape(self.devices, own, BLK), ("grp", "nar"), 0, 0, tiled=True
         )
-        return join(parts, 0)
+        return join(list(parts))
 
     def gather(self, value):
         held = {0: value}
@@ -304,22 +301,19 @@
         return jnp.concatenate([table, jnp.full((8, BLK), FLOOR, f32)], axis=0)
 
     rows = pltpu.VMEM((tiles, BLK), f32)
-    score_shape = jax.ShapeDtypeStruct((run_blocks, BLK, TOPC * BLK), f32)
+    score_shape = pltpu.VMEM((run_blocks, BLK, TOPC * BLK), f32)
     table_shape = jax.ShapeDtypeStruct((ref_blocks, BLK), f32)
-    rep_shape = jax.ShapeDtypeStruct((run_blocks * BLK, BLK), f32)
+    rep_shape = pltpu.VMEM((run_blocks * BLK, BLK), f32)
     scores, lse = call(
         first_kernel, [smem] * 4 + [vmem] * 5, [score_shape, table_shape], [rows]
     )(group_pairs, order, cand, eff, run_desc, ref_all, padded(pot), log_mass, slot_ref)
 
-    log_half = links.half(log_ref, links.core)
-    half = log_half - links.reduce_half(lse, log_sum)
-    pot = links.whole(half)
+    pot = log_ref - links.reduce_all(lse, log_sum)
 
     weights, peaks, sums = call(
-        second_kernel, [smem] * 3 + [vmem] * 4, [score_shape, rep_shape, table_shape], [rows]
-    )(group_pairs, order, eff, scores, padded(pot), log_mass, onehot)
-    log_gain_half = log_half - jnp.log2(links.reduce_half(sums, jnp.sum))
-    log_gain = links.whole(log_gain_half)
+        second_kernel, [smem] * 3 + [vmem] * 4, [score_shape, rep_shape, table_shape], [rows], {3: 0}
+    )(group_pairs, order, eff, pltpu.with_memory_space_constraint(scores, pltpu.VMEM), padded(pot), log_mass, onehot)
+    log_gain = log_ref - jnp.log2(links.reduce_all(sums, plain_sum))
     pot = pot + log_gain
     gain = jnp.concatenate([jnp.exp2(log_gain), jnp.zeros((8, BLK), f32)], axis=0)
 
@@ -328,8 +322,8 @@
         [smem] * 3 + [vmem] * 5,
         [jax.ShapeDtypeStruct((run_blocks, BLK), f32), table_shape],
         [rows],
-    )(group_pairs, order, eff, weights, peaks, gain, log_mass, onehot)
-    total = links.reduce_own(sums, jnp.sum)
+    )(group_pairs, order, eff, pltpu.with_memory_space_constraint(weights, pltpu.VMEM), pltpu.with_memory_space_constraint(peaks, pltpu.VMEM), gain, log_mass, onehot)
+    total = links.reduce_own(sums, plain_sum)
     start = lax.axis_index("nar") * own_blocks
 
     def mine(table):

time: 124 us -> 93.2 us (0.75)
  Pallas kernels: 50.7 us -> 22.3 us
  blocking collectives: 23.9 us -> 0 us
  starting transfers between devices: 6.43 us -> 27.7 us
  waiting for transfers between devices: 19.8 us -> 30.4 us
  other arithmetic: 15.4 us -> 9.35 us
  local copies, waits for them, and re-layouts: 5.43 us -> 2.28 us
    all_to_all x2 -> x0, blocking collectives: 23.9 us -> none  [reduce_half(): lax.all_to_all(sent, ('grp', 'nar'), 0, 0, axis_index_groups=groups, tile...]
    ppermute x10 -> x20, starting transfers between devices: 3.86 us -> 23.3 us  [swap(): return lax.ppermute(value, ('grp', 'nar'), pairs)]
    pallas_call x1, Pallas kernels: 18.3 us -> 6.83 us  [shards(): call(second_kernel, [smem] * 3 + [vmem] * 4, [score_shape, rep_shape, tab...]
    ppermute x10 -> x20, waiting for transfers between devices: 11.6 us -> 22.2 us  [swap(): return lax.ppermute(value, ('grp', 'nar'), pairs)]
    pallas_call x1, Pallas kernels: 21.4 us -> 10.8 us  [shards(): call(first_kernel, [smem] * 4 + [vmem] * 5, [score_shape, table_shape], [...]
    pallas_call x1, Pallas kernels: 11 us -> 4.6 us  [shards(): call(third_kernel, [smem] * 3 + [vmem] * 5, [jax.ShapeDtypeStruct((run_bl...]
    all_to_all x1, starting transfers between devices: 2.57 us -> 4.34 us  [reduce_own(): lax.all_to_all(sent.reshape(self.devices, own, BLK), ('grp', 'nar'), 0, 0...]
    select_n x4 -> x0, other arithmetic: 1.44 us -> none  [the longest x2 1.43 us: half(): return jnp.where(which == 0, value[:count], value[count:])]
  transfers between devices with their start and end apart: 11 -> 21, of which waited for: 7 -> 16; matrix products, arithmetic and copies ran while one was open for 7% -> 7% of each run, Pallas kernels for 0% -> 0%
where the time goes in v2:
time: 93.2 us; the launch traced here: 92.7 us
  waiting for transfers between devices  30.4 us (33%)
  starting transfers between devices  27.7 us (30%)
  Pallas kernels  22.3 us (24%)
  other arithmetic  9.35 us (10%)
  local copies, waits for them, and re-layouts  2.28 us (2%)
    ppermute x20, starting transfers between devices, swap(): return lax.ppermute(value, ('grp', 'nar'), pairs)  23.3 us
    ppermute x20, waiting for transfers between devices, swap(): return lax.ppermute(value, ('grp', 'nar'), pairs)  22.2 us
    pallas_call x1, Pallas kernels, shards(): call(first_kernel, [smem] * 4 + [vmem] * 5, [score_shape, table_shape], [...  10.8 us
    all_to_all x1, waiting for transfers between devices, reduce_own(): lax.all_to_all(sent.reshape(self.devices, own, BLK), ('grp', 'nar'), 0, 0...  8.22 us
    pallas_call x1, Pallas kernels, shards(): call(second_kernel, [smem] * 3 + [vmem] * 4, [score_shape, rep_shape, tab...  6.83 us
    pallas_call x1, Pallas kernels, shards(): call(third_kernel, [smem] * 3 + [vmem] * 5, [jax.ShapeDtypeStruct((run_bl...  4.6 us
    all_to_all x1, starting transfers between devices, reduce_own(): lax.all_to_all(sent.reshape(self.devices, own, BLK), ('grp', 'nar'), 0, 0...  4.34 us
    unnamed x3, other arithmetic  2.08 us
  transfers between devices with their start and end apart: 21, of which 16 were waited for; matrix products, arithmetic and copies ran while one was open for 7% of the time, Pallas kernels for 0%

profile of v2, /device:TPU:0, one launch (start us, length us, event | category | flops | bytes accessed | tf_op | source)
XLA Modules:
  0.0 92.7 jit_solution(6115133597750752681)
XLA Ops:
  1.8 2.6 %collective-permute-start.3 = (f32[2,8,128]{2,1,0:T(8,128)S(1)}, f32[2,8,128]{2,1,0:T(8,128)S(1)}, u32[]{:S(2)}, u32[]{:S(2)}) collective-permute-start(f32[2,8,128]{2,1,0:T(8,128)S(1)} %pad_maximum_fusion.2), channel_id=1, source_target_pairs={{0,2},{1,3},{2,0},{3,1},{4,6},{5,7},{6,4},{7,5},{8,10},{9,11},{10,... | collective-permute-start | bytes 24584 | tf_op jit(solution)/shard_map/ppermute | solution.py:218
  5.4 0.8 select_reduce_fusion.1
  6.2 1.3 %select_reduce_fusion.cand = s32[32,8]{1,0:T(8,128)S(1)} fusion(s32[32,8]{0,1:T(8,128)} %param.9, pred[32,32]{1,0:T(8,128)(4,1)S(1)} %iota_compare_fusion.2), kind=kLoop, calls=%fused_computation.9 | loop fusion | flops 16128 | bytes 3072 | tf_op jit(solution)/shard_map/reduce_sum | solution.py:286
  7.6 0.7 log_multiply_fusion
  9.6 0.7 bitcast_select_fusion.5
  11.0 7.5 %collective-permute-done = bf16[1024,256]{1,0:T(8,128)(2,1)S(1)} collective-permute-done((bf16[1024,256]{1,0:T(8,128)(2,1)}, bf16[1024,256]{1,0:T(8,128)(2,1)S(1)}, u32[]{:S(2)}, u32[]{:S(2)}) %collective-permute-start) | collective-permute-done | bytes 524320 | tf_op jit(solution)/shard_map/ppermute | solution.py:218
  20.5 1.2 %broadcast_select_fusion.7 = (bf16[1024,256]{1,0:T(8,128)(2,1)S(1)}, bf16[1024,256]{1,0:T(8,128)(2,1)S(1)}, bf16[1024,256]{1,0:T(8,128)(2,1)S(1)}, bf16[1024,256]{1,0:T(8,128)(2,1)S(1)}) fusion(pred[]{:T(512)S(6)} %ne.34, bf16[1024,256]{1,0:T(8,128)(2,1)S(1)} %collective-permute-done.1, bf16[1024,256]{1,0:T(8,128)(2,1)S(1)} %collective-permute-done, ...), kind=kLoop, calls=%fused_computation.8 | loop fusion | flops 2097152 | bytes 4194306 | tf_op jit(solution)/shard_map/jit(_where)/select_n | solution.py:254
  22.6 0.7 copy-done
  23.3 10.8 %shard_map.86 = (f32[32,128,1024]{2,1,0:T(8,128)S(1)}, f32[32,128]{1,0:T(8,128)S(1)}) custom-call(s32[8]{0:T(128)S(1)} %slice.21.group_pairs, s32[32]{0:T(128)S(1)} %get-tuple-element.16.order, s32[32,8]{1,0:T(8,128)S(1)} %select_reduce_fusion.cand, s32[32,8]{1,0:T(8,128)S(1)} %fusion.13.eff, bf16[4096,256]{1,0:T(8,128)(2,1)S(1)} %copy-done, ...), custom_call_target="tpu_custom_call" | custom-call | tf_op jit(solution)/shard_map/pallas_call | solution.py:307
  34.1 2.4 %collective-permute-start.6 = (f32[32,128]{1,0:T(8,128)S(1)}, f32[32,128]{1,0:T(8,128)S(1)}, u32[]{:S(2)}, u32[]{:S(2)}) collective-permute-start(f32[32,128]{1,0:T(8,128)S(1)} %get-tuple-element.10), channel_id=1, source_target_pairs={{0,1},{1,0},{2,3},{3,2},{4,5},{5,4},{6,7},{7,6},{8,9},{9,8},{10,11... | collective-permute-start | bytes 49160 | tf_op jit(solution)/shard_map/ppermute | solution.py:218
  36.5 0.8 collective-permute-done.6
  37.4 2.5 %collective-permute-start.9 = (f32[32,128]{1,0:T(8,128)S(1)}, f32[32,128]{1,0:T(8,128)S(1)}, u32[]{:S(2)}, u32[]{:S(2)}) collective-permute-start(f32[32,128]{1,0:T(8,128)S(1)} %multiply_add_fusion.1), channel_id=1, source_target_pairs={{0,6},{1,7},{2,4},{3,5},{4,2},{5,3},{6,0},{7,1},{8,14},{9,15},{10,... | collective-permute-start | bytes 49160 | tf_op jit(solution)/shard_map/ppermute | solution.py:218
  40.2 1.4 %collective-permute-start.7 = (f32[32,128]{1,0:T(8,128)S(1)}, f32[32,128]{1,0:T(8,128)S(1)}, u32[]{:S(2)}, u32[]{:S(2)}) collective-permute-start(f32[32,128]{1,0:T(8,128)S(1)} %multiply_add_fusion.1), channel_id=1, source_target_pairs={{0,2},{1,3},{2,0},{3,1},{4,6},{5,7},{6,4},{7,5},{8,10},{9,11},{10,... | collective-permute-start | bytes 49160 | tf_op jit(solution)/shard_map/ppermute | solution.py:218
  42.1 1.5 %collective-permute-done.8 = f32[32,128]{1,0:T(8,128)S(1)} collective-permute-done((f32[32,128]{1,0:T(8,128)S(1)}, f32[32,128]{1,0:T(8,128)S(1)}, u32[]{:S(2)}, u32[]{:S(2)}) %collective-permute-start.8) | collective-permute-done | bytes 16416 | tf_op jit(solution)/shard_map/ppermute | solution.py:218
  44.0 4.4 %collective-permute-start.12 = (f32[32,128]{1,0:T(8,128)S(1)}, f32[32,128]{1,0:T(8,128)S(1)}, u32[]{:S(2)}, u32[]{:S(2)}) collective-permute-start(f32[32,128]{1,0:T(8,128)S(1)} %multiply_add_fusion), channel_id=1, source_target_pairs={{0,24},{1,25},{2,26},{3,27},{4,28},{5,29},{6,30},{7,31},{8,16},{9,... | collective-permute-start | bytes 49160 | tf_op jit(solution)/shard_map/ppermute | solution.py:218
  49.0 1.1 %collective-permute-done.12 = f32[32,128]{1,0:T(8,128)S(1)} collective-permute-done((f32[32,128]{1,0:T(8,128)S(1)}, f32[32,128]{1,0:T(8,128)S(1)}, u32[]{:S(2)}, u32[]{:S(2)}) %collective-permute-start.12) | collective-permute-done | bytes 16416 | tf_op jit(solution)/shard_map/ppermute | solution.py:218
  50.1 2.9 %collective-permute-done.11 = f32[32,128]{1,0:T(8,128)S(1)} collective-permute-done((f32[32,128]{1,0:T(8,128)S(1)}, f32[32,128]{1,0:T(8,128)S(1)}, u32[]{:S(2)}, u32[]{:S(2)}) %collective-permute-start.11) | collective-permute-done | bytes 16416 | tf_op jit(solution)/shard_map/ppermute | solution.py:218
  53.0 6.8 %shard_map.87 = (f32[32,128,1024]{2,1,0:T(8,128)S(1)}, f32[4096,128]{1,0:T(8,128)S(1)}, f32[32,128]{1,0:T(8,128)S(1)}) custom-call(s32[8]{0:T(128)S(1)} %slice.21.group_pairs, s32[32]{0:T(128)S(1)} %get-tuple-element.16.order, s32[32,8]{1,0:T(8,128)S(1)} %fusion.13.eff, ...), custom_call_target="tpu_custom_call", output_to_operand_aliasing={{0}: (3, {})} | custom-call | tf_op jit(solution)/shard_map/pallas_call | solution.py:313
  60.0 1.2 %collective-permute-done.13 = f32[32,128]{1,0:T(8,128)S(1)} collective-permute-done((f32[32,128]{1,0:T(8,128)S(1)}, f32[32,128]{1,0:T(8,128)S(1)}, u32[]{:S(2)}, u32[]{:S(2)}) %collective-permute-start.13) | collective-permute-done | bytes 16416 | tf_op jit(solution)/shard_map/ppermute | solution.py:218
  61.1 1.8 %collective-permute-start.16 = (f32[32,128]{1,0:T(8,128)S(1)}, f32[32,128]{1,0:T(8,128)S(1)}, u32[]{:S(2)}, u32[]{:S(2)}) collective-permute-start(f32[32,128]{1,0:T(8,128)S(1)} %add.213), channel_id=1, source_target_pairs={{0,6},{1,7},{2,4},{3,5},{4,2},{5,3},{6,0},{7,1},{8,14},{9,15},{10,... | collective-permute-start | bytes 49160 | tf_op jit(solution)/shard_map/ppermute | solution.py:218
  62.9 0.9 collective-permute-start.15
  63.8 0.9 collective-permute-start.14
  64.6 1.2 %collective-permute-done.16 = f32[32,128]{1,0:T(8,128)S(1)} collective-permute-done((f32[32,128]{1,0:T(8,128)S(1)}, f32[32,128]{1,0:T(8,128)S(1)}, u32[]{:S(2)}, u32[]{:S(2)}) %collective-permute-start.16) | collective-permute-done | bytes 16416 | tf_op jit(solution)/shard_map/ppermute | solution.py:218
  65.9 0.8 collective-permute-done.15
  66.6 0.9 collective-permute-done.14
  67.5 2.1 %collective-permute-start.19 = (f32[32,128]{1,0:T(8,128)S(1)}, f32[32,128]{1,0:T(8,128)S(1)}, u32[]{:S(2)}, u32[]{:S(2)}) collective-permute-start(f32[32,128]{1,0:T(8,128)S(1)} %add_add_fusion), channel_id=1, source_target_pairs={{0,24},{1,25},{2,26},{3,27},{4,28},{5,29},{6,30},{7,31},{8,16},{9,... | collective-permute-start | bytes 49160 | tf_op jit(solution)/shard_map/ppermute | solution.py:218
  70.0 2.0 %collective-permute-start.17 = (f32[32,128]{1,0:T(8,128)S(1)}, f32[32,128]{1,0:T(8,128)S(1)}, u32[]{:S(2)}, u32[]{:S(2)}) collective-permute-start(f32[32,128]{1,0:T(8,128)S(1)} %add_add_fusion), channel_id=1, source_target_pairs={{0,8},{1,9},{2,10},{3,11},{4,12},{5,13},{6,14},{7,15},{8,0},{9,1},... | collective-permute-start | bytes 49160 | tf_op jit(solution)/shard_map/ppermute | solution.py:218
  71.9 1.2 %collective-permute-done.19 = f32[32,128]{1,0:T(8,128)S(1)} collective-permute-done((f32[32,128]{1,0:T(8,128)S(1)}, f32[32,128]{1,0:T(8,128)S(1)}, u32[]{:S(2)}, u32[]{:S(2)}) %collective-permute-start.19) | collective-permute-done | bytes 16416 | tf_op jit(solution)/shard_map/ppermute | solution.py:218
  73.1 1.1 %collective-permute-done.18 = f32[32,128]{1,0:T(8,128)S(1)} collective-permute-done((f32[32,128]{1,0:T(8,128)S(1)}, f32[32,128]{1,0:T(8,128)S(1)}, u32[]{:S(2)}, u32[]{:S(2)}) %collective-permute-start.18) | collective-permute-done | bytes 16416 | tf_op jit(solution)/shard_map/ppermute | solution.py:218
  74.3 4.6 %shard_map.88 = (f32[32,128]{1,0:T(8,128)}, f32[32,128]{1,0:T(8,128)S(1)}) custom-call(s32[8]{0:T(128)S(1)} %slice.21.group_pairs, s32[32]{0:T(128)S(1)} %get-tuple-element.16.order, s32[32,8]{1,0:T(8,128)S(1)} %fusion.13.eff, f32[32,128,1024]{2,1,0:T(8,128)S(1)} %get-tuple-element.11.weights, f32[4096,128]{1,0:T(8,128)S(1)} %get-tuple-element.12.peaks, ...), custom_call_target="tpu_custom_call" | custom-call | tf_op jit(solution)/shard_map/pallas_call | solution.py:320
  79.5 4.3 %all-to-all-start = ((f32[32,8,128]{2,1,0:T(8,128)}), f32[32,8,128]{2,1,0:T(8,128)S(1)}, u32[]{:S(2)}, u32[]{:S(2)}) async-start(f32[32,8,128]{2,1,0:T(8,128)} %bitcast.12), calls=%async_computation | async-start | bytes 262144 | tf_op jit(solution)/shard_map/all_to_all | solution.py:234
  83.9 8.2 %all-to-all-done = f32[32,8,128]{2,1,0:T(8,128)S(1)} async-done(((f32[32,8,128]{2,1,0:T(8,128)}), f32[32,8,128]{2,1,0:T(8,128)S(1)}, u32[]{:S(2)}, u32[]{:S(2)}) %all-to-all-start) | async-done | bytes 131104 | tf_op jit(solution)/shard_map/all_to_all | solution.py:234
  (47 shorter events, 10.7 us)
Async XLA Ops:
  1.3 7.7 %collective-permute-start.5 = (f32[2,8,128]{2,1,0:T(8,128)S(1)}, f32[2,8,128]{2,1,0:T(8,128)S(1)}, u32[]{:S(2)}, u32[]{:S(2)}) collective-permute-start(f32[2,8,128]{2,1,0:T(8,128)S(1)} %pad_maximum_fusion.2), channel_id=1, source_target_pairs={{0,1},{1,0},{2,3},{3,2},{4,5},{5,4},{6,7},{7,6},{8,9},{9,8},{10,11... | collective-permute-start | bytes 24584 | tf_op jit(solution)/shard_map/ppermute | solution.py:218
  1.8 6.5 %collective-permute-start.3 = (f32[2,8,128]{2,1,0:T(8,128)S(1)}, f32[2,8,128]{2,1,0:T(8,128)S(1)}, u32[]{:S(2)}, u32[]{:S(2)}) collective-permute-start(f32[2,8,128]{2,1,0:T(8,128)S(1)} %pad_maximum_fusion.2), channel_id=1, source_target_pairs={{0,2},{1,3},{2,0},{3,1},{4,6},{5,7},{6,4},{7,5},{8,10},{9,11},{10,... | collective-permute-start | bytes 24584 | tf_op jit(solution)/shard_map/ppermute | solution.py:218
  4.4 14.2 %collective-permute-start = (bf16[1024,256]{1,0:T(8,128)(2,1)}, bf16[1024,256]{1,0:T(8,128)(2,1)S(1)}, u32[]{:S(2)}, u32[]{:S(2)}) collective-permute-start(bf16[1024,256]{1,0:T(8,128)(2,1)} %param.8), channel_id=1, source_target_pairs={{0,2},{1,3},{2,0},{3,1},{4,6},{5,7},{6,4},{7,5},{8,10},{9,11},{10,... | collective-permute-start | bytes 1572872 | tf_op jit(solution)/shard_map/ppermute | solution.py:218
  4.5 15.5 %collective-permute-start.2 = (bf16[1024,256]{1,0:T(8,128)(2,1)}, bf16[1024,256]{1,0:T(8,128)(2,1)S(1)}, u32[]{:S(2)}, u32[]{:S(2)}) collective-permute-start(bf16[1024,256]{1,0:T(8,128)(2,1)} %param.8), channel_id=1, source_target_pairs={{0,1},{1,0},{2,3},{3,2},{4,5},{5,4},{6,7},{7,6},{8,9},{9,8},{10,11... | collective-permute-start | bytes 1572872 | tf_op jit(solution)/shard_map/ppermute | solution.py:218
  8.3 1.3 %collective-permute-start.4 = (f32[2,8,128]{2,1,0:T(8,128)S(1)}, f32[2,8,128]{2,1,0:T(8,128)S(1)}, u32[]{:S(2)}, u32[]{:S(2)}) collective-permute-start(f32[2,8,128]{2,1,0:T(8,128)S(1)} %collective-permute-done.3), channel_id=1, source_target_pairs={{0,1},{1,0},{2,3},{3,2},{4,5},{5,4},{6,7},{7,6},{8,9},{9,8},{10,11... | collective-permute-start | bytes 24584 | tf_op jit(solution)/shard_map/ppermute | solution.py:218
  18.6 1.9 %collective-permute-start.1 = (bf16[1024,256]{1,0:T(8,128)(2,1)S(1)}, bf16[1024,256]{1,0:T(8,128)(2,1)S(1)}, u32[]{:S(2)}, u32[]{:S(2)}) collective-permute-start(bf16[1024,256]{1,0:T(8,128)(2,1)S(1)} %collective-permute-done), channel_id=1, source_target_pairs={{0,1},{1,0},{2,3},{3,2},{4,5},{5,4},{6,7},{7,6},{8,9},{9,8},{10,11... | collective-permute-start | bytes 1572872 | tf_op jit(solution)/shard_map/ppermute | solution.py:218
  21.7 1.6 %copy-start = (bf16[4096,256]{1,0:T(8,128)(2,1)S(1)}, bf16[4096,256]{1,0:T(8,128)(2,1)}, u32[]{:S(2)}) copy-start(bf16[4096,256]{1,0:T(8,128)(2,1)} %run.1) | copy-start | bytes 6291460
  34.1 3.2 %collective-permute-start.6 = (f32[32,128]{1,0:T(8,128)S(1)}, f32[32,128]{1,0:T(8,128)S(1)}, u32[]{:S(2)}, u32[]{:S(2)}) collective-permute-start(f32[32,128]{1,0:T(8,128)S(1)} %get-tuple-element.10), channel_id=1, source_target_pairs={{0,1},{1,0},{2,3},{3,2},{4,5},{5,4},{6,7},{7,6},{8,9},{9,8},{10,11... | collective-permute-start | bytes 49160 | tf_op jit(solution)/shard_map/ppermute | solution.py:218
  37.4 4.7 %collective-permute-start.9 = (f32[32,128]{1,0:T(8,128)S(1)}, f32[32,128]{1,0:T(8,128)S(1)}, u32[]{:S(2)}, u32[]{:S(2)}) collective-permute-start(f32[32,128]{1,0:T(8,128)S(1)} %multiply_add_fusion.1), channel_id=1, source_target_pairs={{0,6},{1,7},{2,4},{3,5},{4,2},{5,3},{6,0},{7,1},{8,14},{9,15},{10,... | collective-permute-start | bytes 49160 | tf_op jit(solution)/shard_map/ppermute | solution.py:218
  39.8 3.7 %collective-permute-start.8 = (f32[32,128]{1,0:T(8,128)S(1)}, f32[32,128]{1,0:T(8,128)S(1)}, u32[]{:S(2)}, u32[]{:S(2)}) collective-permute-start(f32[32,128]{1,0:T(8,128)S(1)} %multiply_add_fusion.1), channel_id=1, source_target_pairs={{0,4},{1,5},{2,6},{3,7},{4,0},{5,1},{6,2},{7,3},{8,12},{9,13},{10,... | collective-permute-start | bytes 49160 | tf_op jit(solution)/shard_map/ppermute | solution.py:218
  40.2 3.7 %collective-permute-start.7 = (f32[32,128]{1,0:T(8,128)S(1)}, f32[32,128]{1,0:T(8,128)S(1)}, u32[]{:S(2)}, u32[]{:S(2)}) collective-permute-start(f32[32,128]{1,0:T(8,128)S(1)} %multiply_add_fusion.1), channel_id=1, source_target_pairs={{0,2},{1,3},{2,0},{3,1},{4,6},{5,7},{6,4},{7,5},{8,10},{9,11},{10,... | collective-permute-start | bytes 49160 | tf_op jit(solution)/shard_map/ppermute | solution.py:218
  44.0 6.1 %collective-permute-start.12 = (f32[32,128]{1,0:T(8,128)S(1)}, f32[32,128]{1,0:T(8,128)S(1)}, u32[]{:S(2)}, u32[]{:S(2)}) collective-permute-start(f32[32,128]{1,0:T(8,128)S(1)} %multiply_add_fusion), channel_id=1, source_target_pairs={{0,24},{1,25},{2,26},{3,27},{4,28},{5,29},{6,30},{7,31},{8,16},{9,... | collective-permute-start | bytes 49160 | tf_op jit(solution)/shard_map/ppermute | solution.py:218
  48.4 4.6 %collective-permute-start.11 = (f32[32,128]{1,0:T(8,128)S(1)}, f32[32,128]{1,0:T(8,128)S(1)}, u32[]{:S(2)}, u32[]{:S(2)}) collective-permute-start(f32[32,128]{1,0:T(8,128)S(1)} %multiply_add_fusion), channel_id=1, source_target_pairs={{0,16},{1,17},{2,18},{3,19},{4,20},{5,21},{6,22},{7,23},{8,24},{9,... | collective-permute-start | bytes 49160 | tf_op jit(solution)/shard_map/ppermute | solution.py:218
  48.4 4.6 %collective-permute-start.10 = (f32[32,128]{1,0:T(8,128)S(1)}, f32[32,128]{1,0:T(8,128)S(1)}, u32[]{:S(2)}, u32[]{:S(2)}) collective-permute-start(f32[32,128]{1,0:T(8,128)S(1)} %multiply_add_fusion), channel_id=1, source_target_pairs={{0,8},{1,9},{2,10},{3,11},{4,12},{5,13},{6,14},{7,15},{8,0},{9,1},... | collective-permute-start | bytes 49160 | tf_op jit(solution)/shard_map/ppermute | solution.py:218
  59.9 1.2 %collective-permute-start.13 = (f32[32,128]{1,0:T(8,128)S(1)}, f32[32,128]{1,0:T(8,128)S(1)}, u32[]{:S(2)}, u32[]{:S(2)}) collective-permute-start(f32[32,128]{1,0:T(8,128)S(1)} %get-tuple-element.13), channel_id=1, source_target_pairs={{0,1},{1,0},{2,3},{3,2},{4,5},{5,4},{6,7},{7,6},{8,9},{9,8},{10,11... | collective-permute-start | bytes 49160 | tf_op jit(solution)/shard_map/ppermute | solution.py:218
  61.1 4.7 %collective-permute-start.16 = (f32[32,128]{1,0:T(8,128)S(1)}, f32[32,128]{1,0:T(8,128)S(1)}, u32[]{:S(2)}, u32[]{:S(2)}) collective-permute-start(f32[32,128]{1,0:T(8,128)S(1)} %add.213), channel_id=1, source_target_pairs={{0,6},{1,7},{2,4},{3,5},{4,2},{5,3},{6,0},{7,1},{8,14},{9,15},{10,... | collective-permute-start | bytes 49160 | tf_op jit(solution)/shard_map/ppermute | solution.py:218
  62.9 3.7 %collective-permute-start.15 = (f32[32,128]{1,0:T(8,128)S(1)}, f32[32,128]{1,0:T(8,128)S(1)}, u32[]{:S(2)}, u32[]{:S(2)}) collective-permute-start(f32[32,128]{1,0:T(8,128)S(1)} %add.213), channel_id=1, source_target_pairs={{0,4},{1,5},{2,6},{3,7},{4,0},{5,1},{6,2},{7,3},{8,12},{9,13},{10,... | collective-permute-start | bytes 49160 | tf_op jit(solution)/shard_map/ppermute | solution.py:218
  63.8 3.7 %collective-permute-start.14 = (f32[32,128]{1,0:T(8,128)S(1)}, f32[32,128]{1,0:T(8,128)S(1)}, u32[]{:S(2)}, u32[]{:S(2)}) collective-permute-start(f32[32,128]{1,0:T(8,128)S(1)} %add.213), channel_id=1, source_target_pairs={{0,2},{1,3},{2,0},{3,1},{4,6},{5,7},{6,4},{7,5},{8,10},{9,11},{10,... | collective-permute-start | bytes 49160 | tf_op jit(solution)/shard_map/ppermute | solution.py:218
  67.5 5.6 %collective-permute-start.19 = (f32[32,128]{1,0:T(8,128)S(1)}, f32[32,128]{1,0:T(8,128)S(1)}, u32[]{:S(2)}, u32[]{:S(2)}) collective-permute-start(f32[32,128]{1,0:T(8,128)S(1)} %add_add_fusion), channel_id=1, source_target_pairs={{0,24},{1,25},{2,26},{3,27},{4,28},{5,29},{6,30},{7,31},{8,16},{9,... | collective-permute-start | bytes 49160 | tf_op jit(solution)/shard_map/ppermute | solution.py:218
  69.6 4.6 %collective-permute-start.18 = (f32[32,128]{1,0:T(8,128)S(1)}, f32[32,128]{1,0:T(8,128)S(1)}, u32[]{:S(2)}, u32[]{:S(2)}) collective-permute-start(f32[32,128]{1,0:T(8,128)S(1)} %add_add_fusion), channel_id=1, source_target_pairs={{0,16},{1,17},{2,18},{3,19},{4,20},{5,21},{6,22},{7,23},{8,24},{9,... | collective-permute-start | bytes 49160 | tf_op jit(solution)/shard_map/ppermute | solution.py:218
  70.0 4.3 %collective-permute-start.17 = (f32[32,128]{1,0:T(8,128)S(1)}, f32[32,128]{1,0:T(8,128)S(1)}, u32[]{:S(2)}, u32[]{:S(2)}) collective-permute-start(f32[32,128]{1,0:T(8,128)S(1)} %add_add_fusion), channel_id=1, source_target_pairs={{0,8},{1,9},{2,10},{3,11},{4,12},{5,13},{6,14},{7,15},{8,0},{9,1},... | collective-permute-start | bytes 49160 | tf_op jit(solution)/shard_map/ppermute | solution.py:218
  79.5 12.6 %all-to-all-start = ((f32[32,8,128]{2,1,0:T(8,128)}), f32[32,8,128]{2,1,0:T(8,128)S(1)}, u32[]{:S(2)}, u32[]{:S(2)}) async-start(f32[32,8,128]{2,1,0:T(8,128)} %bitcast.12), calls=%async_computation | async-start | bytes 262144 | tf_op jit(solution)/shard_map/all_to_all | solution.py:234

commit v3 on v2

v3 whole, which is shorter than its diff:
```python
import functools
import math

import jax
import jax.numpy as jnp
from jax import lax
from jax.experimental import pallas as pl
from jax.experimental.pallas import tpu as pltpu
from jax.sharding import PartitionSpec as P

BLK = 128
TOPC = 8
JOINED = 8
LOG2E = math.log2(math.e)
FLOOR = -1e30
VMEM_LIMIT = 8 * 1024 * 1024

vmem = pl.BlockSpec(memory_space=pltpu.VMEM)
smem = pl.BlockSpec(memory_space=pltpu.SMEM)


def group_size(run_blocks):
    for size in (4, 2):
        if run_blocks % size == 0:
            return size
    return 1


class Table:
    def __init__(self, ref, run_blocks):
        self.ref = ref
        self.run_blocks = run_blocks

    def order(self, place):
        return self.ref[place]

    def live(self, place):
        return self.ref[self.run_blocks + place]

    def cand(self, place, slot):
        return self.ref[2 * self.run_blocks + place * TOPC + slot]

    def eff(self, place, slot):
        return self.ref[(2 + TOPC) * self.run_blocks + place * TOPC + slot]

    def offset(self, index):
        return self.ref[(2 + 2 * TOPC) * self.run_blocks + index]

    def by_groups(self, body, grain):
        size = group_size(self.run_blocks)

        def step(group, carry):
            most = self.live(group * size)
            for count in range(grain, TOPC + 1, grain):

                @pl.when((most <= count) & (most > count - grain))
                def _():
                    body(count, [group * size + k for k in range(size)])

            return carry

        lax.fori_loop(0, self.run_blocks // size, step, 0)


def rows_of(block):
    return pl.ds(pl.multiple_of(block * BLK, BLK), BLK)


def side(parts):
    return parts[0] if len(parts) == 1 else jnp.concatenate(parts, axis=1)


def pair_row(values, table, place, pair):
    return side([values[pl.ds(table.eff(place, slot), 1), :] for slot in pair])


def spread(column):
    return jnp.broadcast_to(column, (BLK, BLK))


def wide(tile, pair):
    return side([tile] * len(pair))


def pairs_of(count):
    return [range(first, min(first + 2, count)) for first in range(0, count, 2)]


def span(pair):
    return slice(BLK * pair[0], BLK * (pair[-1] + 1))


def put_rows(rows, place, pair, row):
    for index, slot in enumerate(pair):
        rows[pl.ds(place * TOPC + slot, 1), :] = row[:, BLK * index : BLK * (index + 1)]


def halves(join, tile):
    return tile if tile.shape[1] == BLK else join(tile[:, :BLK], tile[:, BLK:])


def first_kernel(table, run_hbm, mass_hbm, own_hbm, pot, slot_ref, *rest):
    pieces, (scores, log_mass, lse, rows, ref, run, run_mass, own, arrived) = rest[:-9], rest[-9:]
    run_blocks = scores.shape[0]
    table = Table(table, run_blocks)
    copies = [
        pltpu.make_async_copy(mass_hbm, run_mass, arrived.at[0]),
        pltpu.make_async_copy(own_hbm, own, arrived.at[1]),
        pltpu.make_async_copy(run_hbm, run, arrived.at[2]),
    ]
    for copy in copies:
        copy.start()
    own_blocks = own_hbm.shape[0] // BLK
    for index, piece in enumerate(pieces):
        start = table.offset(index + 1) // BLK
        for block in range(own_blocks):
            ref[start + block] = piece[BLK * block : BLK * (block + 1), :].T
    copies[0].wait()

    def fill(block, carry):
        row = jnp.log2(run_mass[pl.ds(block, 1), :])
        log_mass[rows_of(block), :] = jnp.broadcast_to(row, (BLK, BLK)).T
        return carry

    lax.fori_loop(0, run_blocks, fill, 0, unroll=math.gcd(run_blocks, 8))
    copies[1].wait()
    for block in range(own_blocks):
        ref[table.offset(0) // BLK + block] = own[BLK * block : BLK * (block + 1), :].T
    copies[2].wait()
    ref_blocks = lse.shape[0]
    scale = 2.0 * LOG2E / math.sqrt(run.shape[1])

    def body(count, places):
        peaks = []
        for place in places:
            mine = run[rows_of(table.order(place)), :]
            peak = None
            for pair in pairs_of(count):
                both = jnp.concatenate(
                    [ref[table.cand(place, slot)] for slot in pair], axis=1
                )
                tile = lax.dot_general(
                    mine, both, (((1,), (0,)), ((), ())), preferred_element_type=jnp.float32
                )
                tile = tile * scale
                scores[place, :, span(pair)] = tile
                top = halves(jnp.maximum, tile + pair_row(pot, table, place, pair))
                peak = top if peak is None else jnp.maximum(peak, top)
            peaks.append(peak)
        peaks = [spread(jnp.max(peak, axis=1, keepdims=True)) for peak in peaks]
        totals = []
        for place, peak in zip(places, peaks):
            total = None
            for pair in pairs_of(count):
                tile = scores[place, :, span(pair)] + pair_row(pot, table, place, pair)
                part = halves(jnp.add, jnp.exp2(tile - wide(peak, pair)))
                total = part if total is None else total + part
            totals.append(total)
        totals = [spread(jnp.sum(total, axis=1, keepdims=True)) for total in totals]
        potentials = [
            log_mass[rows_of(table.order(place)), :] - (peak + jnp.log2(total))
            for place, peak, total in zip(places, peaks, totals)
        ]
        for place, potential in zip(places, potentials):
            for pair in pairs_of(count):
                tile = scores[place, :, span(pair)] + wide(potential, pair)
                top = jnp.max(tile, axis=0, keepdims=True)
                row = top + jnp.log2(jnp.sum(jnp.exp2(tile - top), axis=0, keepdims=True))
                put_rows(rows, place, pair, row)

    table.by_groups(body, 1)

    def join(step, carry):
        for k in range(JOINED):
            block = step * JOINED + k
            picked = jnp.where(slot_ref[...] == block, rows[...], FLOOR)
            top = jnp.max(picked, axis=0, keepdims=True)
            total = jnp.sum(jnp.exp2(picked - top), axis=0, keepdims=True)
            lse[pl.ds(block, 1), :] = top + jnp.log2(total)
        return carry

    lax.fori_loop(0, ref_blocks // JOINED, join, 0)


def second_kernel(table, scores, pot, log_mass, onehot, weights, peaks, sums, rows):
    run_blocks = weights.shape[0]
    table = Table(table, run_blocks)
    rows[...] = jnp.zeros_like(rows)

    def body(count, places):
        tops = []
        for place in places:
            peak = None
            for pair in pairs_of(count):
                tile = scores[place, :, span(pair)] + pair_row(pot, table, place, pair)
                top = halves(jnp.maximum, tile)
                peak = top if peak is None else jnp.maximum(peak, top)
            tops.append(peak)
        tops = [spread(jnp.max(peak, axis=1, keepdims=True)) for peak in tops]
        totals = []
        for place, peak in zip(places, tops):
            peaks[rows_of(place), :] = peak
            total = None
            for pair in pairs_of(count):
                tile = scores[place, :, span(pair)] + pair_row(pot, table, place, pair)
                weight = jnp.exp2(tile - wide(peak, pair))
                weights[place, :, span(pair)] = weight
                part = halves(jnp.add, weight)
                total = part if total is None else total + part
            totals.append(total)
        totals = [spread(jnp.sum(total, axis=1, keepdims=True)) for total in totals]
        factors = [
            jnp.exp2(log_mass[rows_of(table.order(place)), :] - jnp.log2(total))
            for place, total in zip(places, totals)
        ]
        for place, factor in zip(places, factors):
            for pair in pairs_of(count):
                weight = weights[place, :, span(pair)] * wide(factor, pair)
                put_rows(rows, place, pair, jnp.sum(weight, axis=0, keepdims=True))

    table.by_groups(body, 2)
    sums[...] = jnp.dot(
        onehot[...],
        rows[...],
        precision=lax.Precision.HIGHEST,
        preferred_element_type=jnp.float32,
    )


def third_kernel(table, weights, peaks, gain, log_mass, onehot, out, sums, rows):
    run_blocks = weights.shape[0]
    table = Table(table, run_blocks)
    rows[...] = jnp.zeros_like(rows)
    diagonal = lax.broadcasted_iota(jnp.int32, (BLK, BLK), 0) == lax.broadcasted_iota(
        jnp.int32, (BLK, BLK), 1
    )

    def body(count, places):
        totals = []
        for place in places:
            total = None
            for pair in pairs_of(count):
                weight = weights[place, :, span(pair)] * pair_row(gain, table, place, pair)
                part = halves(jnp.add, weight)
                total = part if total is None else total + part
            totals.append(total)
        totals = [spread(jnp.sum(total, axis=1, keepdims=True)) for total in totals]
        factors = []
        for place, total in zip(places, totals):
            block = table.order(place)
            log_factor = log_mass[rows_of(block), :] - jnp.log2(total)
            factors.append(jnp.exp2(log_factor))
            potential = (log_factor - peaks[rows_of(place), :]) * (0.5 / LOG2E)
            out[pl.ds(block, 1), :] = jnp.sum(
                jnp.where(diagonal, potential, 0.0), axis=0, keepdims=True
            )
        for place, factor in zip(places, factors):
            for pair in pairs_of(count):
                weight = weights[place, :, span(pair)] * wide(factor, pair)
                put_rows(rows, place, pair, jnp.sum(weight, axis=0, keepdims=True))

    table.by_groups(body, 2)
    total = jnp.dot(
        onehot[...],
        rows[...],
        precision=lax.Precision.HIGHEST,
        preferred_element_type=jnp.float32,
    )
    for group in range(sums.shape[0]):
        sums[group] = total


def call(kernel, ins, outs, scratch, aliases={}):
    return pl.pallas_call(
        kernel,
        in_specs=ins,
        out_specs=[vmem] * len(outs),
        out_shape=outs,
        scratch_shapes=scratch,
        input_output_aliases=aliases,
        compiler_params=pltpu.CompilerParams(vmem_limit_bytes=VMEM_LIMIT),
    )


def by_twos(join, parts):
    while len(parts) > 1:
        parts = [join(*parts[k : k + 2]) for k in range(0, len(parts), 2)]
    return parts[0]


def log_sum(parts):
    top = by_twos(jnp.maximum, parts)
    return top + jnp.log2(by_twos(jnp.add, [jnp.exp2(part - top) for part in parts]))


def plain_sum(parts):
    return by_twos(jnp.add, parts)


class Links:
    def __init__(self, groups, width):
        self.width = width
        self.groups = groups
        self.devices = groups * width

    def swap(self, value, mask):
        pairs = [(k, k ^ mask) for k in range(self.devices)]
        return lax.ppermute(value, ("grp", "nar"), pairs)

    def reduce_all(self, value, join):
        masks, bit = [[1]], 2
        while bit < self.devices:
            wide = 4 * bit <= self.devices
            masks.append([bit, 2 * bit, 3 * bit] if wide else [bit])
            bit *= 4 if wide else 2
        for stage in masks:
            value = join([value] + [self.swap(value, mask) for mask in stage])
        return value

    def reduce_own(self, copies, join):
        own = copies.shape[1] // self.width
        sent = copies.reshape(self.devices, own, BLK)
        return join(list(lax.all_to_all(sent, ("grp", "nar"), 0, 0, tiled=True)))

    def gather(self, value):
        held = {0: value}
        mask = self.width // 2
        while mask:
            held.update({key ^ mask: self.swap(part, mask) for key, part in list(held.items())})
            mask //= 2
        return [held[key] for key in range(self.width)]

    def offsets(self, rows):
        me = lax.axis_index("nar")
        return jnp.stack([(key ^ me) * rows for key in range(self.width)]).astype(jnp.int32)

    def arrange(self, parts):
        me = lax.axis_index("nar")
        bit = 1
        parts = list(parts)
        while bit < self.width:
            flip = (me & bit) != 0
            parts = [
                jnp.where(flip, parts[key ^ bit], parts[key]) for key in range(self.width)
            ]
            bit *= 2
        return jnp.concatenate(parts, axis=0)


def shards(run_desc, ref_desc, candidates, live_slots, run_mass, ref_mass, ref_start):
    run_blocks = candidates.shape[0]
    links = Links(lax.axis_size("grp"), lax.axis_size("nar"))
    own_blocks = ref_desc.shape[0] // BLK
    ref_blocks = own_blocks * links.width
    depth = run_desc.shape[1]
    f32 = jnp.float32

    shape = (own_blocks, BLK)
    pot = links.arrange(links.gather(ref_start.reshape(shape))) * (2.0 * LOG2E)
    log_ref = jnp.log2(links.arrange(links.gather(ref_mass.reshape(shape))))
    pieces = links.gather(ref_desc)
    offsets = links.offsets(ref_desc.shape[0])
    blocks = jnp.arange(run_blocks, dtype=jnp.int32)
    rank_key = live_slots * run_blocks - blocks
    place = jnp.sum((rank_key[None, :] > rank_key[:, None]).astype(jnp.int32), axis=1)
    moved = place[None, :] == blocks[:, None]
    order = jnp.sum(jnp.where(moved, blocks[None, :], 0), axis=1)
    cand = jnp.sum(jnp.where(moved[:, :, None], candidates[None], 0), axis=1)
    live = jnp.sum(jnp.where(moved, live_slots[None, :], 0), axis=1)
    slots = jnp.arange(TOPC, dtype=jnp.int32)
    eff = jnp.where(slots[None, :] < live[:, None], cand, ref_blocks)
    table = jnp.concatenate([order, live, cand.reshape(-1), eff.reshape(-1), offsets])
    tiles = run_blocks * TOPC
    slot_ref = jnp.broadcast_to(eff.reshape(tiles, 1), (tiles, BLK))
    onehot = (
        eff.reshape(1, tiles) == jnp.arange(ref_blocks, dtype=jnp.int32)[:, None]
    ).astype(f32)
    def padded(table):
        return jnp.concatenate([table, jnp.full((8, BLK), FLOOR, f32)], axis=0)

    rows = pltpu.VMEM((tiles, BLK), f32)
    score_shape = pltpu.VMEM((run_blocks, BLK, TOPC * BLK), f32)
    table_shape = jax.ShapeDtypeStruct((ref_blocks, BLK), f32)
    rep_shape = pltpu.VMEM((run_blocks * BLK, BLK), f32)
    scores, log_mass, lse = call(
        first_kernel,
        [smem] + [pl.BlockSpec(memory_space=pltpu.HBM)] * 3 + [vmem] * (2 + len(pieces) - 1),
        [score_shape, rep_shape, table_shape],
        [
            rows,
            pltpu.VMEM((ref_blocks, depth, BLK), ref_desc.dtype),
            pltpu.VMEM(run_desc.shape, run_desc.dtype),
            pltpu.VMEM((run_blocks, BLK), f32),
            pltpu.VMEM(ref_desc.shape, ref_desc.dtype),
            pltpu.SemaphoreType.DMA((3,)),
        ],
    )(
        table,
        pltpu.with_memory_space_constraint(run_desc, pltpu.HBM),
        pltpu.with_memory_space_constraint(run_mass.reshape(run_blocks, BLK), pltpu.HBM),
        pltpu.with_memory_space_constraint(pieces[0], pltpu.HBM),
        padded(pot),
        slot_ref,
        *pieces[1:],
    )

    pot = log_ref - links.reduce_all(lse, log_sum)

    weights, peaks, sums = call(
        second_kernel, [smem] + [vmem] * 4, [score_shape, rep_shape, table_shape], [rows], {1: 0}
    )(table, pltpu.with_memory_space_constraint(scores, pltpu.VMEM), padded(pot), log_mass, onehot)
    log_gain = log_ref - jnp.log2(links.reduce_all(sums, plain_sum))
    pot = pot + log_gain
    gain = jnp.concatenate([jnp.exp2(log_gain), jnp.zeros((8, BLK), f32)], axis=0)

    run_pot, sums = call(
        third_kernel,
        [smem] + [vmem] * 5,
        [
            jax.ShapeDtypeStruct((run_blocks, BLK), f32),
            jax.ShapeDtypeStruct((links.groups, ref_blocks, BLK), f32),
        ],
        [rows],
    )(table, pltpu.with_memory_space_constraint(weights, pltpu.VMEM), pltpu.with_memory_space_constraint(peaks, pltpu.VMEM), gain, log_mass, onehot)
    total = links.reduce_own(sums, plain_sum)
    start = lax.axis_index("nar") * own_blocks

    def mine(table):
        return lax.dynamic_slice_in_dim(table, start, own_blocks, 0)

    own = (mine(log_ref) + mine(pot) - mine(log_gain) - jnp.log2(total)) * (0.5 / LOG2E)
    return run_pot.reshape(-1), own.reshape(-1)


def solution(mesh):
    return jax.shard_map(
        shards,
        mesh=mesh,
        in_specs=(
            P(("grp", "nar"), None),
            P("nar", None),
            P(("grp", "nar"), None),
            P(("grp", "nar")),
            P(("grp", "nar")),
            P("nar"),
            P("nar"),
        ),
        out_specs=(P(("grp", "nar")), P("nar")),
        check_vma=False,
    )
```

time: 93.2 us -> 83.9 us (0.900)
  other arithmetic: 9.35 us -> 4.46 us
  Pallas kernels: 22.3 us -> 19.5 us
  local copies, waits for them, and re-layouts: 2.28 us -> 0.38 us
  waiting for transfers between devices: 30.4 us -> 32.3 us
  starting transfers between devices: 27.7 us -> 25.9 us
    pallas_call x3, Pallas kernels: 22.3 us -> 19.5 us  [the longest x1 10.4 us: shards(): call(first_kernel, [smem] + [pl.BlockSpec(memory_space=pltpu.HBM)] * 3 +...]
    unnamed x3 -> x0, other arithmetic: 2.08 us -> none
    ppermute x20 -> x23, waiting for transfers between devices: 22.2 us -> 24.1 us  [swap(): return lax.ppermute(value, ('grp', 'nar'), pairs)]
    ppermute x20 -> x23, starting transfers between devices: 23.3 us -> 21.8 us  [swap(): return lax.ppermute(value, ('grp', 'nar'), pairs)]
    broadcast_in_dim x2 -> x0, local copies, waits for them, and re-layouts: 1.26 us -> none  [the longest x1 0.66 us: reduce_own(): jnp.broadcast_to(pieces, (self.devices // self.width,) + pieces.shape[1:])]
    select_n x2, other arithmetic: 1.93 us -> 0.7 us  [arrange(): jnp.where(flip, parts[key ^ bit], parts[key])]
  transfers between devices with their start and end apart: 21 -> 24, of which waited for: 16 -> 14; matrix products, arithmetic and copies ran while one was open for 7% -> 5% of each run, Pallas kernels for 0% -> 0%
where the time goes in v3:
time: 83.9 us; the launch traced here: 83.3 us
  waiting for transfers between devices  32.3 us (38%)
  starting transfers between devices  25.9 us (31%)
  Pallas kernels  19.5 us (23%)
  other arithmetic  4.46 us (5%)
    ppermute x23, waiting for transfers between devices, swap(): return lax.ppermute(value, ('grp', 'nar'), pairs)  24.1 us
    ppermute x23, starting transfers between devices, swap(): return lax.ppermute(value, ('grp', 'nar'), pairs)  21.8 us
    pallas_call x1, Pallas kernels, shards(): call(first_kernel, [smem] + [pl.BlockSpec(memory_space=pltpu.HBM)] * 3 +...  10.4 us
    all_to_all x1, waiting for transfers between devices, reduce_own(): return join(list(lax.all_to_all(sent, ('grp', 'nar'), 0, 0, tiled=True)))  8.22 us
    pallas_call x1, Pallas kernels, shards(): call(second_kernel, [smem] + [vmem] * 4, [score_shape, rep_shape, table_s...  5.11 us
    all_to_all x1, starting transfers between devices, reduce_own(): return join(list(lax.all_to_all(sent, ('grp', 'nar'), 0, 0, tiled=True)))  4.14 us
    pallas_call x1, Pallas kernels, shards(): call(third_kernel, [smem] + [vmem] * 5, [jax.ShapeDtypeStruct((run_blocks...  3.99 us
  transfers between devices with their start and end apart: 24, of which 14 were waited for; matrix products, arithmetic and copies ran while one was open for 5% of the time, Pallas kernels for 0%

profile of v3, /device:TPU:0, one launch (start us, length us, event | category | flops | bytes accessed | tf_op | source)
XLA Modules:
  0.0 83.3 jit_solution(5383240723784629239)
XLA Ops:
  1.1 2.6 %collective-permute-start = (f32[8,128]{1,0:T(8,128)}, f32[8,128]{1,0:T(8,128)S(1)}, u32[]{:S(2)}, u32[]{:S(2)}) collective-permute-start(f32[8,128]{1,0:T(8,128)} %bitcast.29), channel_id=1, source_target_pairs={{0,2},{1,3},{2,0},{3,1},{4,6},{5,7},{6,4},{7,5},{8,10},{9,11},{10,... | collective-permute-start | bytes 12296 | tf_op jit(solution)/shard_map/ppermute | solution.py:308
  4.2 0.7 iota_subtract_fusion
  5.0 0.8 select_reduce_fusion.1
  5.9 1.3 %select_reduce_fusion = s32[32,8]{1,0:T(8,128)S(1)} fusion(s32[32,8]{0,1:T(8,128)} %param.9, pred[32,32]{1,0:T(8,128)(4,1)S(1)} %iota_compare_fusion.2), kind=kLoop, calls=%fused_computation | loop fusion | flops 16128 | bytes 3072 | tf_op jit(solution)/shard_map/reduce_sum | solution.py:368
  7.5 10.8 %collective-permute-done.4.rest_1_ = bf16[1024,256]{1,0:T(8,128)(2,1)S(1)} collective-permute-done((bf16[1024,256]{1,0:T(8,128)(2,1)}, bf16[1024,256]{1,0:T(8,128)(2,1)S(1)}, u32[]{:S(2)}, u32[]{:S(2)}) %collective-permute-start.4) | collective-permute-done | bytes 524320 | tf_op jit(solution)/shard_map/ppermute | solution.py:308
  18.4 0.7 broadcast_select_fusion.15
  19.1 1.1 %collective-permute-done.5.rest_2_ = bf16[1024,256]{1,0:T(8,128)(2,1)S(1)} collective-permute-done((bf16[1024,256]{1,0:T(8,128)(2,1)S(1)}, bf16[1024,256]{1,0:T(8,128)(2,1)S(1)}, u32[]{:S(2)}, u32[]{:S(2)}) %collective-permute-start.5) | collective-permute-done | bytes 524320 | tf_op jit(solution)/shard_map/ppermute | solution.py:308
  20.3 10.4 %shard_map.86 = (f32[32,128,1024]{2,1,0:T(8,128)S(1)}, f32[4096,128]{1,0:T(8,128)S(1)}, f32[32,128]{1,0:T(8,128)S(1)}) custom-call(s32[580]{0:T(1024)S(1)} %concatenate.18.table, bf16[4096,256]{1,0:T(8,128)(2,1)} %run_hbm.1, f32[32,128]{1,0:T(8,128)} %bitcast.27, bf16[1024,256]{1,0:T(8,128)(2,1)} %own_hbm.1, f32[40,128]{1,0:T(8,128)S(1)} %concatenate.20.pot, ...), custom_call_target="tpu_custom_call" | custom-call | tf_op jit(solution)/shard_map/pallas_call | solution.py:385
  31.3 0.8 %collective-permute-start.6 = (f32[8,128]{1,0:T(8,128)S(1)}, f32[8,128]{1,0:T(8,128)S(1)}, u32[]{:S(2)}, u32[]{:S(2)}) collective-permute-start(f32[8,128]{1,0:T(8,128)S(1)} %bitcast.31), channel_id=1, source_target_pairs={{0,2},{1,3},{2,0},{3,1},{4,6},{5,7},{6,4},{7,5},{8,10},{9,11},{10,... | collective-permute-start | bytes 12296 | tf_op jit(solution)/shard_map/ppermute | solution.py:308
  32.2 2.5 %collective-permute-start.12 = (f32[32,128]{1,0:T(8,128)S(1)}, f32[32,128]{1,0:T(8,128)S(1)}, u32[]{:S(2)}, u32[]{:S(2)}) collective-permute-start(f32[32,128]{1,0:T(8,128)S(1)} %multiply_add_fusion.1), channel_id=1, source_target_pairs={{0,6},{1,7},{2,4},{3,5},{4,2},{5,3},{6,0},{7,1},{8,14},{9,15},{10,... | collective-permute-start | bytes 49160 | tf_op jit(solution)/shard_map/ppermute | solution.py:308
  34.9 0.8 %collective-permute-start.10 = (f32[32,128]{1,0:T(8,128)S(1)}, f32[32,128]{1,0:T(8,128)S(1)}, u32[]{:S(2)}, u32[]{:S(2)}) collective-permute-start(f32[32,128]{1,0:T(8,128)S(1)} %multiply_add_fusion.1), channel_id=1, source_target_pairs={{0,2},{1,3},{2,0},{3,1},{4,6},{5,7},{6,4},{7,5},{8,10},{9,11},{10,... | collective-permute-start | bytes 49160 | tf_op jit(solution)/shard_map/ppermute | solution.py:308
  35.8 1.1 %collective-permute-done.12 = f32[32,128]{1,0:T(8,128)S(1)} collective-permute-done((f32[32,128]{1,0:T(8,128)S(1)}, f32[32,128]{1,0:T(8,128)S(1)}, u32[]{:S(2)}, u32[]{:S(2)}) %collective-permute-start.12) | collective-permute-done | bytes 16416 | tf_op jit(solution)/shard_map/ppermute | solution.py:308
  36.9 1.6 %collective-permute-done.11 = f32[32,128]{1,0:T(8,128)S(1)} collective-permute-done((f32[32,128]{1,0:T(8,128)S(1)}, f32[32,128]{1,0:T(8,128)S(1)}, u32[]{:S(2)}, u32[]{:S(2)}) %collective-permute-start.11) | collective-permute-done | bytes 16416 | tf_op jit(solution)/shard_map/ppermute | solution.py:308
  38.6 4.4 %collective-permute-start.15 = (f32[32,128]{1,0:T(8,128)S(1)}, f32[32,128]{1,0:T(8,128)S(1)}, u32[]{:S(2)}, u32[]{:S(2)}) collective-permute-start(f32[32,128]{1,0:T(8,128)S(1)} %multiply_add_fusion), channel_id=1, source_target_pairs={{0,24},{1,25},{2,26},{3,27},{4,28},{5,29},{6,30},{7,31},{8,16},{9,... | collective-permute-start | bytes 49160 | tf_op jit(solution)/shard_map/ppermute | solution.py:308
  43.0 0.6 collective-permute-start.13
  43.7 1.2 %collective-permute-done.15 = f32[32,128]{1,0:T(8,128)S(1)} collective-permute-done((f32[32,128]{1,0:T(8,128)S(1)}, f32[32,128]{1,0:T(8,128)S(1)}, u32[]{:S(2)}, u32[]{:S(2)}) %collective-permute-start.15) | collective-permute-done | bytes 16416 | tf_op jit(solution)/shard_map/ppermute | solution.py:308
  44.8 2.8 %collective-permute-done.14 = f32[32,128]{1,0:T(8,128)S(1)} collective-permute-done((f32[32,128]{1,0:T(8,128)S(1)}, f32[32,128]{1,0:T(8,128)S(1)}, u32[]{:S(2)}, u32[]{:S(2)}) %collective-permute-start.14) | collective-permute-done | bytes 16416 | tf_op jit(solution)/shard_map/ppermute | solution.py:308
  47.7 5.1 %shard_map.87 = (f32[32,128,1024]{2,1,0:T(8,128)S(1)}, f32[4096,128]{1,0:T(8,128)S(1)}, f32[32,128]{1,0:T(8,128)S(1)}) custom-call(s32[580]{0:T(1024)S(1)} %concatenate.18.table, f32[32,128,1024]{2,1,0:T(8,128)S(1)} %get-tuple-element.10.scores, f32[40,128]{1,0:T(8,128)S(1)} %concatenate.22.pot, ...), custom_call_target="tpu_custom_call", output_to_operand_aliasing={{0}: (1, {})} | custom-call | tf_op jit(solution)/shard_map/pallas_call | solution.py:409
  52.9 1.2 %collective-permute-done.16 = f32[32,128]{1,0:T(8,128)S(1)} collective-permute-done((f32[32,128]{1,0:T(8,128)S(1)}, f32[32,128]{1,0:T(8,128)S(1)}, u32[]{:S(2)}, u32[]{:S(2)}) %collective-permute-start.16) | collective-permute-done | bytes 16416 | tf_op jit(solution)/shard_map/ppermute | solution.py:308
  54.1 0.6 collective-permute-start.19
  54.7 1.7 %collective-permute-start.18 = (f32[32,128]{1,0:T(8,128)S(1)}, f32[32,128]{1,0:T(8,128)S(1)}, u32[]{:S(2)}, u32[]{:S(2)}) collective-permute-start(f32[32,128]{1,0:T(8,128)S(1)} %add.205), channel_id=1, source_target_pairs={{0,4},{1,5},{2,6},{3,7},{4,0},{5,1},{6,2},{7,3},{8,12},{9,13},{10,... | collective-permute-start | bytes 49160 | tf_op jit(solution)/shard_map/ppermute | solution.py:308
  56.4 1.2 %collective-permute-start.17 = (f32[32,128]{1,0:T(8,128)S(1)}, f32[32,128]{1,0:T(8,128)S(1)}, u32[]{:S(2)}, u32[]{:S(2)}) collective-permute-start(f32[32,128]{1,0:T(8,128)S(1)} %add.205), channel_id=1, source_target_pairs={{0,2},{1,3},{2,0},{3,1},{4,6},{5,7},{6,4},{7,5},{8,10},{9,11},{10,... | collective-permute-start | bytes 49160 | tf_op jit(solution)/shard_map/ppermute | solution.py:308
  57.6 1.2 %collective-permute-done.19 = f32[32,128]{1,0:T(8,128)S(1)} collective-permute-done((f32[32,128]{1,0:T(8,128)S(1)}, f32[32,128]{1,0:T(8,128)S(1)}, u32[]{:S(2)}, u32[]{:S(2)}) %collective-permute-start.19) | collective-permute-done | bytes 16416 | tf_op jit(solution)/shard_map/ppermute | solution.py:308
  58.7 1.4 %collective-permute-done.17 = f32[32,128]{1,0:T(8,128)S(1)} collective-permute-done((f32[32,128]{1,0:T(8,128)S(1)}, f32[32,128]{1,0:T(8,128)S(1)}, u32[]{:S(2)}, u32[]{:S(2)}) %collective-permute-start.17) | collective-permute-done | bytes 16416 | tf_op jit(solution)/shard_map/ppermute | solution.py:308
  60.1 1.1 %collective-permute-start.22 = (f32[32,128]{1,0:T(8,128)S(1)}, f32[32,128]{1,0:T(8,128)S(1)}, u32[]{:S(2)}, u32[]{:S(2)}) collective-permute-start(f32[32,128]{1,0:T(8,128)S(1)} %add_add_fusion), channel_id=1, source_target_pairs={{0,24},{1,25},{2,26},{3,27},{4,28},{5,29},{6,30},{7,31},{8,16},{9,... | collective-permute-start | bytes 49160 | tf_op jit(solution)/shard_map/ppermute | solution.py:308
  61.3 0.8 collective-permute-start.21
  62.1 2.5 %collective-permute-start.20 = (f32[32,128]{1,0:T(8,128)S(1)}, f32[32,128]{1,0:T(8,128)S(1)}, u32[]{:S(2)}, u32[]{:S(2)}) collective-permute-start(f32[32,128]{1,0:T(8,128)S(1)} %add_add_fusion), channel_id=1, source_target_pairs={{0,8},{1,9},{2,10},{3,11},{4,12},{5,13},{6,14},{7,15},{8,0},{9,1},... | collective-permute-start | bytes 49160 | tf_op jit(solution)/shard_map/ppermute | solution.py:308
  64.6 1.1 %collective-permute-done.22 = f32[32,128]{1,0:T(8,128)S(1)} collective-permute-done((f32[32,128]{1,0:T(8,128)S(1)}, f32[32,128]{1,0:T(8,128)S(1)}, u32[]{:S(2)}, u32[]{:S(2)}) %collective-permute-start.22) | collective-permute-done | bytes 16416 | tf_op jit(solution)/shard_map/ppermute | solution.py:308
  66.3 4.0 %shard_map.88 = (f32[32,128]{1,0:T(8,128)}, f32[8,32,128]{2,1,0:T(8,128)}) custom-call(s32[580]{0:T(1024)S(1)} %concatenate.18.table, f32[32,128,1024]{2,1,0:T(8,128)S(1)} %get-tuple-element.13.weights, f32[4096,128]{1,0:T(8,128)S(1)} %get-tuple-element.14.peaks, f32[40,128]{1,0:T(8,128)S(1)} %concatenate.23.gain, ...), custom_call_target="tpu_custom_call" | custom-call | tf_op jit(solution)/shard_map/pallas_call | solution.py:416
  70.3 4.1 %all-to-all-start = ((f32[32,8,128]{2,1,0:T(8,128)}), f32[32,8,128]{2,1,0:T(8,128)S(1)}, u32[]{:S(2)}, u32[]{:S(2)}) async-start(f32[32,8,128]{2,1,0:T(8,128)} %bitcast.8), calls=%async_computation | async-start | bytes 262144 | tf_op jit(solution)/shard_map/all_to_all | solution.py:323
  74.5 8.2 %all-to-all-done = f32[32,8,128]{2,1,0:T(8,128)S(1)} async-done(((f32[32,8,128]{2,1,0:T(8,128)}), f32[32,8,128]{2,1,0:T(8,128)S(1)}, u32[]{:S(2)}, u32[]{:S(2)}) %all-to-all-start) | async-done | bytes 131104 | tf_op jit(solution)/shard_map/all_to_all | solution.py:323
  82.7 0.6 fusion.23
  (46 shorter events, 3.6 us)
Async XLA Ops:
  0.6 17.8 %collective-permute-start.2 = (f32[8,128]{1,0:T(8,128)}, f32[8,128]{1,0:T(8,128)S(1)}, u32[]{:S(2)}, u32[]{:S(2)}) collective-permute-start(f32[8,128]{1,0:T(8,128)} %bitcast.28), channel_id=1, source_target_pairs={{0,1},{1,0},{2,3},{3,2},{4,5},{5,4},{6,7},{7,6},{8,9},{9,8},{10,11... | collective-permute-start | bytes 12296 | tf_op jit(solution)/shard_map/ppermute | solution.py:308
  1.1 6.2 %collective-permute-start = (f32[8,128]{1,0:T(8,128)}, f32[8,128]{1,0:T(8,128)S(1)}, u32[]{:S(2)}, u32[]{:S(2)}) collective-permute-start(f32[8,128]{1,0:T(8,128)} %bitcast.29), channel_id=1, source_target_pairs={{0,2},{1,3},{2,0},{3,1},{4,6},{5,7},{6,4},{7,5},{8,10},{9,11},{10,... | collective-permute-start | bytes 12296 | tf_op jit(solution)/shard_map/ppermute | solution.py:308
  3.7 15.4 %collective-permute-start.3 = (bf16[1024,256]{1,0:T(8,128)(2,1)}, bf16[1024,256]{1,0:T(8,128)(2,1)S(1)}, u32[]{:S(2)}, u32[]{:S(2)}) collective-permute-start(bf16[1024,256]{1,0:T(8,128)(2,1)} %own_hbm.1), channel_id=1, source_target_pairs={{0,1},{1,0},{2,3},{3,2},{4,5},{5,4},{6,7},{7,6},{8,9},{9,8},{10,11... | collective-permute-start | bytes 1572872 | tf_op jit(solution)/shard_map/ppermute | solution.py:308
  3.9 14.4 %collective-permute-start.4 = (bf16[1024,256]{1,0:T(8,128)(2,1)}, bf16[1024,256]{1,0:T(8,128)(2,1)S(1)}, u32[]{:S(2)}, u32[]{:S(2)}) collective-permute-start(bf16[1024,256]{1,0:T(8,128)(2,1)} %own_hbm.1), channel_id=1, source_target_pairs={{0,2},{1,3},{2,0},{3,1},{4,6},{5,7},{6,4},{7,5},{8,10},{9,11},{10,... | collective-permute-start | bytes 1572872 | tf_op jit(solution)/shard_map/ppermute | solution.py:308
  7.4 11.0 %collective-permute-start.1 = (f32[8,128]{1,0:T(8,128)S(1)}, f32[8,128]{1,0:T(8,128)S(1)}, u32[]{:S(2)}, u32[]{:S(2)}) collective-permute-start(f32[8,128]{1,0:T(8,128)S(1)} %collective-permute-done), channel_id=1, source_target_pairs={{0,1},{1,0},{2,3},{3,2},{4,5},{5,4},{6,7},{7,6},{8,9},{9,8},{10,11... | collective-permute-start | bytes 12296 | tf_op jit(solution)/shard_map/ppermute | solution.py:308
  18.3 1.9 %collective-permute-start.5 = (bf16[1024,256]{1,0:T(8,128)(2,1)S(1)}, bf16[1024,256]{1,0:T(8,128)(2,1)S(1)}, u32[]{:S(2)}, u32[]{:S(2)}) collective-permute-start(bf16[1024,256]{1,0:T(8,128)(2,1)S(1)} %collective-permute-done.4.rest_1_), channel_id=1, source_target_pairs={{0,1},{1,0},{2,3},{3,2},{4,5},{5,4},{6,7},{7,6},{8,9},{9,8},{10,11... | collective-permute-start | bytes 1572872 | tf_op jit(solution)/shard_map/ppermute | solution.py:308
  20.3 10.5 %copy-start = (f32[1024]{0:T(1024)S(1)}, f32[1024]{0:T(1024)}, u32[]{:S(2)}) copy-start(f32[1024]{0:T(1024)} %param.12) | copy-start | bytes 12292
  30.7 1.4 %collective-permute-start.9 = (f32[32,128]{1,0:T(8,128)S(1)}, f32[32,128]{1,0:T(8,128)S(1)}, u32[]{:S(2)}, u32[]{:S(2)}) collective-permute-start(f32[32,128]{1,0:T(8,128)S(1)} %get-tuple-element.11), channel_id=1, source_target_pairs={{0,1},{1,0},{2,3},{3,2},{4,5},{5,4},{6,7},{7,6},{8,9},{9,8},{10,11... | collective-permute-start | bytes 49160 | tf_op jit(solution)/shard_map/ppermute | solution.py:308
  30.8 12.9 %collective-permute-start.8 = (f32[8,128]{1,0:T(8,128)S(1)}, f32[8,128]{1,0:T(8,128)S(1)}, u32[]{:S(2)}, u32[]{:S(2)}) collective-permute-start(f32[8,128]{1,0:T(8,128)S(1)} %bitcast.30), channel_id=1, source_target_pairs={{0,1},{1,0},{2,3},{3,2},{4,5},{5,4},{6,7},{7,6},{8,9},{9,8},{10,11... | collective-permute-start | bytes 12296 | tf_op jit(solution)/shard_map/ppermute | solution.py:308
  31.3 4.4 %collective-permute-start.6 = (f32[8,128]{1,0:T(8,128)S(1)}, f32[8,128]{1,0:T(8,128)S(1)}, u32[]{:S(2)}, u32[]{:S(2)}) collective-permute-start(f32[8,128]{1,0:T(8,128)S(1)} %bitcast.31), channel_id=1, source_target_pairs={{0,2},{1,3},{2,0},{3,1},{4,6},{5,7},{6,4},{7,5},{8,10},{9,11},{10,... | collective-permute-start | bytes 12296 | tf_op jit(solution)/shard_map/ppermute | solution.py:308
  32.2 4.7 %collective-permute-start.12 = (f32[32,128]{1,0:T(8,128)S(1)}, f32[32,128]{1,0:T(8,128)S(1)}, u32[]{:S(2)}, u32[]{:S(2)}) collective-permute-start(f32[32,128]{1,0:T(8,128)S(1)} %multiply_add_fusion.1), channel_id=1, source_target_pairs={{0,6},{1,7},{2,4},{3,5},{4,2},{5,3},{6,0},{7,1},{8,14},{9,15},{10,... | collective-permute-start | bytes 49160 | tf_op jit(solution)/shard_map/ppermute | solution.py:308
  34.7 3.7 %collective-permute-start.11 = (f32[32,128]{1,0:T(8,128)S(1)}, f32[32,128]{1,0:T(8,128)S(1)}, u32[]{:S(2)}, u32[]{:S(2)}) collective-permute-start(f32[32,128]{1,0:T(8,128)S(1)} %multiply_add_fusion.1), channel_id=1, source_target_pairs={{0,4},{1,5},{2,6},{3,7},{4,0},{5,1},{6,2},{7,3},{8,12},{9,13},{10,... | collective-permute-start | bytes 49160 | tf_op jit(solution)/shard_map/ppermute | solution.py:308
  34.9 3.7 %collective-permute-start.10 = (f32[32,128]{1,0:T(8,128)S(1)}, f32[32,128]{1,0:T(8,128)S(1)}, u32[]{:S(2)}, u32[]{:S(2)}) collective-permute-start(f32[32,128]{1,0:T(8,128)S(1)} %multiply_add_fusion.1), channel_id=1, source_target_pairs={{0,2},{1,3},{2,0},{3,1},{4,6},{5,7},{6,4},{7,5},{8,10},{9,11},{10,... | collective-permute-start | bytes 49160 | tf_op jit(solution)/shard_map/ppermute | solution.py:308
  35.7 7.9 %collective-permute-start.7 = (f32[8,128]{1,0:T(8,128)S(1)}, f32[8,128]{1,0:T(8,128)S(1)}, u32[]{:S(2)}, u32[]{:S(2)}) collective-permute-start(f32[8,128]{1,0:T(8,128)S(1)} %collective-permute-done.6), channel_id=1, source_target_pairs={{0,1},{1,0},{2,3},{3,2},{4,5},{5,4},{6,7},{7,6},{8,9},{9,8},{10,11... | collective-permute-start | bytes 12296 | tf_op jit(solution)/shard_map/ppermute | solution.py:308
  38.6 6.2 %collective-permute-start.15 = (f32[32,128]{1,0:T(8,128)S(1)}, f32[32,128]{1,0:T(8,128)S(1)}, u32[]{:S(2)}, u32[]{:S(2)}) collective-permute-start(f32[32,128]{1,0:T(8,128)S(1)} %multiply_add_fusion), channel_id=1, source_target_pairs={{0,24},{1,25},{2,26},{3,27},{4,28},{5,29},{6,30},{7,31},{8,16},{9,... | collective-permute-start | bytes 49160 | tf_op jit(solution)/shard_map/ppermute | solution.py:308
  43.0 4.6 %collective-permute-start.14 = (f32[32,128]{1,0:T(8,128)S(1)}, f32[32,128]{1,0:T(8,128)S(1)}, u32[]{:S(2)}, u32[]{:S(2)}) collective-permute-start(f32[32,128]{1,0:T(8,128)S(1)} %multiply_add_fusion), channel_id=1, source_target_pairs={{0,16},{1,17},{2,18},{3,19},{4,20},{5,21},{6,22},{7,23},{8,24},{9,... | collective-permute-start | bytes 49160 | tf_op jit(solution)/shard_map/ppermute | solution.py:308
  43.0 4.6 %collective-permute-start.13 = (f32[32,128]{1,0:T(8,128)S(1)}, f32[32,128]{1,0:T(8,128)S(1)}, u32[]{:S(2)}, u32[]{:S(2)}) collective-permute-start(f32[32,128]{1,0:T(8,128)S(1)} %multiply_add_fusion), channel_id=1, source_target_pairs={{0,8},{1,9},{2,10},{3,11},{4,12},{5,13},{6,14},{7,15},{8,0},{9,1},... | collective-permute-start | bytes 49160 | tf_op jit(solution)/shard_map/ppermute | solution.py:308
  52.8 1.2 %collective-permute-start.16 = (f32[32,128]{1,0:T(8,128)S(1)}, f32[32,128]{1,0:T(8,128)S(1)}, u32[]{:S(2)}, u32[]{:S(2)}) collective-permute-start(f32[32,128]{1,0:T(8,128)S(1)} %get-tuple-element.15), channel_id=1, source_target_pairs={{0,1},{1,0},{2,3},{3,2},{4,5},{5,4},{6,7},{7,6},{8,9},{9,8},{10,11... | collective-permute-start | bytes 49160 | tf_op jit(solution)/shard_map/ppermute | solution.py:308
  54.1 4.6 %collective-permute-start.19 = (f32[32,128]{1,0:T(8,128)S(1)}, f32[32,128]{1,0:T(8,128)S(1)}, u32[]{:S(2)}, u32[]{:S(2)}) collective-permute-start(f32[32,128]{1,0:T(8,128)S(1)} %add.205), channel_id=1, source_target_pairs={{0,6},{1,7},{2,4},{3,5},{4,2},{5,3},{6,0},{7,1},{8,14},{9,15},{10,... | collective-permute-start | bytes 49160 | tf_op jit(solution)/shard_map/ppermute | solution.py:308
  54.7 4.0 %collective-permute-start.18 = (f32[32,128]{1,0:T(8,128)S(1)}, f32[32,128]{1,0:T(8,128)S(1)}, u32[]{:S(2)}, u32[]{:S(2)}) collective-permute-start(f32[32,128]{1,0:T(8,128)S(1)} %add.205), channel_id=1, source_target_pairs={{0,4},{1,5},{2,6},{3,7},{4,0},{5,1},{6,2},{7,3},{8,12},{9,13},{10,... | collective-permute-start | bytes 49160 | tf_op jit(solution)/shard_map/ppermute | solution.py:308
  56.4 3.7 %collective-permute-start.17 = (f32[32,128]{1,0:T(8,128)S(1)}, f32[32,128]{1,0:T(8,128)S(1)}, u32[]{:S(2)}, u32[]{:S(2)}) collective-permute-start(f32[32,128]{1,0:T(8,128)S(1)} %add.205), channel_id=1, source_target_pairs={{0,2},{1,3},{2,0},{3,1},{4,6},{5,7},{6,4},{7,5},{8,10},{9,11},{10,... | collective-permute-start | bytes 49160 | tf_op jit(solution)/shard_map/ppermute | solution.py:308
  60.1 5.6 %collective-permute-start.22 = (f32[32,128]{1,0:T(8,128)S(1)}, f32[32,128]{1,0:T(8,128)S(1)}, u32[]{:S(2)}, u32[]{:S(2)}) collective-permute-start(f32[32,128]{1,0:T(8,128)S(1)} %add_add_fusion), channel_id=1, source_target_pairs={{0,24},{1,25},{2,26},{3,27},{4,28},{5,29},{6,30},{7,31},{8,16},{9,... | collective-permute-start | bytes 49160 | tf_op jit(solution)/shard_map/ppermute | solution.py:308
  61.3 4.6 %collective-permute-start.21 = (f32[32,128]{1,0:T(8,128)S(1)}, f32[32,128]{1,0:T(8,128)S(1)}, u32[]{:S(2)}, u32[]{:S(2)}) collective-permute-start(f32[32,128]{1,0:T(8,128)S(1)} %add_add_fusion), channel_id=1, source_target_pairs={{0,16},{1,17},{2,18},{3,19},{4,20},{5,21},{6,22},{7,23},{8,24},{9,... | collective-permute-start | bytes 49160 | tf_op jit(solution)/shard_map/ppermute | solution.py:308
  62.1 4.2 %collective-permute-start.20 = (f32[32,128]{1,0:T(8,128)S(1)}, f32[32,128]{1,0:T(8,128)S(1)}, u32[]{:S(2)}, u32[]{:S(2)}) collective-permute-start(f32[32,128]{1,0:T(8,128)S(1)} %add_add_fusion), channel_id=1, source_target_pairs={{0,8},{1,9},{2,10},{3,11},{4,12},{5,13},{6,14},{7,15},{8,0},{9,1},... | collective-permute-start | bytes 49160 | tf_op jit(solution)/shard_map/ppermute | solution.py:308
  70.3 12.4 %all-to-all-start = ((f32[32,8,128]{2,1,0:T(8,128)}), f32[32,8,128]{2,1,0:T(8,128)S(1)}, u32[]{:S(2)}, u32[]{:S(2)}) async-start(f32[32,8,128]{2,1,0:T(8,128)} %bitcast.8), calls=%async_computation | async-start | bytes 262144 | tf_op jit(solution)/shard_map/all_to_all | solution.py:323

commit v4 on v3

--- a/solution.py
+++ b/solution.py
@@ -113,7 +113,7 @@
     own_blocks = own_hbm.shape[0] // BLK
     for index, piece in enumerate(pieces):
         start = table.offset(index + 1) // BLK
-        for block in range(own_blocks):
+        for block in range(piece.shape[0] // BLK):
             ref[start + block] = piece[BLK * block : BLK * (block + 1), :].T
     copies[0].wait()
 
@@ -144,6 +144,8 @@
                 )
                 tile = tile * scale
                 scores[place, :, span(pair)] = tile
+                if len(pair) == 1:
+                    scores[place, :, span([count])] = jnp.zeros_like(tile)
                 top = halves(jnp.maximum, tile + pair_row(pot, table, place, pair))
                 peak = top if peak is None else jnp.maximum(peak, top)
             peaks.append(peak)
@@ -270,6 +272,14 @@
         sums[group] = total
 
 
+def in_hbm(value):
+    return pltpu.with_memory_space_constraint(value, pltpu.HBM)
+
+
+def in_vmem(value):
+    return pltpu.with_memory_space_constraint(value, pltpu.VMEM)
+
+
 def call(kernel, ins, outs, scratch, aliases={}):
     return pl.pallas_call(
         kernel,
@@ -330,9 +340,29 @@
             mask //= 2
         return [held[key] for key in range(self.width)]
 
-    def offsets(self, rows):
+    def gather_pieces(self, value):
         me = lax.axis_index("nar")
-        return jnp.stack([(key ^ me) * rows for key in range(self.width)]).astype(jnp.int32)
+        side = lax.axis_index("grp") % 2
+        rows = value.shape[0]
+        cut = rows // 4 // BLK * BLK
+        parted = self.width > 2 and self.groups % 2 == 0 and cut > 0
+        mask = self.width // 2
+        held = {0: [(value, 0)]}
+        while mask:
+            for key, pieces in list(held.items()):
+                if parted and key == 0 and mask == self.width // 2:
+                    start = side * (rows - cut)
+                    near = self.swap(lax.dynamic_slice_in_dim(value, start, cut, 0), mask)
+                    middle = self.swap(value[cut : rows - cut], mask)
+                    far = self.swap(near, self.width)
+                    got = [(near, start), (far, (1 - side) * (rows - cut)), (middle, cut)]
+                else:
+                    got = [(self.swap(part, mask), start) for part, start in pieces]
+                held[key ^ mask] = got
+            mask //= 2
+        parts = [part for key in held for part, _ in held[key]]
+        starts = [(key ^ me) * rows + start for key in held for _, start in held[key]]
+        return parts, jnp.stack([jnp.asarray(start, jnp.int32) for start in starts])
 
     def arrange(self, parts):
         me = lax.axis_index("nar")
@@ -356,10 +386,10 @@
     f32 = jnp.float32
 
     shape = (own_blocks, BLK)
-    pot = links.arrange(links.gather(ref_start.reshape(shape))) * (2.0 * LOG2E)
-    log_ref = jnp.log2(links.arrange(links.gather(ref_mass.reshape(shape))))
-    pieces = links.gather(ref_desc)
-    offsets = links.offsets(ref_desc.shape[0])
+    both = links.gather(jnp.stack([ref_start.reshape(shape), ref_mass.reshape(shape)]))
+    pot = links.arrange([part[0] for part in both]) * (2.0 * LOG2E)
+    log_ref = jnp.log2(links.arrange([part[1] for part in both]))
+    pieces, offsets = links.gather_pieces(ref_desc)
     blocks = jnp.arange(run_blocks, dtype=jnp.int32)
     rank_key = live_slots * run_blocks - blocks
     place = jnp.sum((rank_key[None, :] > rank_key[:, None]).astype(jnp.int32), axis=1)
@@ -375,6 +405,7 @@
     onehot = (
         eff.reshape(1, tiles) == jnp.arange(ref_blocks, dtype=jnp.int32)[:, None]
     ).astype(f32)
+
     def padded(table):
         return jnp.concatenate([table, jnp.full((8, BLK), FLOOR, f32)], axis=0)
 
@@ -396,9 +427,9 @@
         ],
     )(
         table,
-        pltpu.with_memory_space_constraint(run_desc, pltpu.HBM),
-        pltpu.with_memory_space_constraint(run_mass.reshape(run_blocks, BLK), pltpu.HBM),
-        pltpu.with_memory_space_constraint(pieces[0], pltpu.HBM),
+        in_hbm(run_desc),
+        in_hbm(run_mass.reshape(run_blocks, BLK)),
+        in_hbm(pieces[0]),
         padded(pot),
         slot_ref,
         *pieces[1:],
@@ -408,7 +439,7 @@
 
     weights, peaks, sums = call(
         second_kernel, [smem] + [vmem] * 4, [score_shape, rep_shape, table_shape], [rows], {1: 0}
-    )(table, pltpu.with_memory_space_constraint(scores, pltpu.VMEM), padded(pot), log_mass, onehot)
+    )(table, in_vmem(scores), padded(pot), log_mass, onehot)
     log_gain = log_ref - jnp.log2(links.reduce_all(sums, plain_sum))
     pot = pot + log_gain
     gain = jnp.concatenate([jnp.exp2(log_gain), jnp.zeros((8, BLK), f32)], axis=0)
@@ -421,7 +452,7 @@
             jax.ShapeDtypeStruct((links.groups, ref_blocks, BLK), f32),
         ],
         [rows],
-    )(table, pltpu.with_memory_space_constraint(weights, pltpu.VMEM), pltpu.with_memory_space_constraint(peaks, pltpu.VMEM), gain, log_mass, onehot)
+    )(table, in_vmem(weights), in_vmem(peaks), gain, log_mass, onehot)
     total = links.reduce_own(sums, plain_sum)
     start = lax.axis_index("nar") * own_blocks
 

time: 83.9 us -> 83.5 us (level)
  waiting for transfers between devices: 32.3 us -> 26.6 us
  starting transfers between devices: 25.9 us -> 30.8 us
  Pallas kernels: 19.5 us -> 16.9 us
  local copies, waits for them, and re-layouts: 0.38 us -> 2.26 us
    ppermute x23 -> x24, waiting for transfers between devices: 24.1 us -> 18.3 us  [swap(): return lax.ppermute(value, ('grp', 'nar'), pairs)]
    ppermute x23 -> x24, starting transfers between devices: 21.8 us -> 27.2 us  [swap(): return lax.ppermute(value, ('grp', 'nar'), pairs)]
    pallas_call x1, Pallas kernels: 10.4 us -> 9.22 us  [shards(): call(first_kernel, [smem] + [pl.BlockSpec(memory_space=pltpu.HBM)] * 3 +...]
    pallas_call x1, Pallas kernels: 5.11 us -> 4.03 us  [shards(): call(second_kernel, [smem] + [vmem] * 4, [score_shape, rep_shape, table_s...]
    slice x0 -> x1, local copies, waits for them, and re-layouts: none -> 0.97 us  [gather_pieces(): middle = self.swap(value[cut:rows - cut], mask)]
    dynamic_slice x0 -> x1, local copies, waits for them, and re-layouts: none -> 0.91 us  [gather_pieces(): near = self.swap(lax.dynamic_slice_in_dim(value, start, cut, 0), mask)]
  transfers between devices with their start and end apart: 24 -> 25, of which waited for: 14 -> 16; matrix products, arithmetic and copies ran while one was open for 5% -> 7% of each run, Pallas kernels for 0% -> 0%
where the time goes in v4:
time: 83.5 us; the launch traced here: 82.5 us
  starting transfers between devices  30.8 us (37%)
  waiting for transfers between devices  26.6 us (32%)
  Pallas kernels  16.9 us (20%)
  other arithmetic  5.16 us (6%)
  local copies, waits for them, and re-layouts  2.26 us (3%)
    ppermute x24, starting transfers between devices, swap(): return lax.ppermute(value, ('grp', 'nar'), pairs)  27.2 us
    ppermute x24, waiting for transfers between devices, swap(): return lax.ppermute(value, ('grp', 'nar'), pairs)  18.3 us
    pallas_call x1, Pallas kernels, shards(): call(first_kernel, [smem] + [pl.BlockSpec(memory_space=pltpu.HBM)] * 3 +...  9.22 us
    all_to_all x1, waiting for transfers between devices, reduce_own(): return join(list(lax.all_to_all(sent, ('grp', 'nar'), 0, 0, tiled=True)))  8.22 us
    pallas_call x1, Pallas kernels, shards(): call(second_kernel, [smem] + [vmem] * 4, [score_shape, rep_shape, table_s...  4.03 us
    pallas_call x1, Pallas kernels, shards(): call(third_kernel, [smem] + [vmem] * 5, [jax.ShapeDtypeStruct((run_blocks...  3.6 us
    all_to_all x1, starting transfers between devices, reduce_own(): return join(list(lax.all_to_all(sent, ('grp', 'nar'), 0, 0, tiled=True)))  3.6 us
  transfers between devices with their start and end apart: 25, of which 16 were waited for; matrix products, arithmetic and copies ran while one was open for 7% of the time, Pallas kernels for 0%

profile of v4, /device:TPU:0, one launch (start us, length us, event | category | flops | bytes accessed | tf_op | source)
XLA Modules:
  0.0 82.5 jit_solution(10681354065292647433)
XLA Ops:
  0.6 0.7 pad_maximum_fusion
  1.8 2.5 %collective-permute-start = (f32[2,8,128]{2,1,0:T(8,128)S(1)}, f32[2,8,128]{2,1,0:T(8,128)S(1)}, u32[]{:S(2)}, u32[]{:S(2)}) collective-permute-start(f32[2,8,128]{2,1,0:T(8,128)S(1)} %pad_maximum_fusion), channel_id=1, source_target_pairs={{0,2},{1,3},{2,0},{3,1},{4,6},{5,7},{6,4},{7,5},{8,10},{9,11},{10,... | collective-permute-start | bytes 24584 | tf_op jit(solution)/shard_map/ppermute | solution.py:318
  4.5 0.9 %constant_dynamic-slice_fusion = bf16[256,256]{1,0:T(8,128)(2,1)S(1)} fusion(bf16[1024,256]{1,0:T(8,128)(2,1)} %own_hbm.1, s32[]{:T(128)S(6)} %select_n.141), kind=kLoop, calls=%fused_computation.93 | loop fusion | bytes 262148 | tf_op jit(solution)/shard_map/dynamic_slice | solution.py:355
  5.8 1.0 %slice.24 = bf16[512,256]{1,0:T(8,128)(2,1)S(1)} slice(bf16[1024,256]{1,0:T(8,128)(2,1)} %own_hbm.1), slice={[256:768], [0:256]} | slice | bytes 524288 | tf_op jit(solution)/shard_map/slice | solution.py:356
  6.8 1.8 %collective-permute-start.5 = (bf16[512,256]{1,0:T(8,128)(2,1)S(1)}, bf16[512,256]{1,0:T(8,128)(2,1)S(1)}, u32[]{:S(2)}, u32[]{:S(2)}) collective-permute-start(bf16[512,256]{1,0:T(8,128)(2,1)S(1)} %slice.24), channel_id=1, source_target_pairs={{0,2},{1,3},{2,0},{3,1},{4,6},{5,7},{6,4},{7,5},{8,10},{9,11},{10,... | collective-permute-start | bytes 786440 | tf_op jit(solution)/shard_map/ppermute | solution.py:318
  9.4 0.8 select_reduce_fusion.1
  10.3 1.3 %select_reduce_fusion = s32[32,8]{1,0:T(8,128)S(1)} fusion(s32[32,8]{0,1:T(8,128)} %param.9, pred[32,32]{1,0:T(8,128)(4,1)S(1)} %iota_compare_fusion.2), kind=kLoop, calls=%fused_computation | loop fusion | flops 16128 | bytes 3072 | tf_op jit(solution)/shard_map/reduce_sum | solution.py:398
  11.9 1.6 %collective-permute-start.4 = (bf16[256,256]{1,0:T(8,128)(2,1)S(1)}, bf16[256,256]{1,0:T(8,128)(2,1)S(1)}, u32[]{:S(2)}, u32[]{:S(2)}) collective-permute-start(bf16[256,256]{1,0:T(8,128)(2,1)S(1)} %collective-permute-done.3.rest_0_), channel_id=1, source_target_pairs={{0,4},{1,5},{2,6},{3,7},{4,0},{5,1},{6,2},{7,3},{8,12},{9,13},{10,... | collective-permute-start | bytes 393224 | tf_op jit(solution)/shard_map/ppermute | solution.py:318
  13.8 4.0 %collective-permute-done.4.rest_1_ = bf16[256,256]{1,0:T(8,128)(2,1)S(1)} collective-permute-done((bf16[256,256]{1,0:T(8,128)(2,1)S(1)}, bf16[256,256]{1,0:T(8,128)(2,1)S(1)}, u32[]{:S(2)}, u32[]{:S(2)}) %collective-permute-start.4) | collective-permute-done | bytes 131104 | tf_op jit(solution)/shard_map/ppermute | solution.py:318
  19.6 9.2 %shard_map.86 = (f32[32,128,1024]{2,1,0:T(8,128)S(1)}, f32[4096,128]{1,0:T(8,128)S(1)}, f32[32,128]{1,0:T(8,128)S(1)}) custom-call(s32[584]{0:T(1024)S(1)} %concatenate.18.table, bf16[4096,256]{1,0:T(8,128)(2,1)} %run_hbm.1, f32[32,128]{1,0:T(8,128)} %bitcast.85, bf16[1024,256]{1,0:T(8,128)(2,1)} %own_hbm.1, f32[40,128]{1,0:T(8,128)S(1)} %concatenate.20.pot, ...), custom_call_target="tpu_custom_call" | custom-call | tf_op jit(solution)/shard_map/pallas_call | solution.py:416
  28.9 1.2 %collective-permute-done.10 = f32[32,128]{1,0:T(8,128)S(1)} collective-permute-done((f32[32,128]{1,0:T(8,128)S(1)}, f32[32,128]{1,0:T(8,128)S(1)}, u32[]{:S(2)}, u32[]{:S(2)}) %collective-permute-start.10) | collective-permute-done | bytes 16416 | tf_op jit(solution)/shard_map/ppermute | solution.py:318
  30.1 3.4 %collective-permute-start.13 = (f32[32,128]{1,0:T(8,128)S(1)}, f32[32,128]{1,0:T(8,128)S(1)}, u32[]{:S(2)}, u32[]{:S(2)}) collective-permute-start(f32[32,128]{1,0:T(8,128)S(1)} %multiply_add_fusion.1), channel_id=1, source_target_pairs={{0,6},{1,7},{2,4},{3,5},{4,2},{5,3},{6,0},{7,1},{8,14},{9,15},{10,... | collective-permute-start | bytes 49160 | tf_op jit(solution)/shard_map/ppermute | solution.py:318
  33.5 0.9 %collective-permute-start.12 = (f32[32,128]{1,0:T(8,128)S(1)}, f32[32,128]{1,0:T(8,128)S(1)}, u32[]{:S(2)}, u32[]{:S(2)}) collective-permute-start(f32[32,128]{1,0:T(8,128)S(1)} %multiply_add_fusion.1), channel_id=1, source_target_pairs={{0,4},{1,5},{2,6},{3,7},{4,0},{5,1},{6,2},{7,3},{8,12},{9,13},{10,... | collective-permute-start | bytes 49160 | tf_op jit(solution)/shard_map/ppermute | solution.py:318
  34.4 1.2 %collective-permute-start.11 = (f32[32,128]{1,0:T(8,128)S(1)}, f32[32,128]{1,0:T(8,128)S(1)}, u32[]{:S(2)}, u32[]{:S(2)}) collective-permute-start(f32[32,128]{1,0:T(8,128)S(1)} %multiply_add_fusion.1), channel_id=1, source_target_pairs={{0,2},{1,3},{2,0},{3,1},{4,6},{5,7},{6,4},{7,5},{8,10},{9,11},{10,... | collective-permute-start | bytes 49160 | tf_op jit(solution)/shard_map/ppermute | solution.py:318
  35.7 1.6 %collective-permute-done.12 = f32[32,128]{1,0:T(8,128)S(1)} collective-permute-done((f32[32,128]{1,0:T(8,128)S(1)}, f32[32,128]{1,0:T(8,128)S(1)}, u32[]{:S(2)}, u32[]{:S(2)}) %collective-permute-start.12) | collective-permute-done | bytes 16416 | tf_op jit(solution)/shard_map/ppermute | solution.py:318
  37.2 0.9 %collective-permute-done.11 = f32[32,128]{1,0:T(8,128)S(1)} collective-permute-done((f32[32,128]{1,0:T(8,128)S(1)}, f32[32,128]{1,0:T(8,128)S(1)}, u32[]{:S(2)}, u32[]{:S(2)}) %collective-permute-start.11) | collective-permute-done | bytes 16416 | tf_op jit(solution)/shard_map/ppermute | solution.py:318
  38.2 3.4 %collective-permute-start.16 = (f32[32,128]{1,0:T(8,128)S(1)}, f32[32,128]{1,0:T(8,128)S(1)}, u32[]{:S(2)}, u32[]{:S(2)}) collective-permute-start(f32[32,128]{1,0:T(8,128)S(1)} %multiply_add_fusion), channel_id=1, source_target_pairs={{0,24},{1,25},{2,26},{3,27},{4,28},{5,29},{6,30},{7,31},{8,16},{9,... | collective-permute-start | bytes 49160 | tf_op jit(solution)/shard_map/ppermute | solution.py:318
  41.6 1.1 %collective-permute-start.14 = (f32[32,128]{1,0:T(8,128)S(1)}, f32[32,128]{1,0:T(8,128)S(1)}, u32[]{:S(2)}, u32[]{:S(2)}) collective-permute-start(f32[32,128]{1,0:T(8,128)S(1)} %multiply_add_fusion), channel_id=1, source_target_pairs={{0,8},{1,9},{2,10},{3,11},{4,12},{5,13},{6,14},{7,15},{8,0},{9,1},... | collective-permute-start | bytes 49160 | tf_op jit(solution)/shard_map/ppermute | solution.py:318
  42.6 1.1 %collective-permute-done.16 = f32[32,128]{1,0:T(8,128)S(1)} collective-permute-done((f32[32,128]{1,0:T(8,128)S(1)}, f32[32,128]{1,0:T(8,128)S(1)}, u32[]{:S(2)}, u32[]{:S(2)}) %collective-permute-start.16) | collective-permute-done | bytes 16416 | tf_op jit(solution)/shard_map/ppermute | solution.py:318
  43.8 2.4 %collective-permute-done.15 = f32[32,128]{1,0:T(8,128)S(1)} collective-permute-done((f32[32,128]{1,0:T(8,128)S(1)}, f32[32,128]{1,0:T(8,128)S(1)}, u32[]{:S(2)}, u32[]{:S(2)}) %collective-permute-start.15) | collective-permute-done | bytes 16416 | tf_op jit(solution)/shard_map/ppermute | solution.py:318
  46.2 4.0 %shard_map.87 = (f32[32,128,1024]{2,1,0:T(8,128)S(1)}, f32[4096,128]{1,0:T(8,128)S(1)}, f32[32,128]{1,0:T(8,128)S(1)}) custom-call(s32[584]{0:T(1024)S(1)} %concatenate.18.table, f32[32,128,1024]{2,1,0:T(8,128)S(1)} %get-tuple-element.10.scores, f32[40,128]{1,0:T(8,128)S(1)} %concatenate.22.pot, ...), custom_call_target="tpu_custom_call", output_to_operand_aliasing={{0}: (1, {})} | custom-call | tf_op jit(solution)/shard_map/pallas_call | solution.py:440
  50.4 1.2 %collective-permute-done.17 = f32[32,128]{1,0:T(8,128)S(1)} collective-permute-done((f32[32,128]{1,0:T(8,128)S(1)}, f32[32,128]{1,0:T(8,128)S(1)}, u32[]{:S(2)}, u32[]{:S(2)}) %collective-permute-start.17) | collective-permute-done | bytes 16416 | tf_op jit(solution)/shard_map/ppermute | solution.py:318
  51.5 4.3 %collective-permute-start.20 = (f32[32,128]{1,0:T(8,128)S(1)}, f32[32,128]{1,0:T(8,128)S(1)}, u32[]{:S(2)}, u32[]{:S(2)}) collective-permute-start(f32[32,128]{1,0:T(8,128)S(1)} %add.238), channel_id=1, source_target_pairs={{0,6},{1,7},{2,4},{3,5},{4,2},{5,3},{6,0},{7,1},{8,14},{9,15},{10,... | collective-permute-start | bytes 49160 | tf_op jit(solution)/shard_map/ppermute | solution.py:318
  56.5 1.1 %collective-permute-done.20 = f32[32,128]{1,0:T(8,128)S(1)} collective-permute-done((f32[32,128]{1,0:T(8,128)S(1)}, f32[32,128]{1,0:T(8,128)S(1)}, u32[]{:S(2)}, u32[]{:S(2)}) %collective-permute-start.20) | collective-permute-done | bytes 16416 | tf_op jit(solution)/shard_map/ppermute | solution.py:318
  57.6 1.9 %collective-permute-done.19 = f32[32,128]{1,0:T(8,128)S(1)} collective-permute-done((f32[32,128]{1,0:T(8,128)S(1)}, f32[32,128]{1,0:T(8,128)S(1)}, u32[]{:S(2)}, u32[]{:S(2)}) %collective-permute-start.19) | collective-permute-done | bytes 16416 | tf_op jit(solution)/shard_map/ppermute | solution.py:318
  60.2 1.0 %collective-permute-start.23 = (f32[32,128]{1,0:T(8,128)S(1)}, f32[32,128]{1,0:T(8,128)S(1)}, u32[]{:S(2)}, u32[]{:S(2)}) collective-permute-start(f32[32,128]{1,0:T(8,128)S(1)} %add_add_fusion), channel_id=1, source_target_pairs={{0,24},{1,25},{2,26},{3,27},{4,28},{5,29},{6,30},{7,31},{8,16},{9,... | collective-permute-start | bytes 49160 | tf_op jit(solution)/shard_map/ppermute | solution.py:318
  61.2 1.1 %collective-permute-start.22 = (f32[32,128]{1,0:T(8,128)S(1)}, f32[32,128]{1,0:T(8,128)S(1)}, u32[]{:S(2)}, u32[]{:S(2)}) collective-permute-start(f32[32,128]{1,0:T(8,128)S(1)} %add_add_fusion), channel_id=1, source_target_pairs={{0,16},{1,17},{2,18},{3,19},{4,20},{5,21},{6,22},{7,23},{8,24},{9,... | collective-permute-start | bytes 49160 | tf_op jit(solution)/shard_map/ppermute | solution.py:318
  62.4 2.3 %collective-permute-start.21 = (f32[32,128]{1,0:T(8,128)S(1)}, f32[32,128]{1,0:T(8,128)S(1)}, u32[]{:S(2)}, u32[]{:S(2)}) collective-permute-start(f32[32,128]{1,0:T(8,128)S(1)} %add_add_fusion), channel_id=1, source_target_pairs={{0,8},{1,9},{2,10},{3,11},{4,12},{5,13},{6,14},{7,15},{8,0},{9,1},... | collective-permute-start | bytes 49160 | tf_op jit(solution)/shard_map/ppermute | solution.py:318
  64.7 1.2 %collective-permute-done.23 = f32[32,128]{1,0:T(8,128)S(1)} collective-permute-done((f32[32,128]{1,0:T(8,128)S(1)}, f32[32,128]{1,0:T(8,128)S(1)}, u32[]{:S(2)}, u32[]{:S(2)}) %collective-permute-start.23) | collective-permute-done | bytes 16416 | tf_op jit(solution)/shard_map/ppermute | solution.py:318
  66.4 3.6 %shard_map.88 = (f32[32,128]{1,0:T(8,128)}, f32[8,32,128]{2,1,0:T(8,128)}) custom-call(s32[584]{0:T(1024)S(1)} %concatenate.18.table, f32[32,128,1024]{2,1,0:T(8,128)S(1)} %get-tuple-element.13.weights, f32[4096,128]{1,0:T(8,128)S(1)} %get-tuple-element.14.peaks, f32[40,128]{1,0:T(8,128)S(1)} %concatenate.23.gain, ...), custom_call_target="tpu_custom_call" | custom-call | tf_op jit(solution)/shard_map/pallas_call | solution.py:447
  70.0 3.6 %all-to-all-start = ((f32[32,8,128]{2,1,0:T(8,128)}), f32[32,8,128]{2,1,0:T(8,128)S(1)}, u32[]{:S(2)}, u32[]{:S(2)}) async-start(f32[32,8,128]{2,1,0:T(8,128)} %bitcast.20), calls=%async_computation | async-start | bytes 262144 | tf_op jit(solution)/shard_map/all_to_all | solution.py:333
  73.7 8.2 %all-to-all-done = f32[32,8,128]{2,1,0:T(8,128)S(1)} async-done(((f32[32,8,128]{2,1,0:T(8,128)}), f32[32,8,128]{2,1,0:T(8,128)S(1)}, u32[]{:S(2)}, u32[]{:S(2)}) %all-to-all-start) | async-done | bytes 131104 | tf_op jit(solution)/shard_map/all_to_all | solution.py:333
  (51 shorter events, 7.1 us)
Async XLA Ops:
  1.3 12.2 %collective-permute-start.2 = (f32[2,8,128]{2,1,0:T(8,128)S(1)}, f32[2,8,128]{2,1,0:T(8,128)S(1)}, u32[]{:S(2)}, u32[]{:S(2)}) collective-permute-start(f32[2,8,128]{2,1,0:T(8,128)S(1)} %pad_maximum_fusion), channel_id=1, source_target_pairs={{0,1},{1,0},{2,3},{3,2},{4,5},{5,4},{6,7},{7,6},{8,9},{9,8},{10,11... | collective-permute-start | bytes 24584 | tf_op jit(solution)/shard_map/ppermute | solution.py:318
  1.8 10.0 %collective-permute-start = (f32[2,8,128]{2,1,0:T(8,128)S(1)}, f32[2,8,128]{2,1,0:T(8,128)S(1)}, u32[]{:S(2)}, u32[]{:S(2)}) collective-permute-start(f32[2,8,128]{2,1,0:T(8,128)S(1)} %pad_maximum_fusion), channel_id=1, source_target_pairs={{0,2},{1,3},{2,0},{3,1},{4,6},{5,7},{6,4},{7,5},{8,10},{9,11},{10,... | collective-permute-start | bytes 24584 | tf_op jit(solution)/shard_map/ppermute | solution.py:318
  4.3 15.2 %collective-permute-start.6 = (bf16[1024,256]{1,0:T(8,128)(2,1)}, bf16[1024,256]{1,0:T(8,128)(2,1)S(1)}, u32[]{:S(2)}, u32[]{:S(2)}) collective-permute-start(bf16[1024,256]{1,0:T(8,128)(2,1)} %own_hbm.1), channel_id=1, source_target_pairs={{0,1},{1,0},{2,3},{3,2},{4,5},{5,4},{6,7},{7,6},{8,9},{9,8},{10,11... | collective-permute-start | bytes 1572872 | tf_op jit(solution)/shard_map/ppermute | solution.py:318
  5.5 6.4 %collective-permute-start.3 = (bf16[256,256]{1,0:T(8,128)(2,1)S(1)}, bf16[256,256]{1,0:T(8,128)(2,1)S(1)}, u32[]{:S(2)}, u32[]{:S(2)}) collective-permute-start(bf16[256,256]{1,0:T(8,128)(2,1)S(1)} %constant_dynamic-slice_fusion), channel_id=1, source_target_pairs={{0,2},{1,3},{2,0},{3,1},{4,6},{5,7},{6,4},{7,5},{8,10},{9,11},{10,... | collective-permute-start | bytes 393224 | tf_op jit(solution)/shard_map/ppermute | solution.py:318
  6.8 11.0 %collective-permute-start.5 = (bf16[512,256]{1,0:T(8,128)(2,1)S(1)}, bf16[512,256]{1,0:T(8,128)(2,1)S(1)}, u32[]{:S(2)}, u32[]{:S(2)}) collective-permute-start(bf16[512,256]{1,0:T(8,128)(2,1)S(1)} %slice.24), channel_id=1, source_target_pairs={{0,2},{1,3},{2,0},{3,1},{4,6},{5,7},{6,4},{7,5},{8,10},{9,11},{10,... | collective-permute-start | bytes 786440 | tf_op jit(solution)/shard_map/ppermute | solution.py:318
  11.8 6.5 %collective-permute-start.1 = (f32[2,8,128]{2,1,0:T(8,128)S(1)}, f32[2,8,128]{2,1,0:T(8,128)S(1)}, u32[]{:S(2)}, u32[]{:S(2)}) collective-permute-start(f32[2,8,128]{2,1,0:T(8,128)S(1)} %collective-permute-done), channel_id=1, source_target_pairs={{0,1},{1,0},{2,3},{3,2},{4,5},{5,4},{6,7},{7,6},{8,9},{9,8},{10,11... | collective-permute-start | bytes 24584 | tf_op jit(solution)/shard_map/ppermute | solution.py:318
  11.9 5.9 %collective-permute-start.4 = (bf16[256,256]{1,0:T(8,128)(2,1)S(1)}, bf16[256,256]{1,0:T(8,128)(2,1)S(1)}, u32[]{:S(2)}, u32[]{:S(2)}) collective-permute-start(bf16[256,256]{1,0:T(8,128)(2,1)S(1)} %collective-permute-done.3.rest_0_), channel_id=1, source_target_pairs={{0,4},{1,5},{2,6},{3,7},{4,0},{5,1},{6,2},{7,3},{8,12},{9,13},{10,... | collective-permute-start | bytes 393224 | tf_op jit(solution)/shard_map/ppermute | solution.py:318
  13.5 5.5 %collective-permute-start.7 = (bf16[256,256]{1,0:T(8,128)(2,1)S(1)}, bf16[256,256]{1,0:T(8,128)(2,1)S(1)}, u32[]{:S(2)}, u32[]{:S(2)}) collective-permute-start(bf16[256,256]{1,0:T(8,128)(2,1)S(1)} %collective-permute-done.3.rest_0_), channel_id=1, source_target_pairs={{0,1},{1,0},{2,3},{3,2},{4,5},{5,4},{6,7},{7,6},{8,9},{9,8},{10,11... | collective-permute-start | bytes 393224 | tf_op jit(solution)/shard_map/ppermute | solution.py:318
  17.8 1.3 %collective-permute-start.8 = (bf16[256,256]{1,0:T(8,128)(2,1)S(1)}, bf16[256,256]{1,0:T(8,128)(2,1)S(1)}, u32[]{:S(2)}, u32[]{:S(2)}) collective-permute-start(bf16[256,256]{1,0:T(8,128)(2,1)S(1)} %collective-permute-done.4.rest_1_), channel_id=1, source_target_pairs={{0,1},{1,0},{2,3},{3,2},{4,5},{5,4},{6,7},{7,6},{8,9},{9,8},{10,11... | collective-permute-start | bytes 393224 | tf_op jit(solution)/shard_map/ppermute | solution.py:318
  17.8 1.7 %collective-permute-start.9 = (bf16[512,256]{1,0:T(8,128)(2,1)S(1)}, bf16[512,256]{1,0:T(8,128)(2,1)S(1)}, u32[]{:S(2)}, u32[]{:S(2)}) collective-permute-start(bf16[512,256]{1,0:T(8,128)(2,1)S(1)} %collective-permute-done.5.rest_2_), channel_id=1, source_target_pairs={{0,1},{1,0},{2,3},{3,2},{4,5},{5,4},{6,7},{7,6},{8,9},{9,8},{10,11... | collective-permute-start | bytes 786440 | tf_op jit(solution)/shard_map/ppermute | solution.py:318
  19.6 23.0 %copy-start = (f32[1024]{0:T(1024)S(1)}, f32[1024]{0:T(1024)}, u32[]{:S(2)}) copy-start(f32[1024]{0:T(1024)} %param.12) | copy-start | bytes 12292
  28.8 1.2 %collective-permute-start.10 = (f32[32,128]{1,0:T(8,128)S(1)}, f32[32,128]{1,0:T(8,128)S(1)}, u32[]{:S(2)}, u32[]{:S(2)}) collective-permute-start(f32[32,128]{1,0:T(8,128)S(1)} %get-tuple-element.11), channel_id=1, source_target_pairs={{0,1},{1,0},{2,3},{3,2},{4,5},{5,4},{6,7},{7,6},{8,9},{9,8},{10,11... | collective-permute-start | bytes 49160 | tf_op jit(solution)/shard_map/ppermute | solution.py:318
  30.1 5.5 %collective-permute-start.13 = (f32[32,128]{1,0:T(8,128)S(1)}, f32[32,128]{1,0:T(8,128)S(1)}, u32[]{:S(2)}, u32[]{:S(2)}) collective-permute-start(f32[32,128]{1,0:T(8,128)S(1)} %multiply_add_fusion.1), channel_id=1, source_target_pairs={{0,6},{1,7},{2,4},{3,5},{4,2},{5,3},{6,0},{7,1},{8,14},{9,15},{10,... | collective-permute-start | bytes 49160 | tf_op jit(solution)/shard_map/ppermute | solution.py:318
  33.5 3.7 %collective-permute-start.12 = (f32[32,128]{1,0:T(8,128)S(1)}, f32[32,128]{1,0:T(8,128)S(1)}, u32[]{:S(2)}, u32[]{:S(2)}) collective-permute-start(f32[32,128]{1,0:T(8,128)S(1)} %multiply_add_fusion.1), channel_id=1, source_target_pairs={{0,4},{1,5},{2,6},{3,7},{4,0},{5,1},{6,2},{7,3},{8,12},{9,13},{10,... | collective-permute-start | bytes 49160 | tf_op jit(solution)/shard_map/ppermute | solution.py:318
  34.4 3.7 %collective-permute-start.11 = (f32[32,128]{1,0:T(8,128)S(1)}, f32[32,128]{1,0:T(8,128)S(1)}, u32[]{:S(2)}, u32[]{:S(2)}) collective-permute-start(f32[32,128]{1,0:T(8,128)S(1)} %multiply_add_fusion.1), channel_id=1, source_target_pairs={{0,2},{1,3},{2,0},{3,1},{4,6},{5,7},{6,4},{7,5},{8,10},{9,11},{10,... | collective-permute-start | bytes 49160 | tf_op jit(solution)/shard_map/ppermute | solution.py:318
  38.2 5.6 %collective-permute-start.16 = (f32[32,128]{1,0:T(8,128)S(1)}, f32[32,128]{1,0:T(8,128)S(1)}, u32[]{:S(2)}, u32[]{:S(2)}) collective-permute-start(f32[32,128]{1,0:T(8,128)S(1)} %multiply_add_fusion), channel_id=1, source_target_pairs={{0,24},{1,25},{2,26},{3,27},{4,28},{5,29},{6,30},{7,31},{8,16},{9,... | collective-permute-start | bytes 49160 | tf_op jit(solution)/shard_map/ppermute | solution.py:318
  41.5 4.6 %collective-permute-start.15 = (f32[32,128]{1,0:T(8,128)S(1)}, f32[32,128]{1,0:T(8,128)S(1)}, u32[]{:S(2)}, u32[]{:S(2)}) collective-permute-start(f32[32,128]{1,0:T(8,128)S(1)} %multiply_add_fusion), channel_id=1, source_target_pairs={{0,16},{1,17},{2,18},{3,19},{4,20},{5,21},{6,22},{7,23},{8,24},{9,... | collective-permute-start | bytes 49160 | tf_op jit(solution)/shard_map/ppermute | solution.py:318
  41.6 4.6 %collective-permute-start.14 = (f32[32,128]{1,0:T(8,128)S(1)}, f32[32,128]{1,0:T(8,128)S(1)}, u32[]{:S(2)}, u32[]{:S(2)}) collective-permute-start(f32[32,128]{1,0:T(8,128)S(1)} %multiply_add_fusion), channel_id=1, source_target_pairs={{0,8},{1,9},{2,10},{3,11},{4,12},{5,13},{6,14},{7,15},{8,0},{9,1},... | collective-permute-start | bytes 49160 | tf_op jit(solution)/shard_map/ppermute | solution.py:318
  50.3 1.2 %collective-permute-start.17 = (f32[32,128]{1,0:T(8,128)S(1)}, f32[32,128]{1,0:T(8,128)S(1)}, u32[]{:S(2)}, u32[]{:S(2)}) collective-permute-start(f32[32,128]{1,0:T(8,128)S(1)} %get-tuple-element.15), channel_id=1, source_target_pairs={{0,1},{1,0},{2,3},{3,2},{4,5},{5,4},{6,7},{7,6},{8,9},{9,8},{10,11... | collective-permute-start | bytes 49160 | tf_op jit(solution)/shard_map/ppermute | solution.py:318
  51.5 6.1 %collective-permute-start.20 = (f32[32,128]{1,0:T(8,128)S(1)}, f32[32,128]{1,0:T(8,128)S(1)}, u32[]{:S(2)}, u32[]{:S(2)}) collective-permute-start(f32[32,128]{1,0:T(8,128)S(1)} %add.238), channel_id=1, source_target_pairs={{0,6},{1,7},{2,4},{3,5},{4,2},{5,3},{6,0},{7,1},{8,14},{9,15},{10,... | collective-permute-start | bytes 49160 | tf_op jit(solution)/shard_map/ppermute | solution.py:318
  55.8 3.7 %collective-permute-start.19 = (f32[32,128]{1,0:T(8,128)S(1)}, f32[32,128]{1,0:T(8,128)S(1)}, u32[]{:S(2)}, u32[]{:S(2)}) collective-permute-start(f32[32,128]{1,0:T(8,128)S(1)} %add.238), channel_id=1, source_target_pairs={{0,4},{1,5},{2,6},{3,7},{4,0},{5,1},{6,2},{7,3},{8,12},{9,13},{10,... | collective-permute-start | bytes 49160 | tf_op jit(solution)/shard_map/ppermute | solution.py:318
  56.5 3.7 %collective-permute-start.18 = (f32[32,128]{1,0:T(8,128)S(1)}, f32[32,128]{1,0:T(8,128)S(1)}, u32[]{:S(2)}, u32[]{:S(2)}) collective-permute-start(f32[32,128]{1,0:T(8,128)S(1)} %add.238), channel_id=1, source_target_pairs={{0,2},{1,3},{2,0},{3,1},{4,6},{5,7},{6,4},{7,5},{8,10},{9,11},{10,... | collective-permute-start | bytes 49160 | tf_op jit(solution)/shard_map/ppermute | solution.py:318
  60.2 5.6 %collective-permute-start.23 = (f32[32,128]{1,0:T(8,128)S(1)}, f32[32,128]{1,0:T(8,128)S(1)}, u32[]{:S(2)}, u32[]{:S(2)}) collective-permute-start(f32[32,128]{1,0:T(8,128)S(1)} %add_add_fusion), channel_id=1, source_target_pairs={{0,24},{1,25},{2,26},{3,27},{4,28},{5,29},{6,30},{7,31},{8,16},{9,... | collective-permute-start | bytes 49160 | tf_op jit(solution)/shard_map/ppermute | solution.py:318
  61.2 4.8 %collective-permute-start.22 = (f32[32,128]{1,0:T(8,128)S(1)}, f32[32,128]{1,0:T(8,128)S(1)}, u32[]{:S(2)}, u32[]{:S(2)}) collective-permute-start(f32[32,128]{1,0:T(8,128)S(1)} %add_add_fusion), channel_id=1, source_target_pairs={{0,16},{1,17},{2,18},{3,19},{4,20},{5,21},{6,22},{7,23},{8,24},{9,... | collective-permute-start | bytes 49160 | tf_op jit(solution)/shard_map/ppermute | solution.py:318
  62.4 4.0 %collective-permute-start.21 = (f32[32,128]{1,0:T(8,128)S(1)}, f32[32,128]{1,0:T(8,128)S(1)}, u32[]{:S(2)}, u32[]{:S(2)}) collective-permute-start(f32[32,128]{1,0:T(8,128)S(1)} %add_add_fusion), channel_id=1, source_target_pairs={{0,8},{1,9},{2,10},{3,11},{4,12},{5,13},{6,14},{7,15},{8,0},{9,1},... | collective-permute-start | bytes 49160 | tf_op jit(solution)/shard_map/ppermute | solution.py:318
  70.0 11.8 %all-to-all-start = ((f32[32,8,128]{2,1,0:T(8,128)}), f32[32,8,128]{2,1,0:T(8,128)S(1)}, u32[]{:S(2)}, u32[]{:S(2)}) async-start(f32[32,8,128]{2,1,0:T(8,128)} %bitcast.20), calls=%async_computation | async-start | bytes 262144 | tf_op jit(solution)/shard_map/all_to_all | solution.py:333

commit v5 on v4

--- a/solution.py
+++ b/solution.py
@@ -27,24 +27,25 @@
 
 
 class Table:
-    def __init__(self, ref, run_blocks):
+    def __init__(self, ref, run_blocks, ref_blocks):
         self.ref = ref
         self.run_blocks = run_blocks
+        self.ref_blocks = ref_blocks
 
     def order(self, place):
         return self.ref[place]
 
     def live(self, place):
-        return self.ref[self.run_blocks + place]
+        return self.ref[self.run_blocks + self.order(place)]
 
     def cand(self, place, slot):
-        return self.ref[2 * self.run_blocks + place * TOPC + slot]
+        return self.ref[(2 + slot) * self.run_blocks + self.order(place)]
 
     def eff(self, place, slot):
-        return self.ref[(2 + TOPC) * self.run_blocks + place * TOPC + slot]
+        return jnp.where(slot < self.live(place), self.cand(place, slot), self.ref_blocks)
 
     def offset(self, index):
-        return self.ref[(2 + 2 * TOPC) * self.run_blocks + index]
+        return self.ref[(2 + TOPC) * self.run_blocks + index]
 
     def by_groups(self, body, grain):
         size = group_size(self.run_blocks)
@@ -90,9 +91,10 @@
     return slice(BLK * pair[0], BLK * (pair[-1] + 1))
 
 
-def put_rows(rows, place, pair, row):
+def put_rows(rows, block, pair, row):
     for index, slot in enumerate(pair):
-        rows[pl.ds(place * TOPC + slot, 1), :] = row[:, BLK * index : BLK * (index + 1)]
+        at = block + slot * (rows.shape[0] // TOPC)
+        rows[pl.ds(at, 1), :] = row[:, BLK * index : BLK * (index + 1)]
 
 
 def halves(join, tile):
@@ -102,7 +104,7 @@
 def first_kernel(table, run_hbm, mass_hbm, own_hbm, pot, slot_ref, *rest):
     pieces, (scores, log_mass, lse, rows, ref, run, run_mass, own, arrived) = rest[:-9], rest[-9:]
     run_blocks = scores.shape[0]
-    table = Table(table, run_blocks)
+    table = Table(table, run_blocks, lse.shape[0])
     copies = [
         pltpu.make_async_copy(mass_hbm, run_mass, arrived.at[0]),
         pltpu.make_async_copy(own_hbm, own, arrived.at[1]),
@@ -168,7 +170,7 @@
                 tile = scores[place, :, span(pair)] + wide(potential, pair)
                 top = jnp.max(tile, axis=0, keepdims=True)
                 row = top + jnp.log2(jnp.sum(jnp.exp2(tile - top), axis=0, keepdims=True))
-                put_rows(rows, place, pair, row)
+                put_rows(rows, table.order(place), pair, row)
 
     table.by_groups(body, 1)
 
@@ -186,7 +188,7 @@
 
 def second_kernel(table, scores, pot, log_mass, onehot, weights, peaks, sums, rows):
     run_blocks = weights.shape[0]
-    table = Table(table, run_blocks)
+    table = Table(table, run_blocks, pot.shape[0] - 8)
     rows[...] = jnp.zeros_like(rows)
 
     def body(count, places):
@@ -218,7 +220,7 @@
         for place, factor in zip(places, factors):
             for pair in pairs_of(count):
                 weight = weights[place, :, span(pair)] * wide(factor, pair)
-                put_rows(rows, place, pair, jnp.sum(weight, axis=0, keepdims=True))
+                put_rows(rows, table.order(place), pair, jnp.sum(weight, axis=0, keepdims=True))
 
     table.by_groups(body, 2)
     sums[...] = jnp.dot(
@@ -231,7 +233,7 @@
 
 def third_kernel(table, weights, peaks, gain, log_mass, onehot, out, sums, rows):
     run_blocks = weights.shape[0]
-    table = Table(table, run_blocks)
+    table = Table(table, run_blocks, gain.shape[0] - 8)
     rows[...] = jnp.zeros_like(rows)
     diagonal = lax.broadcasted_iota(jnp.int32, (BLK, BLK), 0) == lax.broadcasted_iota(
         jnp.int32, (BLK, BLK), 1
@@ -259,7 +261,7 @@
         for place, factor in zip(places, factors):
             for pair in pairs_of(count):
                 weight = weights[place, :, span(pair)] * wide(factor, pair)
-                put_rows(rows, place, pair, jnp.sum(weight, axis=0, keepdims=True))
+                put_rows(rows, table.order(place), pair, jnp.sum(weight, axis=0, keepdims=True))
 
     table.by_groups(body, 2)
     total = jnp.dot(
@@ -321,7 +323,8 @@
         masks, bit = [[1]], 2
         while bit < self.devices:
             wide = 4 * bit <= self.devices
-            masks.append([bit, 2 * bit, 3 * bit] if wide else [bit])
+            stage = [bit, 2 * bit, 3 * bit] if wide else [bit]
+            masks.append([mask ^ 1 for mask in stage])
             bit *= 4 if wide else 2
         for stage in masks:
             value = join([value] + [self.swap(value, mask) for mask in stage])
@@ -332,12 +335,17 @@
         sent = copies.reshape(self.devices, own, BLK)
         return join(list(lax.all_to_all(sent, ("grp", "nar"), 0, 0, tiled=True)))
 
+    def masks(self):
+        steps, bit = [], self.width // 2
+        while bit > 1:
+            steps.append(bit ^ 1)
+            bit //= 2
+        return steps + [1] * (self.width > 1)
+
     def gather(self, value):
         held = {0: value}
-        mask = self.width // 2
-        while mask:
+        for mask in self.masks():
             held.update({key ^ mask: self.swap(part, mask) for key, part in list(held.items())})
-            mask //= 2
         return [held[key] for key in range(self.width)]
 
     def gather_pieces(self, value):
@@ -346,11 +354,10 @@
         rows = value.shape[0]
         cut = rows // 4 // BLK * BLK
         parted = self.width > 2 and self.groups % 2 == 0 and cut > 0
-        mask = self.width // 2
         held = {0: [(value, 0)]}
-        while mask:
+        for step, mask in enumerate(self.masks()):
             for key, pieces in list(held.items()):
-                if parted and key == 0 and mask == self.width // 2:
+                if parted and step == 0:
                     start = side * (rows - cut)
                     near = self.swap(lax.dynamic_slice_in_dim(value, start, cut, 0), mask)
                     middle = self.swap(value[cut : rows - cut], mask)
@@ -359,7 +366,6 @@
                 else:
                     got = [(self.swap(part, mask), start) for part, start in pieces]
                 held[key ^ mask] = got
-            mask //= 2
         parts = [part for key in held for part, _ in held[key]]
         starts = [(key ^ me) * rows + start for key in held for _, start in held[key]]
         return parts, jnp.stack([jnp.asarray(start, jnp.int32) for start in starts])
@@ -395,11 +401,10 @@
     place = jnp.sum((rank_key[None, :] > rank_key[:, None]).astype(jnp.int32), axis=1)
     moved = place[None, :] == blocks[:, None]
     order = jnp.sum(jnp.where(moved, blocks[None, :], 0), axis=1)
-    cand = jnp.sum(jnp.where(moved[:, :, None], candidates[None], 0), axis=1)
-    live = jnp.sum(jnp.where(moved, live_slots[None, :], 0), axis=1)
+    cand = candidates.T
+    table = jnp.concatenate([order, live_slots, cand.reshape(-1), offsets])
     slots = jnp.arange(TOPC, dtype=jnp.int32)
-    eff = jnp.where(slots[None, :] < live[:, None], cand, ref_blocks)
-    table = jnp.concatenate([order, live, cand.reshape(-1), eff.reshape(-1), offsets])
+    eff = jnp.where(slots[:, None] < live_slots[None, :], cand, ref_blocks)
     tiles = run_blocks * TOPC
     slot_ref = jnp.broadcast_to(eff.reshape(tiles, 1), (tiles, BLK))
     onehot = (

time: 83.5 us -> 79.9 us (0.957)
  Pallas kernels: 16.9 us -> 22 us
  waiting for transfers between devices: 26.6 us -> 22.4 us
  starting transfers between devices: 30.8 us -> 27 us
  other arithmetic: 5.16 us -> 3.81 us
  local copies, waits for them, and re-layouts: 2.26 us -> 3.56 us
    ppermute x24, waiting for transfers between devices: 18.3 us -> 14.2 us  [swap(): return lax.ppermute(value, ('grp', 'nar'), pairs)]
    ppermute x24, starting transfers between devices: 27.2 us -> 23.4 us  [swap(): return lax.ppermute(value, ('grp', 'nar'), pairs)]
    pallas_call x1, Pallas kernels: 9.22 us -> 11.7 us  [shards(): call(first_kernel, [smem] + [pl.BlockSpec(memory_space=pltpu.HBM)] * 3 +...]
    reduce_sum x2 -> x1, other arithmetic: 2.08 us -> 0.11 us  [shards(): order = jnp.sum(jnp.where(moved, blocks[None, :], 0), axis=1)]
    pallas_call x1, Pallas kernels: 4.03 us -> 5.97 us  [shards(): call(second_kernel, [smem] + [vmem] * 4, [score_shape, rep_shape, table_s...]
where the time goes in v5:
time: 79.9 us; the launch traced here: 79.6 us
  starting transfers between devices  27 us (34%)
  waiting for transfers between devices  22.4 us (28%)
  Pallas kernels  22 us (28%)
  other arithmetic  3.81 us (5%)
  local copies, waits for them, and re-layouts  3.56 us (4%)
    ppermute x24, starting transfers between devices, swap(): return lax.ppermute(value, ('grp', 'nar'), pairs)  23.4 us
    ppermute x24, waiting for transfers between devices, swap(): return lax.ppermute(value, ('grp', 'nar'), pairs)  14.2 us
    pallas_call x1, Pallas kernels, shards(): call(first_kernel, [smem] + [pl.BlockSpec(memory_space=pltpu.HBM)] * 3 +...  11.7 us
    all_to_all x1, waiting for transfers between devices, reduce_own(): return join(list(lax.all_to_all(sent, ('grp', 'nar'), 0, 0, tiled=True)))  8.22 us
    pallas_call x1, Pallas kernels, shards(): call(second_kernel, [smem] + [vmem] * 4, [score_shape, rep_shape, table_s...  5.97 us
    pallas_call x1, Pallas kernels, shards(): call(third_kernel, [smem] + [vmem] * 5, [jax.ShapeDtypeStruct((run_blocks...  4.34 us
    all_to_all x1, starting transfers between devices, reduce_own(): return join(list(lax.all_to_all(sent, ('grp', 'nar'), 0, 0, tiled=True)))  3.62 us
  transfers between devices with their start and end apart: 25, of which 16 were waited for; matrix products, arithmetic and copies ran while one was open for 7% of the time, Pallas kernels for 0%

profile of v5, /device:TPU:0, one launch (start us, length us, event | category | flops | bytes accessed | tf_op | source)
XLA Modules:
  0.0 79.6 jit_solution(5694923059577202854)
XLA Ops:
  1.8 2.6 %collective-permute-start = (f32[2,8,128]{2,1,0:T(8,128)S(1)}, f32[2,8,128]{2,1,0:T(8,128)S(1)}, u32[]{:S(2)}, u32[]{:S(2)}) collective-permute-start(f32[2,8,128]{2,1,0:T(8,128)S(1)} %pad_maximum_fusion), channel_id=1, source_target_pairs={{0,3},{1,2},{2,1},{3,0},{4,7},{5,6},{6,5},{7,4},{8,11},{9,10},{10,... | collective-permute-start | bytes 24584 | tf_op jit(solution)/shard_map/ppermute | solution.py:320
  4.4 0.9 %constant_dynamic-slice_fusion = bf16[256,256]{1,0:T(8,128)(2,1)S(1)} fusion(bf16[1024,256]{1,0:T(8,128)(2,1)} %own_hbm.1, s32[]{:T(128)S(6)} %select_n.123), kind=kLoop, calls=%fused_computation.92 | loop fusion | bytes 262148 | tf_op jit(solution)/shard_map/dynamic_slice | solution.py:362
  5.5 1.0 %slice.24 = bf16[512,256]{1,0:T(8,128)(2,1)S(1)} slice(bf16[1024,256]{1,0:T(8,128)(2,1)} %own_hbm.1), slice={[256:768], [0:256]} | slice | bytes 524288 | tf_op jit(solution)/shard_map/slice | solution.py:363
  6.4 1.8 %collective-permute-start.5 = (bf16[512,256]{1,0:T(8,128)(2,1)S(1)}, bf16[512,256]{1,0:T(8,128)(2,1)S(1)}, u32[]{:S(2)}, u32[]{:S(2)}) collective-permute-start(bf16[512,256]{1,0:T(8,128)(2,1)S(1)} %slice.24), channel_id=1, source_target_pairs={{0,3},{1,2},{2,1},{3,0},{4,7},{5,6},{6,5},{7,4},{8,11},{9,10},{10,... | collective-permute-start | bytes 786440 | tf_op jit(solution)/shard_map/ppermute | solution.py:320
  9.6 1.0 %collective-permute-done.3.rest_0_ = bf16[256,256]{1,0:T(8,128)(2,1)S(1)} collective-permute-done((bf16[256,256]{1,0:T(8,128)(2,1)S(1)}, bf16[256,256]{1,0:T(8,128)(2,1)S(1)}, u32[]{:S(2)}, u32[]{:S(2)}) %collective-permute-start.3) | collective-permute-done | bytes 131104 | tf_op jit(solution)/shard_map/ppermute | solution.py:320
  10.6 1.5 %collective-permute-start.4 = (bf16[256,256]{1,0:T(8,128)(2,1)S(1)}, bf16[256,256]{1,0:T(8,128)(2,1)S(1)}, u32[]{:S(2)}, u32[]{:S(2)}) collective-permute-start(bf16[256,256]{1,0:T(8,128)(2,1)S(1)} %collective-permute-done.3.rest_0_), channel_id=1, source_target_pairs={{0,4},{1,5},{2,6},{3,7},{4,0},{5,1},{6,2},{7,3},{8,12},{9,13},{10,... | collective-permute-start | bytes 393224 | tf_op jit(solution)/shard_map/ppermute | solution.py:320
  12.2 1.2 %collective-permute-start.1 = (f32[2,8,128]{2,1,0:T(8,128)S(1)}, f32[2,8,128]{2,1,0:T(8,128)S(1)}, u32[]{:S(2)}, u32[]{:S(2)}) collective-permute-start(f32[2,8,128]{2,1,0:T(8,128)S(1)} %collective-permute-done), channel_id=1, source_target_pairs={{0,1},{1,0},{2,3},{3,2},{4,5},{5,4},{6,7},{7,6},{8,9},{9,8},{10,11... | collective-permute-start | bytes 24584 | tf_op jit(solution)/shard_map/ppermute | solution.py:320
  13.5 0.8 reshape.65
  14.4 0.7 concatenate.18.table
  15.2 1.4 %collective-permute-done.4.rest_1_ = bf16[256,256]{1,0:T(8,128)(2,1)S(1)} collective-permute-done((bf16[256,256]{1,0:T(8,128)(2,1)S(1)}, bf16[256,256]{1,0:T(8,128)(2,1)S(1)}, u32[]{:S(2)}, u32[]{:S(2)}) %collective-permute-start.4) | collective-permute-done | bytes 131104 | tf_op jit(solution)/shard_map/ppermute | solution.py:320
  18.4 11.7 %shard_map.86 = (f32[32,128,1024]{2,1,0:T(8,128)S(1)}, f32[4096,128]{1,0:T(8,128)S(1)}, f32[32,128]{1,0:T(8,128)S(1)}) custom-call(s32[328]{0:T(512)S(1)} %concatenate.18.table, bf16[4096,256]{1,0:T(8,128)(2,1)} %run_hbm.1, f32[32,128]{1,0:T(8,128)} %bitcast.87, bf16[1024,256]{1,0:T(8,128)(2,1)} %own_hbm.1, f32[40,128]{1,0:T(8,128)S(1)} %concatenate.20.pot, ...), custom_call_target="tpu_custom_call" | custom-call | tf_op jit(solution)/shard_map/pallas_call | solution.py:421
  30.5 0.9 %collective-permute-done.10 = f32[32,128]{1,0:T(8,128)S(1)} collective-permute-done((f32[32,128]{1,0:T(8,128)S(1)}, f32[32,128]{1,0:T(8,128)S(1)}, u32[]{:S(2)}, u32[]{:S(2)}) %collective-permute-start.10) | collective-permute-done | bytes 16416 | tf_op jit(solution)/shard_map/ppermute | solution.py:320
  31.4 1.2 %collective-permute-start.13 = (f32[32,128]{1,0:T(8,128)S(1)}, f32[32,128]{1,0:T(8,128)S(1)}, u32[]{:S(2)}, u32[]{:S(2)}) collective-permute-start(f32[32,128]{1,0:T(8,128)S(1)} %multiply_add_fusion.1), channel_id=1, source_target_pairs={{0,7},{1,6},{2,5},{3,4},{4,3},{5,2},{6,1},{7,0},{8,15},{9,14},{10,... | collective-permute-start | bytes 49160 | tf_op jit(solution)/shard_map/ppermute | solution.py:320
  33.1 1.5 %collective-permute-start.11 = (f32[32,128]{1,0:T(8,128)S(1)}, f32[32,128]{1,0:T(8,128)S(1)}, u32[]{:S(2)}, u32[]{:S(2)}) collective-permute-start(f32[32,128]{1,0:T(8,128)S(1)} %multiply_add_fusion.1), channel_id=1, source_target_pairs={{0,3},{1,2},{2,1},{3,0},{4,7},{5,6},{6,5},{7,4},{8,11},{9,10},{10,... | collective-permute-start | bytes 49160 | tf_op jit(solution)/shard_map/ppermute | solution.py:320
  34.6 1.0 %collective-permute-done.13 = f32[32,128]{1,0:T(8,128)S(1)} collective-permute-done((f32[32,128]{1,0:T(8,128)S(1)}, f32[32,128]{1,0:T(8,128)S(1)}, u32[]{:S(2)}, u32[]{:S(2)}) %collective-permute-start.13) | collective-permute-done | bytes 16416 | tf_op jit(solution)/shard_map/ppermute | solution.py:320
  36.3 4.1 %collective-permute-start.16 = (f32[32,128]{1,0:T(8,128)S(1)}, f32[32,128]{1,0:T(8,128)S(1)}, u32[]{:S(2)}, u32[]{:S(2)}) collective-permute-start(f32[32,128]{1,0:T(8,128)S(1)} %multiply_add_fusion), channel_id=1, source_target_pairs={{0,25},{1,24},{2,27},{3,26},{4,29},{5,28},{6,31},{7,30},{8,17},{9,... | collective-permute-start | bytes 49160 | tf_op jit(solution)/shard_map/ppermute | solution.py:320
  40.8 1.0 %collective-permute-done.16 = f32[32,128]{1,0:T(8,128)S(1)} collective-permute-done((f32[32,128]{1,0:T(8,128)S(1)}, f32[32,128]{1,0:T(8,128)S(1)}, u32[]{:S(2)}, u32[]{:S(2)}) %collective-permute-start.16) | collective-permute-done | bytes 16416 | tf_op jit(solution)/shard_map/ppermute | solution.py:320
  41.8 2.6 %collective-permute-done.15 = f32[32,128]{1,0:T(8,128)S(1)} collective-permute-done((f32[32,128]{1,0:T(8,128)S(1)}, f32[32,128]{1,0:T(8,128)S(1)}, u32[]{:S(2)}, u32[]{:S(2)}) %collective-permute-start.15) | collective-permute-done | bytes 16416 | tf_op jit(solution)/shard_map/ppermute | solution.py:320
  44.5 6.0 %shard_map.87 = (f32[32,128,1024]{2,1,0:T(8,128)S(1)}, f32[4096,128]{1,0:T(8,128)S(1)}, f32[32,128]{1,0:T(8,128)S(1)}) custom-call(s32[328]{0:T(512)S(1)} %concatenate.18.table, f32[32,128,1024]{2,1,0:T(8,128)S(1)} %get-tuple-element.10.scores, f32[40,128]{1,0:T(8,128)S(1)} %concatenate.22.pot, ...), custom_call_target="tpu_custom_call", output_to_operand_aliasing={{0}: (1, {})} | custom-call | tf_op jit(solution)/shard_map/pallas_call | solution.py:445
  50.7 1.0 %collective-permute-done.17 = f32[32,128]{1,0:T(8,128)S(1)} collective-permute-done((f32[32,128]{1,0:T(8,128)S(1)}, f32[32,128]{1,0:T(8,128)S(1)}, u32[]{:S(2)}, u32[]{:S(2)}) %collective-permute-start.17) | collective-permute-done | bytes 16416 | tf_op jit(solution)/shard_map/ppermute | solution.py:320
  51.7 1.9 %collective-permute-start.20 = (f32[32,128]{1,0:T(8,128)S(1)}, f32[32,128]{1,0:T(8,128)S(1)}, u32[]{:S(2)}, u32[]{:S(2)}) collective-permute-start(f32[32,128]{1,0:T(8,128)S(1)} %add.238), channel_id=1, source_target_pairs={{0,7},{1,6},{2,5},{3,4},{4,3},{5,2},{6,1},{7,0},{8,15},{9,14},{10,... | collective-permute-start | bytes 49160 | tf_op jit(solution)/shard_map/ppermute | solution.py:320
  53.6 1.1 %collective-permute-start.18 = (f32[32,128]{1,0:T(8,128)S(1)}, f32[32,128]{1,0:T(8,128)S(1)}, u32[]{:S(2)}, u32[]{:S(2)}) collective-permute-start(f32[32,128]{1,0:T(8,128)S(1)} %add.238), channel_id=1, source_target_pairs={{0,3},{1,2},{2,1},{3,0},{4,7},{5,6},{6,5},{7,4},{8,11},{9,10},{10,... | collective-permute-start | bytes 49160 | tf_op jit(solution)/shard_map/ppermute | solution.py:320
  54.7 1.1 %collective-permute-done.20 = f32[32,128]{1,0:T(8,128)S(1)} collective-permute-done((f32[32,128]{1,0:T(8,128)S(1)}, f32[32,128]{1,0:T(8,128)S(1)}, u32[]{:S(2)}, u32[]{:S(2)}) %collective-permute-start.20) | collective-permute-done | bytes 16416 | tf_op jit(solution)/shard_map/ppermute | solution.py:320
  55.8 1.0 %collective-permute-done.19 = f32[32,128]{1,0:T(8,128)S(1)} collective-permute-done((f32[32,128]{1,0:T(8,128)S(1)}, f32[32,128]{1,0:T(8,128)S(1)}, u32[]{:S(2)}, u32[]{:S(2)}) %collective-permute-start.19) | collective-permute-done | bytes 16416 | tf_op jit(solution)/shard_map/ppermute | solution.py:320
  56.8 1.9 %collective-permute-start.23 = (f32[32,128]{1,0:T(8,128)S(1)}, f32[32,128]{1,0:T(8,128)S(1)}, u32[]{:S(2)}, u32[]{:S(2)}) collective-permute-start(f32[32,128]{1,0:T(8,128)S(1)} %add_add_fusion), channel_id=1, source_target_pairs={{0,25},{1,24},{2,27},{3,26},{4,29},{5,28},{6,31},{7,30},{8,17},{9,... | collective-permute-start | bytes 49160 | tf_op jit(solution)/shard_map/ppermute | solution.py:320
  58.7 0.8 collective-permute-start.22
  59.4 1.3 %collective-permute-start.21 = (f32[32,128]{1,0:T(8,128)S(1)}, f32[32,128]{1,0:T(8,128)S(1)}, u32[]{:S(2)}, u32[]{:S(2)}) collective-permute-start(f32[32,128]{1,0:T(8,128)S(1)} %add_add_fusion), channel_id=1, source_target_pairs={{0,9},{1,8},{2,11},{3,10},{4,13},{5,12},{6,15},{7,14},{8,1},{9,0},... | collective-permute-start | bytes 49160 | tf_op jit(solution)/shard_map/ppermute | solution.py:320
  60.7 1.1 %collective-permute-done.23 = f32[32,128]{1,0:T(8,128)S(1)} collective-permute-done((f32[32,128]{1,0:T(8,128)S(1)}, f32[32,128]{1,0:T(8,128)S(1)}, u32[]{:S(2)}, u32[]{:S(2)}) %collective-permute-start.23) | collective-permute-done | bytes 16416 | tf_op jit(solution)/shard_map/ppermute | solution.py:320
  61.8 1.0 %collective-permute-done.22 = f32[32,128]{1,0:T(8,128)S(1)} collective-permute-done((f32[32,128]{1,0:T(8,128)S(1)}, f32[32,128]{1,0:T(8,128)S(1)}, u32[]{:S(2)}, u32[]{:S(2)}) %collective-permute-start.22) | collective-permute-done | bytes 16416 | tf_op jit(solution)/shard_map/ppermute | solution.py:320
  62.8 4.3 %shard_map.88 = (f32[32,128]{1,0:T(8,128)}, f32[8,32,128]{2,1,0:T(8,128)}) custom-call(s32[328]{0:T(512)S(1)} %concatenate.18.table, f32[32,128,1024]{2,1,0:T(8,128)S(1)} %get-tuple-element.13.weights, f32[4096,128]{1,0:T(8,128)S(1)} %get-tuple-element.14.peaks, f32[40,128]{1,0:T(8,128)S(1)} %concatenate.23.gain, ...), custom_call_target="tpu_custom_call" | custom-call | tf_op jit(solution)/shard_map/pallas_call | solution.py:452
  67.2 3.6 %all-to-all-start = ((f32[32,8,128]{2,1,0:T(8,128)}), f32[32,8,128]{2,1,0:T(8,128)S(1)}, u32[]{:S(2)}, u32[]{:S(2)}) async-start(f32[32,8,128]{2,1,0:T(8,128)} %bitcast.21), calls=%async_computation | async-start | bytes 262144 | tf_op jit(solution)/shard_map/all_to_all | solution.py:336
  70.8 8.2 %all-to-all-done = f32[32,8,128]{2,1,0:T(8,128)S(1)} async-done(((f32[32,8,128]{2,1,0:T(8,128)}), f32[32,8,128]{2,1,0:T(8,128)S(1)}, u32[]{:S(2)}, u32[]{:S(2)}) %all-to-all-start) | async-done | bytes 131104 | tf_op jit(solution)/shard_map/all_to_all | solution.py:336
  (48 shorter events, 7.8 us)
Async XLA Ops:
  1.3 13.8 %collective-permute-start.2 = (f32[2,8,128]{2,1,0:T(8,128)S(1)}, f32[2,8,128]{2,1,0:T(8,128)S(1)}, u32[]{:S(2)}, u32[]{:S(2)}) collective-permute-start(f32[2,8,128]{2,1,0:T(8,128)S(1)} %pad_maximum_fusion), channel_id=1, source_target_pairs={{0,1},{1,0},{2,3},{3,2},{4,5},{5,4},{6,7},{7,6},{8,9},{9,8},{10,11... | collective-permute-start | bytes 24584 | tf_op jit(solution)/shard_map/ppermute | solution.py:320
  1.8 10.4 %collective-permute-start = (f32[2,8,128]{2,1,0:T(8,128)S(1)}, f32[2,8,128]{2,1,0:T(8,128)S(1)}, u32[]{:S(2)}, u32[]{:S(2)}) collective-permute-start(f32[2,8,128]{2,1,0:T(8,128)S(1)} %pad_maximum_fusion), channel_id=1, source_target_pairs={{0,3},{1,2},{2,1},{3,0},{4,7},{5,6},{6,5},{7,4},{8,11},{9,10},{10,... | collective-permute-start | bytes 24584 | tf_op jit(solution)/shard_map/ppermute | solution.py:320
  4.4 13.9 %collective-permute-start.6 = (bf16[1024,256]{1,0:T(8,128)(2,1)}, bf16[1024,256]{1,0:T(8,128)(2,1)S(1)}, u32[]{:S(2)}, u32[]{:S(2)}) collective-permute-start(bf16[1024,256]{1,0:T(8,128)(2,1)} %own_hbm.1), channel_id=1, source_target_pairs={{0,1},{1,0},{2,3},{3,2},{4,5},{5,4},{6,7},{7,6},{8,9},{9,8},{10,11... | collective-permute-start | bytes 1572872 | tf_op jit(solution)/shard_map/ppermute | solution.py:320
  5.3 5.2 %collective-permute-start.3 = (bf16[256,256]{1,0:T(8,128)(2,1)S(1)}, bf16[256,256]{1,0:T(8,128)(2,1)S(1)}, u32[]{:S(2)}, u32[]{:S(2)}) collective-permute-start(bf16[256,256]{1,0:T(8,128)(2,1)S(1)} %constant_dynamic-slice_fusion), channel_id=1, source_target_pairs={{0,3},{1,2},{2,1},{3,0},{4,7},{5,6},{6,5},{7,4},{8,11},{9,10},{10,... | collective-permute-start | bytes 393224 | tf_op jit(solution)/shard_map/ppermute | solution.py:320
  6.4 10.3 %collective-permute-start.5 = (bf16[512,256]{1,0:T(8,128)(2,1)S(1)}, bf16[512,256]{1,0:T(8,128)(2,1)S(1)}, u32[]{:S(2)}, u32[]{:S(2)}) collective-permute-start(bf16[512,256]{1,0:T(8,128)(2,1)S(1)} %slice.24), channel_id=1, source_target_pairs={{0,3},{1,2},{2,1},{3,0},{4,7},{5,6},{6,5},{7,4},{8,11},{9,10},{10,... | collective-permute-start | bytes 786440 | tf_op jit(solution)/shard_map/ppermute | solution.py:320
  10.6 6.0 %collective-permute-start.4 = (bf16[256,256]{1,0:T(8,128)(2,1)S(1)}, bf16[256,256]{1,0:T(8,128)(2,1)S(1)}, u32[]{:S(2)}, u32[]{:S(2)}) collective-permute-start(bf16[256,256]{1,0:T(8,128)(2,1)S(1)} %collective-permute-done.3.rest_0_), channel_id=1, source_target_pairs={{0,4},{1,5},{2,6},{3,7},{4,0},{5,1},{6,2},{7,3},{8,12},{9,13},{10,... | collective-permute-start | bytes 393224 | tf_op jit(solution)/shard_map/ppermute | solution.py:320
  12.2 4.9 %collective-permute-start.1 = (f32[2,8,128]{2,1,0:T(8,128)S(1)}, f32[2,8,128]{2,1,0:T(8,128)S(1)}, u32[]{:S(2)}, u32[]{:S(2)}) collective-permute-start(f32[2,8,128]{2,1,0:T(8,128)S(1)} %collective-permute-done), channel_id=1, source_target_pairs={{0,1},{1,0},{2,3},{3,2},{4,5},{5,4},{6,7},{7,6},{8,9},{9,8},{10,11... | collective-permute-start | bytes 24584 | tf_op jit(solution)/shard_map/ppermute | solution.py:320
  15.1 2.7 %collective-permute-start.7 = (bf16[256,256]{1,0:T(8,128)(2,1)S(1)}, bf16[256,256]{1,0:T(8,128)(2,1)S(1)}, u32[]{:S(2)}, u32[]{:S(2)}) collective-permute-start(bf16[256,256]{1,0:T(8,128)(2,1)S(1)} %collective-permute-done.3.rest_0_), channel_id=1, source_target_pairs={{0,1},{1,0},{2,3},{3,2},{4,5},{5,4},{6,7},{7,6},{8,9},{9,8},{10,11... | collective-permute-start | bytes 393224 | tf_op jit(solution)/shard_map/ppermute | solution.py:320
  16.6 1.3 %collective-permute-start.8 = (bf16[256,256]{1,0:T(8,128)(2,1)S(1)}, bf16[256,256]{1,0:T(8,128)(2,1)S(1)}, u32[]{:S(2)}, u32[]{:S(2)}) collective-permute-start(bf16[256,256]{1,0:T(8,128)(2,1)S(1)} %collective-permute-done.4.rest_1_), channel_id=1, source_target_pairs={{0,1},{1,0},{2,3},{3,2},{4,5},{5,4},{6,7},{7,6},{8,9},{9,8},{10,11... | collective-permute-start | bytes 393224 | tf_op jit(solution)/shard_map/ppermute | solution.py:320
  16.8 1.5 %collective-permute-start.9 = (bf16[512,256]{1,0:T(8,128)(2,1)S(1)}, bf16[512,256]{1,0:T(8,128)(2,1)S(1)}, u32[]{:S(2)}, u32[]{:S(2)}) collective-permute-start(bf16[512,256]{1,0:T(8,128)(2,1)S(1)} %collective-permute-done.5.rest_2_), channel_id=1, source_target_pairs={{0,1},{1,0},{2,3},{3,2},{4,5},{5,4},{6,7},{7,6},{8,9},{9,8},{10,11... | collective-permute-start | bytes 786440 | tf_op jit(solution)/shard_map/ppermute | solution.py:320
  18.4 22.4 %copy-start = (f32[1024]{0:T(1024)S(1)}, f32[1024]{0:T(1024)}, u32[]{:S(2)}) copy-start(f32[1024]{0:T(1024)} %param.12) | copy-start | bytes 12292
  30.1 1.2 %collective-permute-start.10 = (f32[32,128]{1,0:T(8,128)S(1)}, f32[32,128]{1,0:T(8,128)S(1)}, u32[]{:S(2)}, u32[]{:S(2)}) collective-permute-start(f32[32,128]{1,0:T(8,128)S(1)} %get-tuple-element.11), channel_id=1, source_target_pairs={{0,1},{1,0},{2,3},{3,2},{4,5},{5,4},{6,7},{7,6},{8,9},{9,8},{10,11... | collective-permute-start | bytes 49160 | tf_op jit(solution)/shard_map/ppermute | solution.py:320
  31.4 4.1 %collective-permute-start.13 = (f32[32,128]{1,0:T(8,128)S(1)}, f32[32,128]{1,0:T(8,128)S(1)}, u32[]{:S(2)}, u32[]{:S(2)}) collective-permute-start(f32[32,128]{1,0:T(8,128)S(1)} %multiply_add_fusion.1), channel_id=1, source_target_pairs={{0,7},{1,6},{2,5},{3,4},{4,3},{5,2},{6,1},{7,0},{8,15},{9,14},{10,... | collective-permute-start | bytes 49160 | tf_op jit(solution)/shard_map/ppermute | solution.py:320
  32.6 3.2 %collective-permute-start.12 = (f32[32,128]{1,0:T(8,128)S(1)}, f32[32,128]{1,0:T(8,128)S(1)}, u32[]{:S(2)}, u32[]{:S(2)}) collective-permute-start(f32[32,128]{1,0:T(8,128)S(1)} %multiply_add_fusion.1), channel_id=1, source_target_pairs={{0,5},{1,4},{2,7},{3,6},{4,1},{5,0},{6,3},{7,2},{8,13},{9,12},{10,... | collective-permute-start | bytes 49160 | tf_op jit(solution)/shard_map/ppermute | solution.py:320
  33.1 3.2 %collective-permute-start.11 = (f32[32,128]{1,0:T(8,128)S(1)}, f32[32,128]{1,0:T(8,128)S(1)}, u32[]{:S(2)}, u32[]{:S(2)}) collective-permute-start(f32[32,128]{1,0:T(8,128)S(1)} %multiply_add_fusion.1), channel_id=1, source_target_pairs={{0,3},{1,2},{2,1},{3,0},{4,7},{5,6},{6,5},{7,4},{8,11},{9,10},{10,... | collective-permute-start | bytes 49160 | tf_op jit(solution)/shard_map/ppermute | solution.py:320
  36.3 5.6 %collective-permute-start.16 = (f32[32,128]{1,0:T(8,128)S(1)}, f32[32,128]{1,0:T(8,128)S(1)}, u32[]{:S(2)}, u32[]{:S(2)}) collective-permute-start(f32[32,128]{1,0:T(8,128)S(1)} %multiply_add_fusion), channel_id=1, source_target_pairs={{0,25},{1,24},{2,27},{3,26},{4,29},{5,28},{6,31},{7,30},{8,17},{9,... | collective-permute-start | bytes 49160 | tf_op jit(solution)/shard_map/ppermute | solution.py:320
  40.4 4.1 %collective-permute-start.15 = (f32[32,128]{1,0:T(8,128)S(1)}, f32[32,128]{1,0:T(8,128)S(1)}, u32[]{:S(2)}, u32[]{:S(2)}) collective-permute-start(f32[32,128]{1,0:T(8,128)S(1)} %multiply_add_fusion), channel_id=1, source_target_pairs={{0,17},{1,16},{2,19},{3,18},{4,21},{5,20},{6,23},{7,22},{8,25},{9,... | collective-permute-start | bytes 49160 | tf_op jit(solution)/shard_map/ppermute | solution.py:320
  40.4 4.1 %collective-permute-start.14 = (f32[32,128]{1,0:T(8,128)S(1)}, f32[32,128]{1,0:T(8,128)S(1)}, u32[]{:S(2)}, u32[]{:S(2)}) collective-permute-start(f32[32,128]{1,0:T(8,128)S(1)} %multiply_add_fusion), channel_id=1, source_target_pairs={{0,9},{1,8},{2,11},{3,10},{4,13},{5,12},{6,15},{7,14},{8,1},{9,0},... | collective-permute-start | bytes 49160 | tf_op jit(solution)/shard_map/ppermute | solution.py:320
  50.5 1.2 %collective-permute-start.17 = (f32[32,128]{1,0:T(8,128)S(1)}, f32[32,128]{1,0:T(8,128)S(1)}, u32[]{:S(2)}, u32[]{:S(2)}) collective-permute-start(f32[32,128]{1,0:T(8,128)S(1)} %get-tuple-element.15), channel_id=1, source_target_pairs={{0,1},{1,0},{2,3},{3,2},{4,5},{5,4},{6,7},{7,6},{8,9},{9,8},{10,11... | collective-permute-start | bytes 49160 | tf_op jit(solution)/shard_map/ppermute | solution.py:320
  51.7 4.1 %collective-permute-start.20 = (f32[32,128]{1,0:T(8,128)S(1)}, f32[32,128]{1,0:T(8,128)S(1)}, u32[]{:S(2)}, u32[]{:S(2)}) collective-permute-start(f32[32,128]{1,0:T(8,128)S(1)} %add.238), channel_id=1, source_target_pairs={{0,7},{1,6},{2,5},{3,4},{4,3},{5,2},{6,1},{7,0},{8,15},{9,14},{10,... | collective-permute-start | bytes 49160 | tf_op jit(solution)/shard_map/ppermute | solution.py:320
  53.6 3.2 %collective-permute-start.19 = (f32[32,128]{1,0:T(8,128)S(1)}, f32[32,128]{1,0:T(8,128)S(1)}, u32[]{:S(2)}, u32[]{:S(2)}) collective-permute-start(f32[32,128]{1,0:T(8,128)S(1)} %add.238), channel_id=1, source_target_pairs={{0,5},{1,4},{2,7},{3,6},{4,1},{5,0},{6,3},{7,2},{8,13},{9,12},{10,... | collective-permute-start | bytes 49160 | tf_op jit(solution)/shard_map/ppermute | solution.py:320
  53.6 3.2 %collective-permute-start.18 = (f32[32,128]{1,0:T(8,128)S(1)}, f32[32,128]{1,0:T(8,128)S(1)}, u32[]{:S(2)}, u32[]{:S(2)}) collective-permute-start(f32[32,128]{1,0:T(8,128)S(1)} %add.238), channel_id=1, source_target_pairs={{0,3},{1,2},{2,1},{3,0},{4,7},{5,6},{6,5},{7,4},{8,11},{9,10},{10,... | collective-permute-start | bytes 49160 | tf_op jit(solution)/shard_map/ppermute | solution.py:320
  56.8 5.0 %collective-permute-start.23 = (f32[32,128]{1,0:T(8,128)S(1)}, f32[32,128]{1,0:T(8,128)S(1)}, u32[]{:S(2)}, u32[]{:S(2)}) collective-permute-start(f32[32,128]{1,0:T(8,128)S(1)} %add_add_fusion), channel_id=1, source_target_pairs={{0,25},{1,24},{2,27},{3,26},{4,29},{5,28},{6,31},{7,30},{8,17},{9,... | collective-permute-start | bytes 49160 | tf_op jit(solution)/shard_map/ppermute | solution.py:320
  58.7 4.1 %collective-permute-start.22 = (f32[32,128]{1,0:T(8,128)S(1)}, f32[32,128]{1,0:T(8,128)S(1)}, u32[]{:S(2)}, u32[]{:S(2)}) collective-permute-start(f32[32,128]{1,0:T(8,128)S(1)} %add_add_fusion), channel_id=1, source_target_pairs={{0,17},{1,16},{2,19},{3,18},{4,21},{5,20},{6,23},{7,22},{8,25},{9,... | collective-permute-start | bytes 49160 | tf_op jit(solution)/shard_map/ppermute | solution.py:320
  59.4 3.3 %collective-permute-start.21 = (f32[32,128]{1,0:T(8,128)S(1)}, f32[32,128]{1,0:T(8,128)S(1)}, u32[]{:S(2)}, u32[]{:S(2)}) collective-permute-start(f32[32,128]{1,0:T(8,128)S(1)} %add_add_fusion), channel_id=1, source_target_pairs={{0,9},{1,8},{2,11},{3,10},{4,13},{5,12},{6,15},{7,14},{8,1},{9,0},... | collective-permute-start | bytes 49160 | tf_op jit(solution)/shard_map/ppermute | solution.py:320
  67.2 11.9 %all-to-all-start = ((f32[32,8,128]{2,1,0:T(8,128)}), f32[32,8,128]{2,1,0:T(8,128)S(1)}, u32[]{:S(2)}, u32[]{:S(2)}) async-start(f32[32,8,128]{2,1,0:T(8,128)} %bitcast.21), calls=%async_computation | async-start | bytes 262144 | tf_op jit(solution)/shard_map/all_to_all | solution.py:336

commit v6 on v5

--- a/solution.py
+++ b/solution.py
@@ -144,11 +144,11 @@
                 tile = lax.dot_general(
                     mine, both, (((1,), (0,)), ((), ())), preferred_element_type=jnp.float32
                 )
-                tile = tile * scale
+                tile = tile * scale + pair_row(pot, table, place, pair)
                 scores[place, :, span(pair)] = tile
                 if len(pair) == 1:
                     scores[place, :, span([count])] = jnp.zeros_like(tile)
-                top = halves(jnp.maximum, tile + pair_row(pot, table, place, pair))
+                top = halves(jnp.maximum, tile)
                 peak = top if peak is None else jnp.maximum(peak, top)
             peaks.append(peak)
         peaks = [spread(jnp.max(peak, axis=1, keepdims=True)) for peak in peaks]
@@ -156,7 +156,7 @@
         for place, peak in zip(places, peaks):
             total = None
             for pair in pairs_of(count):
-                tile = scores[place, :, span(pair)] + pair_row(pot, table, place, pair)
+                tile = scores[place, :, span(pair)]
                 part = halves(jnp.add, jnp.exp2(tile - wide(peak, pair)))
                 total = part if total is None else total + part
             totals.append(total)
@@ -180,7 +180,7 @@
             picked = jnp.where(slot_ref[...] == block, rows[...], FLOOR)
             top = jnp.max(picked, axis=0, keepdims=True)
             total = jnp.sum(jnp.exp2(picked - top), axis=0, keepdims=True)
-            lse[pl.ds(block, 1), :] = top + jnp.log2(total)
+            lse[pl.ds(block, 1), :] = top + jnp.log2(total) - pot[pl.ds(block, 1), :]
         return carry
 
     lax.fori_loop(0, ref_blocks // JOINED, join, 0)
@@ -197,6 +197,7 @@
             peak = None
             for pair in pairs_of(count):
                 tile = scores[place, :, span(pair)] + pair_row(pot, table, place, pair)
+                weights[place, :, span(pair)] = tile
                 top = halves(jnp.maximum, tile)
                 peak = top if peak is None else jnp.maximum(peak, top)
             tops.append(peak)
@@ -206,8 +207,7 @@
             peaks[rows_of(place), :] = peak
             total = None
             for pair in pairs_of(count):
-                tile = scores[place, :, span(pair)] + pair_row(pot, table, place, pair)
-                weight = jnp.exp2(tile - wide(peak, pair))
+                weight = jnp.exp2(weights[place, :, span(pair)] - wide(peak, pair))
                 weights[place, :, span(pair)] = weight
                 part = halves(jnp.add, weight)
                 total = part if total is None else total + part
@@ -440,13 +440,13 @@
         *pieces[1:],
     )
 
-    pot = log_ref - links.reduce_all(lse, log_sum)
+    change = log_ref - links.reduce_all(lse, log_sum) - pot
 
     weights, peaks, sums = call(
         second_kernel, [smem] + [vmem] * 4, [score_shape, rep_shape, table_shape], [rows], {1: 0}
-    )(table, in_vmem(scores), padded(pot), log_mass, onehot)
+    )(table, in_vmem(scores), padded(change), log_mass, onehot)
     log_gain = log_ref - jnp.log2(links.reduce_all(sums, plain_sum))
-    pot = pot + log_gain
+    pot = pot + change + log_gain
     gain = jnp.concatenate([jnp.exp2(log_gain), jnp.zeros((8, BLK), f32)], axis=0)
 
     run_pot, sums = call(

time: 79.9 us -> 79.3 us (level)
  Pallas kernels: 22 us -> 20.1 us
  waiting for transfers between devices: 22.4 us -> 23.9 us
    ppermute x24, waiting for transfers between devices: 14.2 us -> 15.7 us  [swap(): return lax.ppermute(value, ('grp', 'nar'), pairs)]
    pallas_call x1, Pallas kernels: 11.7 us -> 10.7 us  [shards(): call(first_kernel, [smem] + [pl.BlockSpec(memory_space=pltpu.HBM)] * 3 +...]
where the time goes in v6:
time: 79.3 us; the launch traced here: 78.9 us
  starting transfers between devices  26.8 us (34%)
  waiting for transfers between devices  23.9 us (30%)
  Pallas kernels  20.1 us (25%)
  other arithmetic  3.81 us (5%)
  local copies, waits for them, and re-layouts  3.56 us (4%)
    ppermute x24, starting transfers between devices, swap(): return lax.ppermute(value, ('grp', 'nar'), pairs)  23.2 us
    ppermute x24, waiting for transfers between devices, swap(): return lax.ppermute(value, ('grp', 'nar'), pairs)  15.7 us
    pallas_call x1, Pallas kernels, shards(): call(first_kernel, [smem] + [pl.BlockSpec(memory_space=pltpu.HBM)] * 3 +...  10.7 us
    all_to_all x1, waiting for transfers between devices, reduce_own(): return join(list(lax.all_to_all(sent, ('grp', 'nar'), 0, 0, tiled=True)))  8.22 us
    pallas_call x1, Pallas kernels, shards(): call(second_kernel, [smem] + [vmem] * 4, [score_shape, rep_shape, table_s...  5.24 us
    pallas_call x1, Pallas kernels, shards(): call(third_kernel, [smem] + [vmem] * 5, [jax.ShapeDtypeStruct((run_blocks...  4.11 us
    all_to_all x1, starting transfers between devices, reduce_own(): return join(list(lax.all_to_all(sent, ('grp', 'nar'), 0, 0, tiled=True)))  3.63 us
  transfers between devices with their start and end apart: 25, of which 16 were waited for; matrix products, arithmetic and copies ran while one was open for 7% of the time, Pallas kernels for 0%

profile of v6, /device:TPU:0, one launch (start us, length us, event | category | flops | bytes accessed | tf_op | source)
XLA Modules:
  0.0 78.9 jit_solution(17674852388499446820)
XLA Ops:
  1.8 2.6 %collective-permute-start = (f32[2,8,128]{2,1,0:T(8,128)S(1)}, f32[2,8,128]{2,1,0:T(8,128)S(1)}, u32[]{:S(2)}, u32[]{:S(2)}) collective-permute-start(f32[2,8,128]{2,1,0:T(8,128)S(1)} %pad_maximum_fusion), channel_id=1, source_target_pairs={{0,3},{1,2},{2,1},{3,0},{4,7},{5,6},{6,5},{7,4},{8,11},{9,10},{10,... | collective-permute-start | bytes 24584 | tf_op jit(solution)/shard_map/ppermute | solution.py:320
  4.4 0.9 %constant_dynamic-slice_fusion = bf16[256,256]{1,0:T(8,128)(2,1)S(1)} fusion(bf16[1024,256]{1,0:T(8,128)(2,1)} %own_hbm.1, s32[]{:T(128)S(6)} %select_n.123), kind=kLoop, calls=%fused_computation.93 | loop fusion | bytes 262148 | tf_op jit(solution)/shard_map/dynamic_slice | solution.py:362
  5.5 1.0 %slice.24 = bf16[512,256]{1,0:T(8,128)(2,1)S(1)} slice(bf16[1024,256]{1,0:T(8,128)(2,1)} %own_hbm.1), slice={[256:768], [0:256]} | slice | bytes 524288 | tf_op jit(solution)/shard_map/slice | solution.py:363
  6.4 1.8 %collective-permute-start.5 = (bf16[512,256]{1,0:T(8,128)(2,1)S(1)}, bf16[512,256]{1,0:T(8,128)(2,1)S(1)}, u32[]{:S(2)}, u32[]{:S(2)}) collective-permute-start(bf16[512,256]{1,0:T(8,128)(2,1)S(1)} %slice.24), channel_id=1, source_target_pairs={{0,3},{1,2},{2,1},{3,0},{4,7},{5,6},{6,5},{7,4},{8,11},{9,10},{10,... | collective-permute-start | bytes 786440 | tf_op jit(solution)/shard_map/ppermute | solution.py:320
  9.6 1.0 %collective-permute-done.3.rest_0_ = bf16[256,256]{1,0:T(8,128)(2,1)S(1)} collective-permute-done((bf16[256,256]{1,0:T(8,128)(2,1)S(1)}, bf16[256,256]{1,0:T(8,128)(2,1)S(1)}, u32[]{:S(2)}, u32[]{:S(2)}) %collective-permute-start.3) | collective-permute-done | bytes 131104 | tf_op jit(solution)/shard_map/ppermute | solution.py:320
  10.6 1.5 %collective-permute-start.4 = (bf16[256,256]{1,0:T(8,128)(2,1)S(1)}, bf16[256,256]{1,0:T(8,128)(2,1)S(1)}, u32[]{:S(2)}, u32[]{:S(2)}) collective-permute-start(bf16[256,256]{1,0:T(8,128)(2,1)S(1)} %collective-permute-done.3.rest_0_), channel_id=1, source_target_pairs={{0,4},{1,5},{2,6},{3,7},{4,0},{5,1},{6,2},{7,3},{8,12},{9,13},{10,... | collective-permute-start | bytes 393224 | tf_op jit(solution)/shard_map/ppermute | solution.py:320
  12.2 1.2 %collective-permute-start.1 = (f32[2,8,128]{2,1,0:T(8,128)S(1)}, f32[2,8,128]{2,1,0:T(8,128)S(1)}, u32[]{:S(2)}, u32[]{:S(2)}) collective-permute-start(f32[2,8,128]{2,1,0:T(8,128)S(1)} %collective-permute-done), channel_id=1, source_target_pairs={{0,1},{1,0},{2,3},{3,2},{4,5},{5,4},{6,7},{7,6},{8,9},{9,8},{10,11... | collective-permute-start | bytes 24584 | tf_op jit(solution)/shard_map/ppermute | solution.py:320
  13.5 0.8 reshape.65
  14.4 0.7 concatenate.18.table
  15.2 1.4 %collective-permute-done.4.rest_1_ = bf16[256,256]{1,0:T(8,128)(2,1)S(1)} collective-permute-done((bf16[256,256]{1,0:T(8,128)(2,1)S(1)}, bf16[256,256]{1,0:T(8,128)(2,1)S(1)}, u32[]{:S(2)}, u32[]{:S(2)}) %collective-permute-start.4) | collective-permute-done | bytes 131104 | tf_op jit(solution)/shard_map/ppermute | solution.py:320
  18.4 10.7 %shard_map.86 = (f32[32,128,1024]{2,1,0:T(8,128)S(1)}, f32[4096,128]{1,0:T(8,128)S(1)}, f32[32,128]{1,0:T(8,128)S(1)}) custom-call(s32[328]{0:T(512)S(1)} %concatenate.18.table, bf16[4096,256]{1,0:T(8,128)(2,1)} %run_hbm.1, f32[32,128]{1,0:T(8,128)} %bitcast.87, bf16[1024,256]{1,0:T(8,128)(2,1)} %own_hbm.1, f32[40,128]{1,0:T(8,128)S(1)} %concatenate.20.pot, ...), custom_call_target="tpu_custom_call" | custom-call | tf_op jit(solution)/shard_map/pallas_call | solution.py:421
  29.2 1.2 %collective-permute-done.10 = f32[32,128]{1,0:T(8,128)S(1)} collective-permute-done((f32[32,128]{1,0:T(8,128)S(1)}, f32[32,128]{1,0:T(8,128)S(1)}, u32[]{:S(2)}, u32[]{:S(2)}) %collective-permute-start.10) | collective-permute-done | bytes 16416 | tf_op jit(solution)/shard_map/ppermute | solution.py:320
  30.4 2.6 %collective-permute-start.13 = (f32[32,128]{1,0:T(8,128)S(1)}, f32[32,128]{1,0:T(8,128)S(1)}, u32[]{:S(2)}, u32[]{:S(2)}) collective-permute-start(f32[32,128]{1,0:T(8,128)S(1)} %multiply_add_fusion.1), channel_id=1, source_target_pairs={{0,7},{1,6},{2,5},{3,4},{4,3},{5,2},{6,1},{7,0},{8,15},{9,14},{10,... | collective-permute-start | bytes 49160 | tf_op jit(solution)/shard_map/ppermute | solution.py:320
  33.5 1.0 %collective-permute-done.13 = f32[32,128]{1,0:T(8,128)S(1)} collective-permute-done((f32[32,128]{1,0:T(8,128)S(1)}, f32[32,128]{1,0:T(8,128)S(1)}, u32[]{:S(2)}, u32[]{:S(2)}) %collective-permute-start.13) | collective-permute-done | bytes 16416 | tf_op jit(solution)/shard_map/ppermute | solution.py:320
  34.5 1.6 %collective-permute-done.12 = f32[32,128]{1,0:T(8,128)S(1)} collective-permute-done((f32[32,128]{1,0:T(8,128)S(1)}, f32[32,128]{1,0:T(8,128)S(1)}, u32[]{:S(2)}, u32[]{:S(2)}) %collective-permute-start.12) | collective-permute-done | bytes 16416 | tf_op jit(solution)/shard_map/ppermute | solution.py:320
  36.2 4.4 %collective-permute-start.16 = (f32[32,128]{1,0:T(8,128)S(1)}, f32[32,128]{1,0:T(8,128)S(1)}, u32[]{:S(2)}, u32[]{:S(2)}) collective-permute-start(f32[32,128]{1,0:T(8,128)S(1)} %multiply_add_fusion), channel_id=1, source_target_pairs={{0,25},{1,24},{2,27},{3,26},{4,29},{5,28},{6,31},{7,30},{8,17},{9,... | collective-permute-start | bytes 49160 | tf_op jit(solution)/shard_map/ppermute | solution.py:320
  40.9 1.0 %collective-permute-done.16 = f32[32,128]{1,0:T(8,128)S(1)} collective-permute-done((f32[32,128]{1,0:T(8,128)S(1)}, f32[32,128]{1,0:T(8,128)S(1)}, u32[]{:S(2)}, u32[]{:S(2)}) %collective-permute-start.16) | collective-permute-done | bytes 16416 | tf_op jit(solution)/shard_map/ppermute | solution.py:320
  42.0 2.6 %collective-permute-done.15 = f32[32,128]{1,0:T(8,128)S(1)} collective-permute-done((f32[32,128]{1,0:T(8,128)S(1)}, f32[32,128]{1,0:T(8,128)S(1)}, u32[]{:S(2)}, u32[]{:S(2)}) %collective-permute-start.15) | collective-permute-done | bytes 16416 | tf_op jit(solution)/shard_map/ppermute | solution.py:320
  44.6 5.2 %shard_map.87 = (f32[32,128,1024]{2,1,0:T(8,128)S(1)}, f32[4096,128]{1,0:T(8,128)S(1)}, f32[32,128]{1,0:T(8,128)S(1)}) custom-call(s32[328]{0:T(512)S(1)} %concatenate.18.table, f32[32,128,1024]{2,1,0:T(8,128)S(1)} %get-tuple-element.10.scores, f32[40,128]{1,0:T(8,128)S(1)} %concatenate.22.pot, ...), custom_call_target="tpu_custom_call", output_to_operand_aliasing={{0}: (1, {})} | custom-call | tf_op jit(solution)/shard_map/pallas_call | solution.py:445
  50.0 1.2 %collective-permute-done.17 = f32[32,128]{1,0:T(8,128)S(1)} collective-permute-done((f32[32,128]{1,0:T(8,128)S(1)}, f32[32,128]{1,0:T(8,128)S(1)}, u32[]{:S(2)}, u32[]{:S(2)}) %collective-permute-start.17) | collective-permute-done | bytes 16416 | tf_op jit(solution)/shard_map/ppermute | solution.py:320
  51.1 1.0 %collective-permute-start.20 = (f32[32,128]{1,0:T(8,128)S(1)}, f32[32,128]{1,0:T(8,128)S(1)}, u32[]{:S(2)}, u32[]{:S(2)}) collective-permute-start(f32[32,128]{1,0:T(8,128)S(1)} %add.241), channel_id=1, source_target_pairs={{0,7},{1,6},{2,5},{3,4},{4,3},{5,2},{6,1},{7,0},{8,15},{9,14},{10,... | collective-permute-start | bytes 49160 | tf_op jit(solution)/shard_map/ppermute | solution.py:320
  52.1 0.8 %collective-permute-start.19 = (f32[32,128]{1,0:T(8,128)S(1)}, f32[32,128]{1,0:T(8,128)S(1)}, u32[]{:S(2)}, u32[]{:S(2)}) collective-permute-start(f32[32,128]{1,0:T(8,128)S(1)} %add.241), channel_id=1, source_target_pairs={{0,5},{1,4},{2,7},{3,6},{4,1},{5,0},{6,3},{7,2},{8,13},{9,12},{10,... | collective-permute-start | bytes 49160 | tf_op jit(solution)/shard_map/ppermute | solution.py:320
  52.9 1.2 %collective-permute-start.18 = (f32[32,128]{1,0:T(8,128)S(1)}, f32[32,128]{1,0:T(8,128)S(1)}, u32[]{:S(2)}, u32[]{:S(2)}) collective-permute-start(f32[32,128]{1,0:T(8,128)S(1)} %add.241), channel_id=1, source_target_pairs={{0,3},{1,2},{2,1},{3,0},{4,7},{5,6},{6,5},{7,4},{8,11},{9,10},{10,... | collective-permute-start | bytes 49160 | tf_op jit(solution)/shard_map/ppermute | solution.py:320
  54.1 1.1 %collective-permute-done.20 = f32[32,128]{1,0:T(8,128)S(1)} collective-permute-done((f32[32,128]{1,0:T(8,128)S(1)}, f32[32,128]{1,0:T(8,128)S(1)}, u32[]{:S(2)}, u32[]{:S(2)}) %collective-permute-start.20) | collective-permute-done | bytes 16416 | tf_op jit(solution)/shard_map/ppermute | solution.py:320
  55.3 0.8 %collective-permute-done.18 = f32[32,128]{1,0:T(8,128)S(1)} collective-permute-done((f32[32,128]{1,0:T(8,128)S(1)}, f32[32,128]{1,0:T(8,128)S(1)}, u32[]{:S(2)}, u32[]{:S(2)}) %collective-permute-start.18) | collective-permute-done | bytes 16416 | tf_op jit(solution)/shard_map/ppermute | solution.py:320
  56.1 2.1 %collective-permute-start.23 = (f32[32,128]{1,0:T(8,128)S(1)}, f32[32,128]{1,0:T(8,128)S(1)}, u32[]{:S(2)}, u32[]{:S(2)}) collective-permute-start(f32[32,128]{1,0:T(8,128)S(1)} %add_add_fusion), channel_id=1, source_target_pairs={{0,25},{1,24},{2,27},{3,26},{4,29},{5,28},{6,31},{7,30},{8,17},{9,... | collective-permute-start | bytes 49160 | tf_op jit(solution)/shard_map/ppermute | solution.py:320
  58.2 1.8 %collective-permute-start.21 = (f32[32,128]{1,0:T(8,128)S(1)}, f32[32,128]{1,0:T(8,128)S(1)}, u32[]{:S(2)}, u32[]{:S(2)}) collective-permute-start(f32[32,128]{1,0:T(8,128)S(1)} %add_add_fusion), channel_id=1, source_target_pairs={{0,9},{1,8},{2,11},{3,10},{4,13},{5,12},{6,15},{7,14},{8,1},{9,0},... | collective-permute-start | bytes 49160 | tf_op jit(solution)/shard_map/ppermute | solution.py:320
  60.0 1.1 %collective-permute-done.23 = f32[32,128]{1,0:T(8,128)S(1)} collective-permute-done((f32[32,128]{1,0:T(8,128)S(1)}, f32[32,128]{1,0:T(8,128)S(1)}, u32[]{:S(2)}, u32[]{:S(2)}) %collective-permute-start.23) | collective-permute-done | bytes 16416 | tf_op jit(solution)/shard_map/ppermute | solution.py:320
  61.1 1.2 %collective-permute-done.22 = f32[32,128]{1,0:T(8,128)S(1)} collective-permute-done((f32[32,128]{1,0:T(8,128)S(1)}, f32[32,128]{1,0:T(8,128)S(1)}, u32[]{:S(2)}, u32[]{:S(2)}) %collective-permute-start.22) | collective-permute-done | bytes 16416 | tf_op jit(solution)/shard_map/ppermute | solution.py:320
  62.3 4.1 %shard_map.88 = (f32[32,128]{1,0:T(8,128)}, f32[8,32,128]{2,1,0:T(8,128)}) custom-call(s32[328]{0:T(512)S(1)} %concatenate.18.table, f32[32,128,1024]{2,1,0:T(8,128)S(1)} %get-tuple-element.13.weights, f32[4096,128]{1,0:T(8,128)S(1)} %get-tuple-element.14.peaks, f32[40,128]{1,0:T(8,128)S(1)} %concatenate.23.gain, ...), custom_call_target="tpu_custom_call" | custom-call | tf_op jit(solution)/shard_map/pallas_call | solution.py:452
  66.5 3.6 %all-to-all-start = ((f32[32,8,128]{2,1,0:T(8,128)}), f32[32,8,128]{2,1,0:T(8,128)S(1)}, u32[]{:S(2)}, u32[]{:S(2)}) async-start(f32[32,8,128]{2,1,0:T(8,128)} %bitcast.21), calls=%async_computation | async-start | bytes 262144 | tf_op jit(solution)/shard_map/all_to_all | solution.py:336
  70.1 8.2 %all-to-all-done = f32[32,8,128]{2,1,0:T(8,128)S(1)} async-done(((f32[32,8,128]{2,1,0:T(8,128)}), f32[32,8,128]{2,1,0:T(8,128)S(1)}, u32[]{:S(2)}, u32[]{:S(2)}) %all-to-all-start) | async-done | bytes 131104 | tf_op jit(solution)/shard_map/all_to_all | solution.py:336
  (48 shorter events, 6.8 us)
Async XLA Ops:
  1.3 13.8 %collective-permute-start.2 = (f32[2,8,128]{2,1,0:T(8,128)S(1)}, f32[2,8,128]{2,1,0:T(8,128)S(1)}, u32[]{:S(2)}, u32[]{:S(2)}) collective-permute-start(f32[2,8,128]{2,1,0:T(8,128)S(1)} %pad_maximum_fusion), channel_id=1, source_target_pairs={{0,1},{1,0},{2,3},{3,2},{4,5},{5,4},{6,7},{7,6},{8,9},{9,8},{10,11... | collective-permute-start | bytes 24584 | tf_op jit(solution)/shard_map/ppermute | solution.py:320
  1.8 10.4 %collective-permute-start = (f32[2,8,128]{2,1,0:T(8,128)S(1)}, f32[2,8,128]{2,1,0:T(8,128)S(1)}, u32[]{:S(2)}, u32[]{:S(2)}) collective-permute-start(f32[2,8,128]{2,1,0:T(8,128)S(1)} %pad_maximum_fusion), channel_id=1, source_target_pairs={{0,3},{1,2},{2,1},{3,0},{4,7},{5,6},{6,5},{7,4},{8,11},{9,10},{10,... | collective-permute-start | bytes 24584 | tf_op jit(solution)/shard_map/ppermute | solution.py:320
  4.4 13.9 %collective-permute-start.6 = (bf16[1024,256]{1,0:T(8,128)(2,1)}, bf16[1024,256]{1,0:T(8,128)(2,1)S(1)}, u32[]{:S(2)}, u32[]{:S(2)}) collective-permute-start(bf16[1024,256]{1,0:T(8,128)(2,1)} %own_hbm.1), channel_id=1, source_target_pairs={{0,1},{1,0},{2,3},{3,2},{4,5},{5,4},{6,7},{7,6},{8,9},{9,8},{10,11... | collective-permute-start | bytes 1572872 | tf_op jit(solution)/shard_map/ppermute | solution.py:320
  5.3 5.2 %collective-permute-start.3 = (bf16[256,256]{1,0:T(8,128)(2,1)S(1)}, bf16[256,256]{1,0:T(8,128)(2,1)S(1)}, u32[]{:S(2)}, u32[]{:S(2)}) collective-permute-start(bf16[256,256]{1,0:T(8,128)(2,1)S(1)} %constant_dynamic-slice_fusion), channel_id=1, source_target_pairs={{0,3},{1,2},{2,1},{3,0},{4,7},{5,6},{6,5},{7,4},{8,11},{9,10},{10,... | collective-permute-start | bytes 393224 | tf_op jit(solution)/shard_map/ppermute | solution.py:320
  6.4 10.3 %collective-permute-start.5 = (bf16[512,256]{1,0:T(8,128)(2,1)S(1)}, bf16[512,256]{1,0:T(8,128)(2,1)S(1)}, u32[]{:S(2)}, u32[]{:S(2)}) collective-permute-start(bf16[512,256]{1,0:T(8,128)(2,1)S(1)} %slice.24), channel_id=1, source_target_pairs={{0,3},{1,2},{2,1},{3,0},{4,7},{5,6},{6,5},{7,4},{8,11},{9,10},{10,... | collective-permute-start | bytes 786440 | tf_op jit(solution)/shard_map/ppermute | solution.py:320
  10.6 6.0 %collective-permute-start.4 = (bf16[256,256]{1,0:T(8,128)(2,1)S(1)}, bf16[256,256]{1,0:T(8,128)(2,1)S(1)}, u32[]{:S(2)}, u32[]{:S(2)}) collective-permute-start(bf16[256,256]{1,0:T(8,128)(2,1)S(1)} %collective-permute-done.3.rest_0_), channel_id=1, source_target_pairs={{0,4},{1,5},{2,6},{3,7},{4,0},{5,1},{6,2},{7,3},{8,12},{9,13},{10,... | collective-permute-start | bytes 393224 | tf_op jit(solution)/shard_map/ppermute | solution.py:320
  12.2 4.9 %collective-permute-start.1 = (f32[2,8,128]{2,1,0:T(8,128)S(1)}, f32[2,8,128]{2,1,0:T(8,128)S(1)}, u32[]{:S(2)}, u32[]{:S(2)}) collective-permute-start(f32[2,8,128]{2,1,0:T(8,128)S(1)} %collective-permute-done), channel_id=1, source_target_pairs={{0,1},{1,0},{2,3},{3,2},{4,5},{5,4},{6,7},{7,6},{8,9},{9,8},{10,11... | collective-permute-start | bytes 24584 | tf_op jit(solution)/shard_map/ppermute | solution.py:320
  15.1 2.7 %collective-permute-start.7 = (bf16[256,256]{1,0:T(8,128)(2,1)S(1)}, bf16[256,256]{1,0:T(8,128)(2,1)S(1)}, u32[]{:S(2)}, u32[]{:S(2)}) collective-permute-start(bf16[256,256]{1,0:T(8,128)(2,1)S(1)} %collective-permute-done.3.rest_0_), channel_id=1, source_target_pairs={{0,1},{1,0},{2,3},{3,2},{4,5},{5,4},{6,7},{7,6},{8,9},{9,8},{10,11... | collective-permute-start | bytes 393224 | tf_op jit(solution)/shard_map/ppermute | solution.py:320
  16.6 1.3 %collective-permute-start.8 = (bf16[256,256]{1,0:T(8,128)(2,1)S(1)}, bf16[256,256]{1,0:T(8,128)(2,1)S(1)}, u32[]{:S(2)}, u32[]{:S(2)}) collective-permute-start(bf16[256,256]{1,0:T(8,128)(2,1)S(1)} %collective-permute-done.4.rest_1_), channel_id=1, source_target_pairs={{0,1},{1,0},{2,3},{3,2},{4,5},{5,4},{6,7},{7,6},{8,9},{9,8},{10,11... | collective-permute-start | bytes 393224 | tf_op jit(solution)/shard_map/ppermute | solution.py:320
  16.8 1.5 %collective-permute-start.9 = (bf16[512,256]{1,0:T(8,128)(2,1)S(1)}, bf16[512,256]{1,0:T(8,128)(2,1)S(1)}, u32[]{:S(2)}, u32[]{:S(2)}) collective-permute-start(bf16[512,256]{1,0:T(8,128)(2,1)S(1)} %collective-permute-done.5.rest_2_), channel_id=1, source_target_pairs={{0,1},{1,0},{2,3},{3,2},{4,5},{5,4},{6,7},{7,6},{8,9},{9,8},{10,11... | collective-permute-start | bytes 786440 | tf_op jit(solution)/shard_map/ppermute | solution.py:320
  18.4 22.5 %copy-start = (f32[1024]{0:T(1024)S(1)}, f32[1024]{0:T(1024)}, u32[]{:S(2)}) copy-start(f32[1024]{0:T(1024)} %param.12) | copy-start | bytes 12292
  29.1 1.2 %collective-permute-start.10 = (f32[32,128]{1,0:T(8,128)S(1)}, f32[32,128]{1,0:T(8,128)S(1)}, u32[]{:S(2)}, u32[]{:S(2)}) collective-permute-start(f32[32,128]{1,0:T(8,128)S(1)} %get-tuple-element.11), channel_id=1, source_target_pairs={{0,1},{1,0},{2,3},{3,2},{4,5},{5,4},{6,7},{7,6},{8,9},{9,8},{10,11... | collective-permute-start | bytes 49160 | tf_op jit(solution)/shard_map/ppermute | solution.py:320
  30.4 4.1 %collective-permute-start.13 = (f32[32,128]{1,0:T(8,128)S(1)}, f32[32,128]{1,0:T(8,128)S(1)}, u32[]{:S(2)}, u32[]{:S(2)}) collective-permute-start(f32[32,128]{1,0:T(8,128)S(1)} %multiply_add_fusion.1), channel_id=1, source_target_pairs={{0,7},{1,6},{2,5},{3,4},{4,3},{5,2},{6,1},{7,0},{8,15},{9,14},{10,... | collective-permute-start | bytes 49160 | tf_op jit(solution)/shard_map/ppermute | solution.py:320
  33.0 3.2 %collective-permute-start.12 = (f32[32,128]{1,0:T(8,128)S(1)}, f32[32,128]{1,0:T(8,128)S(1)}, u32[]{:S(2)}, u32[]{:S(2)}) collective-permute-start(f32[32,128]{1,0:T(8,128)S(1)} %multiply_add_fusion.1), channel_id=1, source_target_pairs={{0,5},{1,4},{2,7},{3,6},{4,1},{5,0},{6,3},{7,2},{8,13},{9,12},{10,... | collective-permute-start | bytes 49160 | tf_op jit(solution)/shard_map/ppermute | solution.py:320
  33.0 3.2 %collective-permute-start.11 = (f32[32,128]{1,0:T(8,128)S(1)}, f32[32,128]{1,0:T(8,128)S(1)}, u32[]{:S(2)}, u32[]{:S(2)}) collective-permute-start(f32[32,128]{1,0:T(8,128)S(1)} %multiply_add_fusion.1), channel_id=1, source_target_pairs={{0,3},{1,2},{2,1},{3,0},{4,7},{5,6},{6,5},{7,4},{8,11},{9,10},{10,... | collective-permute-start | bytes 49160 | tf_op jit(solution)/shard_map/ppermute | solution.py:320
  36.2 5.8 %collective-permute-start.16 = (f32[32,128]{1,0:T(8,128)S(1)}, f32[32,128]{1,0:T(8,128)S(1)}, u32[]{:S(2)}, u32[]{:S(2)}) collective-permute-start(f32[32,128]{1,0:T(8,128)S(1)} %multiply_add_fusion), channel_id=1, source_target_pairs={{0,25},{1,24},{2,27},{3,26},{4,29},{5,28},{6,31},{7,30},{8,17},{9,... | collective-permute-start | bytes 49160 | tf_op jit(solution)/shard_map/ppermute | solution.py:320
  40.5 4.1 %collective-permute-start.15 = (f32[32,128]{1,0:T(8,128)S(1)}, f32[32,128]{1,0:T(8,128)S(1)}, u32[]{:S(2)}, u32[]{:S(2)}) collective-permute-start(f32[32,128]{1,0:T(8,128)S(1)} %multiply_add_fusion), channel_id=1, source_target_pairs={{0,17},{1,16},{2,19},{3,18},{4,21},{5,20},{6,23},{7,22},{8,25},{9,... | collective-permute-start | bytes 49160 | tf_op jit(solution)/shard_map/ppermute | solution.py:320
  40.5 4.1 %collective-permute-start.14 = (f32[32,128]{1,0:T(8,128)S(1)}, f32[32,128]{1,0:T(8,128)S(1)}, u32[]{:S(2)}, u32[]{:S(2)}) collective-permute-start(f32[32,128]{1,0:T(8,128)S(1)} %multiply_add_fusion), channel_id=1, source_target_pairs={{0,9},{1,8},{2,11},{3,10},{4,13},{5,12},{6,15},{7,14},{8,1},{9,0},... | collective-permute-start | bytes 49160 | tf_op jit(solution)/shard_map/ppermute | solution.py:320
  49.9 1.2 %collective-permute-start.17 = (f32[32,128]{1,0:T(8,128)S(1)}, f32[32,128]{1,0:T(8,128)S(1)}, u32[]{:S(2)}, u32[]{:S(2)}) collective-permute-start(f32[32,128]{1,0:T(8,128)S(1)} %get-tuple-element.15), channel_id=1, source_target_pairs={{0,1},{1,0},{2,3},{3,2},{4,5},{5,4},{6,7},{7,6},{8,9},{9,8},{10,11... | collective-permute-start | bytes 49160 | tf_op jit(solution)/shard_map/ppermute | solution.py:320
  51.1 4.1 %collective-permute-start.20 = (f32[32,128]{1,0:T(8,128)S(1)}, f32[32,128]{1,0:T(8,128)S(1)}, u32[]{:S(2)}, u32[]{:S(2)}) collective-permute-start(f32[32,128]{1,0:T(8,128)S(1)} %add.241), channel_id=1, source_target_pairs={{0,7},{1,6},{2,5},{3,4},{4,3},{5,2},{6,1},{7,0},{8,15},{9,14},{10,... | collective-permute-start | bytes 49160 | tf_op jit(solution)/shard_map/ppermute | solution.py:320
  52.1 3.2 %collective-permute-start.19 = (f32[32,128]{1,0:T(8,128)S(1)}, f32[32,128]{1,0:T(8,128)S(1)}, u32[]{:S(2)}, u32[]{:S(2)}) collective-permute-start(f32[32,128]{1,0:T(8,128)S(1)} %add.241), channel_id=1, source_target_pairs={{0,5},{1,4},{2,7},{3,6},{4,1},{5,0},{6,3},{7,2},{8,13},{9,12},{10,... | collective-permute-start | bytes 49160 | tf_op jit(solution)/shard_map/ppermute | solution.py:320
  52.9 3.2 %collective-permute-start.18 = (f32[32,128]{1,0:T(8,128)S(1)}, f32[32,128]{1,0:T(8,128)S(1)}, u32[]{:S(2)}, u32[]{:S(2)}) collective-permute-start(f32[32,128]{1,0:T(8,128)S(1)} %add.241), channel_id=1, source_target_pairs={{0,3},{1,2},{2,1},{3,0},{4,7},{5,6},{6,5},{7,4},{8,11},{9,10},{10,... | collective-permute-start | bytes 49160 | tf_op jit(solution)/shard_map/ppermute | solution.py:320
  56.1 5.0 %collective-permute-start.23 = (f32[32,128]{1,0:T(8,128)S(1)}, f32[32,128]{1,0:T(8,128)S(1)}, u32[]{:S(2)}, u32[]{:S(2)}) collective-permute-start(f32[32,128]{1,0:T(8,128)S(1)} %add_add_fusion), channel_id=1, source_target_pairs={{0,25},{1,24},{2,27},{3,26},{4,29},{5,28},{6,31},{7,30},{8,17},{9,... | collective-permute-start | bytes 49160 | tf_op jit(solution)/shard_map/ppermute | solution.py:320
  58.2 4.1 %collective-permute-start.22 = (f32[32,128]{1,0:T(8,128)S(1)}, f32[32,128]{1,0:T(8,128)S(1)}, u32[]{:S(2)}, u32[]{:S(2)}) collective-permute-start(f32[32,128]{1,0:T(8,128)S(1)} %add_add_fusion), channel_id=1, source_target_pairs={{0,17},{1,16},{2,19},{3,18},{4,21},{5,20},{6,23},{7,22},{8,25},{9,... | collective-permute-start | bytes 49160 | tf_op jit(solution)/shard_map/ppermute | solution.py:320
  58.2 4.1 %collective-permute-start.21 = (f32[32,128]{1,0:T(8,128)S(1)}, f32[32,128]{1,0:T(8,128)S(1)}, u32[]{:S(2)}, u32[]{:S(2)}) collective-permute-start(f32[32,128]{1,0:T(8,128)S(1)} %add_add_fusion), channel_id=1, source_target_pairs={{0,9},{1,8},{2,11},{3,10},{4,13},{5,12},{6,15},{7,14},{8,1},{9,0},... | collective-permute-start | bytes 49160 | tf_op jit(solution)/shard_map/ppermute | solution.py:320
  66.5 11.9 %all-to-all-start = ((f32[32,8,128]{2,1,0:T(8,128)}), f32[32,8,128]{2,1,0:T(8,128)S(1)}, u32[]{:S(2)}, u32[]{:S(2)}) async-start(f32[32,8,128]{2,1,0:T(8,128)} %bitcast.21), calls=%async_computation | async-start | bytes 262144 | tf_op jit(solution)/shard_map/all_to_all | solution.py:336

commit v7 on v6

--- a/solution.py
+++ b/solution.py
@@ -10,7 +10,7 @@
 
 BLK = 128
 TOPC = 8
-JOINED = 8
+JOINED = 16
 LOG2E = math.log2(math.e)
 FLOOR = -1e30
 VMEM_LIMIT = 8 * 1024 * 1024
@@ -19,11 +19,10 @@
 smem = pl.BlockSpec(memory_space=pltpu.SMEM)
 
 
-def group_size(run_blocks):
-    for size in (4, 2):
-        if run_blocks % size == 0:
-            return size
-    return 1
+def group_size(run_blocks, largest):
+    while run_blocks % largest:
+        largest //= 2
+    return largest
 
 
 class Table:
@@ -47,8 +46,8 @@
     def offset(self, index):
         return self.ref[(2 + TOPC) * self.run_blocks + index]
 
-    def by_groups(self, body, grain):
-        size = group_size(self.run_blocks)
+    def by_groups(self, body, grain, largest=4):
+        size = group_size(self.run_blocks, largest)
 
         def step(group, carry):
             most = self.live(group * size)
@@ -172,7 +171,7 @@
                 row = top + jnp.log2(jnp.sum(jnp.exp2(tile - top), axis=0, keepdims=True))
                 put_rows(rows, table.order(place), pair, row)
 
-    table.by_groups(body, 1)
+    table.by_groups(body, 1, 8)
 
     def join(step, carry):
         for k in range(JOINED):

time: 79.3 us -> 78.3 us (0.987)
  starting transfers between devices: 26.8 us -> 25.6 us
  transfers between devices with their start and end apart: 25 -> 25, of which waited for: 16 -> 17; matrix products, arithmetic and copies ran while one was open for 7% -> 7% of each run, Pallas kernels for 0% -> 0%
where the time goes in v7:
time: 78.3 us; the launch traced here: 77.9 us
  starting transfers between devices  25.6 us (33%)
  waiting for transfers between devices  23.9 us (31%)
  Pallas kernels  20.2 us (26%)
  other arithmetic  3.81 us (5%)
  local copies, waits for them, and re-layouts  3.56 us (5%)
  between operations  0.79 us (1%)
    ppermute x24, starting transfers between devices, swap(): return lax.ppermute(value, ('grp', 'nar'), pairs)  22.4 us
    ppermute x24, waiting for transfers between devices, swap(): return lax.ppermute(value, ('grp', 'nar'), pairs)  15.7 us
    pallas_call x1, Pallas kernels, shards(): call(first_kernel, [smem] + [pl.BlockSpec(memory_space=pltpu.HBM)] * 3 +...  10.6 us
    all_to_all x1, waiting for transfers between devices, reduce_own(): return join(list(lax.all_to_all(sent, ('grp', 'nar'), 0, 0, tiled=True)))  8.22 us
    pallas_call x1, Pallas kernels, shards(): call(second_kernel, [smem] + [vmem] * 4, [score_shape, rep_shape, table_s...  5.44 us
    pallas_call x1, Pallas kernels, shards(): call(third_kernel, [smem] + [vmem] * 5, [jax.ShapeDtypeStruct((run_blocks...  4.18 us
    all_to_all x1, starting transfers between devices, reduce_own(): return join(list(lax.all_to_all(sent, ('grp', 'nar'), 0, 0, tiled=True)))  3.23 us
  transfers between devices with their start and end apart: 25, of which 17 were waited for; matrix products, arithmetic and copies ran while one was open for 7% of the time, Pallas kernels for 0%

profile of v7, /device:TPU:0, one launch (start us, length us, event | category | flops | bytes accessed | tf_op | source)
XLA Modules:
  0.0 77.9 jit_solution(5955093687235054960)
XLA Ops:
  0.6 0.7 pad_maximum_fusion
  1.8 2.6 %collective-permute-start = (f32[2,8,128]{2,1,0:T(8,128)S(1)}, f32[2,8,128]{2,1,0:T(8,128)S(1)}, u32[]{:S(2)}, u32[]{:S(2)}) collective-permute-start(f32[2,8,128]{2,1,0:T(8,128)S(1)} %pad_maximum_fusion), channel_id=1, source_target_pairs={{0,3},{1,2},{2,1},{3,0},{4,7},{5,6},{6,5},{7,4},{8,11},{9,10},{10,... | collective-permute-start | bytes 24584 | tf_op jit(solution)/shard_map/ppermute | solution.py:319
  4.4 0.9 %constant_dynamic-slice_fusion = bf16[256,256]{1,0:T(8,128)(2,1)S(1)} fusion(bf16[1024,256]{1,0:T(8,128)(2,1)} %own_hbm.1, s32[]{:T(128)S(6)} %select_n.123), kind=kLoop, calls=%fused_computation.93 | loop fusion | bytes 262148 | tf_op jit(solution)/shard_map/dynamic_slice | solution.py:361
  5.5 1.0 %slice.24 = bf16[512,256]{1,0:T(8,128)(2,1)S(1)} slice(bf16[1024,256]{1,0:T(8,128)(2,1)} %own_hbm.1), slice={[256:768], [0:256]} | slice | bytes 524288 | tf_op jit(solution)/shard_map/slice | solution.py:362
  6.4 1.8 %collective-permute-start.5 = (bf16[512,256]{1,0:T(8,128)(2,1)S(1)}, bf16[512,256]{1,0:T(8,128)(2,1)S(1)}, u32[]{:S(2)}, u32[]{:S(2)}) collective-permute-start(bf16[512,256]{1,0:T(8,128)(2,1)S(1)} %slice.24), channel_id=1, source_target_pairs={{0,3},{1,2},{2,1},{3,0},{4,7},{5,6},{6,5},{7,4},{8,11},{9,10},{10,... | collective-permute-start | bytes 786440 | tf_op jit(solution)/shard_map/ppermute | solution.py:319
  9.6 1.0 %collective-permute-done.3.rest_0_ = bf16[256,256]{1,0:T(8,128)(2,1)S(1)} collective-permute-done((bf16[256,256]{1,0:T(8,128)(2,1)S(1)}, bf16[256,256]{1,0:T(8,128)(2,1)S(1)}, u32[]{:S(2)}, u32[]{:S(2)}) %collective-permute-start.3) | collective-permute-done | bytes 131104 | tf_op jit(solution)/shard_map/ppermute | solution.py:319
  10.6 1.5 %collective-permute-start.4 = (bf16[256,256]{1,0:T(8,128)(2,1)S(1)}, bf16[256,256]{1,0:T(8,128)(2,1)S(1)}, u32[]{:S(2)}, u32[]{:S(2)}) collective-permute-start(bf16[256,256]{1,0:T(8,128)(2,1)S(1)} %collective-permute-done.3.rest_0_), channel_id=1, source_target_pairs={{0,4},{1,5},{2,6},{3,7},{4,0},{5,1},{6,2},{7,3},{8,12},{9,13},{10,... | collective-permute-start | bytes 393224 | tf_op jit(solution)/shard_map/ppermute | solution.py:319
  12.2 1.2 %collective-permute-start.1 = (f32[2,8,128]{2,1,0:T(8,128)S(1)}, f32[2,8,128]{2,1,0:T(8,128)S(1)}, u32[]{:S(2)}, u32[]{:S(2)}) collective-permute-start(f32[2,8,128]{2,1,0:T(8,128)S(1)} %collective-permute-done), channel_id=1, source_target_pairs={{0,1},{1,0},{2,3},{3,2},{4,5},{5,4},{6,7},{7,6},{8,9},{9,8},{10,11... | collective-permute-start | bytes 24584 | tf_op jit(solution)/shard_map/ppermute | solution.py:319
  13.5 0.8 reshape.65
  14.4 0.7 concatenate.18.table
  15.2 1.4 %collective-permute-done.4.rest_1_ = bf16[256,256]{1,0:T(8,128)(2,1)S(1)} collective-permute-done((bf16[256,256]{1,0:T(8,128)(2,1)S(1)}, bf16[256,256]{1,0:T(8,128)(2,1)S(1)}, u32[]{:S(2)}, u32[]{:S(2)}) %collective-permute-start.4) | collective-permute-done | bytes 131104 | tf_op jit(solution)/shard_map/ppermute | solution.py:319
  18.4 10.6 %shard_map.86 = (f32[32,128,1024]{2,1,0:T(8,128)S(1)}, f32[4096,128]{1,0:T(8,128)S(1)}, f32[32,128]{1,0:T(8,128)S(1)}) custom-call(s32[328]{0:T(512)S(1)} %concatenate.18.table, bf16[4096,256]{1,0:T(8,128)(2,1)} %run_hbm.1, f32[32,128]{1,0:T(8,128)} %bitcast.87, bf16[1024,256]{1,0:T(8,128)(2,1)} %own_hbm.1, f32[40,128]{1,0:T(8,128)S(1)} %concatenate.20.pot, ...), custom_call_target="tpu_custom_call" | custom-call | tf_op jit(solution)/shard_map/pallas_call | solution.py:420
  29.1 1.2 %collective-permute-done.10 = f32[32,128]{1,0:T(8,128)S(1)} collective-permute-done((f32[32,128]{1,0:T(8,128)S(1)}, f32[32,128]{1,0:T(8,128)S(1)}, u32[]{:S(2)}, u32[]{:S(2)}) %collective-permute-start.10) | collective-permute-done | bytes 16416 | tf_op jit(solution)/shard_map/ppermute | solution.py:319
  30.3 1.3 %collective-permute-start.13 = (f32[32,128]{1,0:T(8,128)S(1)}, f32[32,128]{1,0:T(8,128)S(1)}, u32[]{:S(2)}, u32[]{:S(2)}) collective-permute-start(f32[32,128]{1,0:T(8,128)S(1)} %multiply_add_fusion.1), channel_id=1, source_target_pairs={{0,7},{1,6},{2,5},{3,4},{4,3},{5,2},{6,1},{7,0},{8,15},{9,14},{10,... | collective-permute-start | bytes 49160 | tf_op jit(solution)/shard_map/ppermute | solution.py:319
  32.1 1.2 %collective-permute-start.11 = (f32[32,128]{1,0:T(8,128)S(1)}, f32[32,128]{1,0:T(8,128)S(1)}, u32[]{:S(2)}, u32[]{:S(2)}) collective-permute-start(f32[32,128]{1,0:T(8,128)S(1)} %multiply_add_fusion.1), channel_id=1, source_target_pairs={{0,3},{1,2},{2,1},{3,0},{4,7},{5,6},{6,5},{7,4},{8,11},{9,10},{10,... | collective-permute-start | bytes 49160 | tf_op jit(solution)/shard_map/ppermute | solution.py:319
  33.3 1.1 %collective-permute-done.13 = f32[32,128]{1,0:T(8,128)S(1)} collective-permute-done((f32[32,128]{1,0:T(8,128)S(1)}, f32[32,128]{1,0:T(8,128)S(1)}, u32[]{:S(2)}, u32[]{:S(2)}) %collective-permute-start.13) | collective-permute-done | bytes 16416 | tf_op jit(solution)/shard_map/ppermute | solution.py:319
  35.3 3.3 %collective-permute-start.16 = (f32[32,128]{1,0:T(8,128)S(1)}, f32[32,128]{1,0:T(8,128)S(1)}, u32[]{:S(2)}, u32[]{:S(2)}) collective-permute-start(f32[32,128]{1,0:T(8,128)S(1)} %multiply_add_fusion), channel_id=1, source_target_pairs={{0,25},{1,24},{2,27},{3,26},{4,29},{5,28},{6,31},{7,30},{8,17},{9,... | collective-permute-start | bytes 49160 | tf_op jit(solution)/shard_map/ppermute | solution.py:319
  39.3 1.1 %collective-permute-done.16 = f32[32,128]{1,0:T(8,128)S(1)} collective-permute-done((f32[32,128]{1,0:T(8,128)S(1)}, f32[32,128]{1,0:T(8,128)S(1)}, u32[]{:S(2)}, u32[]{:S(2)}) %collective-permute-start.16) | collective-permute-done | bytes 16416 | tf_op jit(solution)/shard_map/ppermute | solution.py:319
  40.4 2.3 %collective-permute-done.15 = f32[32,128]{1,0:T(8,128)S(1)} collective-permute-done((f32[32,128]{1,0:T(8,128)S(1)}, f32[32,128]{1,0:T(8,128)S(1)}, u32[]{:S(2)}, u32[]{:S(2)}) %collective-permute-start.15) | collective-permute-done | bytes 16416 | tf_op jit(solution)/shard_map/ppermute | solution.py:319
  42.8 5.4 %shard_map.87 = (f32[32,128,1024]{2,1,0:T(8,128)S(1)}, f32[4096,128]{1,0:T(8,128)S(1)}, f32[32,128]{1,0:T(8,128)S(1)}) custom-call(s32[328]{0:T(512)S(1)} %concatenate.18.table, f32[32,128,1024]{2,1,0:T(8,128)S(1)} %get-tuple-element.10.scores, f32[40,128]{1,0:T(8,128)S(1)} %concatenate.22.pot, ...), custom_call_target="tpu_custom_call", output_to_operand_aliasing={{0}: (1, {})} | custom-call | tf_op jit(solution)/shard_map/pallas_call | solution.py:444
  48.3 1.2 %collective-permute-done.17 = f32[32,128]{1,0:T(8,128)S(1)} collective-permute-done((f32[32,128]{1,0:T(8,128)S(1)}, f32[32,128]{1,0:T(8,128)S(1)}, u32[]{:S(2)}, u32[]{:S(2)}) %collective-permute-start.17) | collective-permute-done | bytes 16416 | tf_op jit(solution)/shard_map/ppermute | solution.py:319
  49.5 1.8 %collective-permute-start.20 = (f32[32,128]{1,0:T(8,128)S(1)}, f32[32,128]{1,0:T(8,128)S(1)}, u32[]{:S(2)}, u32[]{:S(2)}) collective-permute-start(f32[32,128]{1,0:T(8,128)S(1)} %add.241), channel_id=1, source_target_pairs={{0,7},{1,6},{2,5},{3,4},{4,3},{5,2},{6,1},{7,0},{8,15},{9,14},{10,... | collective-permute-start | bytes 49160 | tf_op jit(solution)/shard_map/ppermute | solution.py:319
  51.4 1.1 %collective-permute-start.18 = (f32[32,128]{1,0:T(8,128)S(1)}, f32[32,128]{1,0:T(8,128)S(1)}, u32[]{:S(2)}, u32[]{:S(2)}) collective-permute-start(f32[32,128]{1,0:T(8,128)S(1)} %add.241), channel_id=1, source_target_pairs={{0,3},{1,2},{2,1},{3,0},{4,7},{5,6},{6,5},{7,4},{8,11},{9,10},{10,... | collective-permute-start | bytes 49160 | tf_op jit(solution)/shard_map/ppermute | solution.py:319
  52.5 1.1 %collective-permute-done.20 = f32[32,128]{1,0:T(8,128)S(1)} collective-permute-done((f32[32,128]{1,0:T(8,128)S(1)}, f32[32,128]{1,0:T(8,128)S(1)}, u32[]{:S(2)}, u32[]{:S(2)}) %collective-permute-start.20) | collective-permute-done | bytes 16416 | tf_op jit(solution)/shard_map/ppermute | solution.py:319
  53.6 0.9 %collective-permute-done.19 = f32[32,128]{1,0:T(8,128)S(1)} collective-permute-done((f32[32,128]{1,0:T(8,128)S(1)}, f32[32,128]{1,0:T(8,128)S(1)}, u32[]{:S(2)}, u32[]{:S(2)}) %collective-permute-start.19) | collective-permute-done | bytes 16416 | tf_op jit(solution)/shard_map/ppermute | solution.py:319
  54.6 3.0 %collective-permute-start.23 = (f32[32,128]{1,0:T(8,128)S(1)}, f32[32,128]{1,0:T(8,128)S(1)}, u32[]{:S(2)}, u32[]{:S(2)}) collective-permute-start(f32[32,128]{1,0:T(8,128)S(1)} %add_add_fusion), channel_id=1, source_target_pairs={{0,25},{1,24},{2,27},{3,26},{4,29},{5,28},{6,31},{7,30},{8,17},{9,... | collective-permute-start | bytes 49160 | tf_op jit(solution)/shard_map/ppermute | solution.py:319
  57.6 1.1 %collective-permute-start.21 = (f32[32,128]{1,0:T(8,128)S(1)}, f32[32,128]{1,0:T(8,128)S(1)}, u32[]{:S(2)}, u32[]{:S(2)}) collective-permute-start(f32[32,128]{1,0:T(8,128)S(1)} %add_add_fusion), channel_id=1, source_target_pairs={{0,9},{1,8},{2,11},{3,10},{4,13},{5,12},{6,15},{7,14},{8,1},{9,0},... | collective-permute-start | bytes 49160 | tf_op jit(solution)/shard_map/ppermute | solution.py:319
  58.6 1.0 %collective-permute-done.23 = f32[32,128]{1,0:T(8,128)S(1)} collective-permute-done((f32[32,128]{1,0:T(8,128)S(1)}, f32[32,128]{1,0:T(8,128)S(1)}, u32[]{:S(2)}, u32[]{:S(2)}) %collective-permute-start.23) | collective-permute-done | bytes 16416 | tf_op jit(solution)/shard_map/ppermute | solution.py:319
  59.6 2.0 %collective-permute-done.22 = f32[32,128]{1,0:T(8,128)S(1)} collective-permute-done((f32[32,128]{1,0:T(8,128)S(1)}, f32[32,128]{1,0:T(8,128)S(1)}, u32[]{:S(2)}, u32[]{:S(2)}) %collective-permute-start.22) | collective-permute-done | bytes 16416 | tf_op jit(solution)/shard_map/ppermute | solution.py:319
  61.7 4.2 %shard_map.88 = (f32[32,128]{1,0:T(8,128)}, f32[8,32,128]{2,1,0:T(8,128)}) custom-call(s32[328]{0:T(512)S(1)} %concatenate.18.table, f32[32,128,1024]{2,1,0:T(8,128)S(1)} %get-tuple-element.13.weights, f32[4096,128]{1,0:T(8,128)S(1)} %get-tuple-element.14.peaks, f32[40,128]{1,0:T(8,128)S(1)} %concatenate.23.gain, ...), custom_call_target="tpu_custom_call" | custom-call | tf_op jit(solution)/shard_map/pallas_call | solution.py:451
  65.9 3.2 %all-to-all-start = ((f32[32,8,128]{2,1,0:T(8,128)}), f32[32,8,128]{2,1,0:T(8,128)S(1)}, u32[]{:S(2)}, u32[]{:S(2)}) async-start(f32[32,8,128]{2,1,0:T(8,128)} %bitcast.21), calls=%async_computation | async-start | bytes 262144 | tf_op jit(solution)/shard_map/all_to_all | solution.py:335
  69.1 8.2 %all-to-all-done = f32[32,8,128]{2,1,0:T(8,128)S(1)} async-done(((f32[32,8,128]{2,1,0:T(8,128)}), f32[32,8,128]{2,1,0:T(8,128)S(1)}, u32[]{:S(2)}, u32[]{:S(2)}) %all-to-all-start) | async-done | bytes 131104 | tf_op jit(solution)/shard_map/all_to_all | solution.py:335
  (48 shorter events, 7.4 us)
Async XLA Ops:
  1.3 13.8 %collective-permute-start.2 = (f32[2,8,128]{2,1,0:T(8,128)S(1)}, f32[2,8,128]{2,1,0:T(8,128)S(1)}, u32[]{:S(2)}, u32[]{:S(2)}) collective-permute-start(f32[2,8,128]{2,1,0:T(8,128)S(1)} %pad_maximum_fusion), channel_id=1, source_target_pairs={{0,1},{1,0},{2,3},{3,2},{4,5},{5,4},{6,7},{7,6},{8,9},{9,8},{10,11... | collective-permute-start | bytes 24584 | tf_op jit(solution)/shard_map/ppermute | solution.py:319
  1.8 10.4 %collective-permute-start = (f32[2,8,128]{2,1,0:T(8,128)S(1)}, f32[2,8,128]{2,1,0:T(8,128)S(1)}, u32[]{:S(2)}, u32[]{:S(2)}) collective-permute-start(f32[2,8,128]{2,1,0:T(8,128)S(1)} %pad_maximum_fusion), channel_id=1, source_target_pairs={{0,3},{1,2},{2,1},{3,0},{4,7},{5,6},{6,5},{7,4},{8,11},{9,10},{10,... | collective-permute-start | bytes 24584 | tf_op jit(solution)/shard_map/ppermute | solution.py:319
  4.4 13.9 %collective-permute-start.6 = (bf16[1024,256]{1,0:T(8,128)(2,1)}, bf16[1024,256]{1,0:T(8,128)(2,1)S(1)}, u32[]{:S(2)}, u32[]{:S(2)}) collective-permute-start(bf16[1024,256]{1,0:T(8,128)(2,1)} %own_hbm.1), channel_id=1, source_target_pairs={{0,1},{1,0},{2,3},{3,2},{4,5},{5,4},{6,7},{7,6},{8,9},{9,8},{10,11... | collective-permute-start | bytes 1572872 | tf_op jit(solution)/shard_map/ppermute | solution.py:319
  5.3 5.2 %collective-permute-start.3 = (bf16[256,256]{1,0:T(8,128)(2,1)S(1)}, bf16[256,256]{1,0:T(8,128)(2,1)S(1)}, u32[]{:S(2)}, u32[]{:S(2)}) collective-permute-start(bf16[256,256]{1,0:T(8,128)(2,1)S(1)} %constant_dynamic-slice_fusion), channel_id=1, source_target_pairs={{0,3},{1,2},{2,1},{3,0},{4,7},{5,6},{6,5},{7,4},{8,11},{9,10},{10,... | collective-permute-start | bytes 393224 | tf_op jit(solution)/shard_map/ppermute | solution.py:319
  6.4 10.3 %collective-permute-start.5 = (bf16[512,256]{1,0:T(8,128)(2,1)S(1)}, bf16[512,256]{1,0:T(8,128)(2,1)S(1)}, u32[]{:S(2)}, u32[]{:S(2)}) collective-permute-start(bf16[512,256]{1,0:T(8,128)(2,1)S(1)} %slice.24), channel_id=1, source_target_pairs={{0,3},{1,2},{2,1},{3,0},{4,7},{5,6},{6,5},{7,4},{8,11},{9,10},{10,... | collective-permute-start | bytes 786440 | tf_op jit(solution)/shard_map/ppermute | solution.py:319
  10.6 6.0 %collective-permute-start.4 = (bf16[256,256]{1,0:T(8,128)(2,1)S(1)}, bf16[256,256]{1,0:T(8,128)(2,1)S(1)}, u32[]{:S(2)}, u32[]{:S(2)}) collective-permute-start(bf16[256,256]{1,0:T(8,128)(2,1)S(1)} %collective-permute-done.3.rest_0_), channel_id=1, source_target_pairs={{0,4},{1,5},{2,6},{3,7},{4,0},{5,1},{6,2},{7,3},{8,12},{9,13},{10,... | collective-permute-start | bytes 393224 | tf_op jit(solution)/shard_map/ppermute | solution.py:319
  12.2 4.9 %collective-permute-start.1 = (f32[2,8,128]{2,1,0:T(8,128)S(1)}, f32[2,8,128]{2,1,0:T(8,128)S(1)}, u32[]{:S(2)}, u32[]{:S(2)}) collective-permute-start(f32[2,8,128]{2,1,0:T(8,128)S(1)} %collective-permute-done), channel_id=1, source_target_pairs={{0,1},{1,0},{2,3},{3,2},{4,5},{5,4},{6,7},{7,6},{8,9},{9,8},{10,11... | collective-permute-start | bytes 24584 | tf_op jit(solution)/shard_map/ppermute | solution.py:319
  15.1 2.7 %collective-permute-start.7 = (bf16[256,256]{1,0:T(8,128)(2,1)S(1)}, bf16[256,256]{1,0:T(8,128)(2,1)S(1)}, u32[]{:S(2)}, u32[]{:S(2)}) collective-permute-start(bf16[256,256]{1,0:T(8,128)(2,1)S(1)} %collective-permute-done.3.rest_0_), channel_id=1, source_target_pairs={{0,1},{1,0},{2,3},{3,2},{4,5},{5,4},{6,7},{7,6},{8,9},{9,8},{10,11... | collective-permute-start | bytes 393224 | tf_op jit(solution)/shard_map/ppermute | solution.py:319
  16.6 1.3 %collective-permute-start.8 = (bf16[256,256]{1,0:T(8,128)(2,1)S(1)}, bf16[256,256]{1,0:T(8,128)(2,1)S(1)}, u32[]{:S(2)}, u32[]{:S(2)}) collective-permute-start(bf16[256,256]{1,0:T(8,128)(2,1)S(1)} %collective-permute-done.4.rest_1_), channel_id=1, source_target_pairs={{0,1},{1,0},{2,3},{3,2},{4,5},{5,4},{6,7},{7,6},{8,9},{9,8},{10,11... | collective-permute-start | bytes 393224 | tf_op jit(solution)/shard_map/ppermute | solution.py:319
  16.8 1.5 %collective-permute-start.9 = (bf16[512,256]{1,0:T(8,128)(2,1)S(1)}, bf16[512,256]{1,0:T(8,128)(2,1)S(1)}, u32[]{:S(2)}, u32[]{:S(2)}) collective-permute-start(bf16[512,256]{1,0:T(8,128)(2,1)S(1)} %collective-permute-done.5.rest_2_), channel_id=1, source_target_pairs={{0,1},{1,0},{2,3},{3,2},{4,5},{5,4},{6,7},{7,6},{8,9},{9,8},{10,11... | collective-permute-start | bytes 786440 | tf_op jit(solution)/shard_map/ppermute | solution.py:319
  18.4 20.9 %copy-start = (f32[1024]{0:T(1024)S(1)}, f32[1024]{0:T(1024)}, u32[]{:S(2)}) copy-start(f32[1024]{0:T(1024)} %param.12) | copy-start | bytes 12292
  29.0 1.2 %collective-permute-start.10 = (f32[32,128]{1,0:T(8,128)S(1)}, f32[32,128]{1,0:T(8,128)S(1)}, u32[]{:S(2)}, u32[]{:S(2)}) collective-permute-start(f32[32,128]{1,0:T(8,128)S(1)} %get-tuple-element.11), channel_id=1, source_target_pairs={{0,1},{1,0},{2,3},{3,2},{4,5},{5,4},{6,7},{7,6},{8,9},{9,8},{10,11... | collective-permute-start | bytes 49160 | tf_op jit(solution)/shard_map/ppermute | solution.py:319
  30.3 4.1 %collective-permute-start.13 = (f32[32,128]{1,0:T(8,128)S(1)}, f32[32,128]{1,0:T(8,128)S(1)}, u32[]{:S(2)}, u32[]{:S(2)}) collective-permute-start(f32[32,128]{1,0:T(8,128)S(1)} %multiply_add_fusion.1), channel_id=1, source_target_pairs={{0,7},{1,6},{2,5},{3,4},{4,3},{5,2},{6,1},{7,0},{8,15},{9,14},{10,... | collective-permute-start | bytes 49160 | tf_op jit(solution)/shard_map/ppermute | solution.py:319
  31.6 3.2 %collective-permute-start.12 = (f32[32,128]{1,0:T(8,128)S(1)}, f32[32,128]{1,0:T(8,128)S(1)}, u32[]{:S(2)}, u32[]{:S(2)}) collective-permute-start(f32[32,128]{1,0:T(8,128)S(1)} %multiply_add_fusion.1), channel_id=1, source_target_pairs={{0,5},{1,4},{2,7},{3,6},{4,1},{5,0},{6,3},{7,2},{8,13},{9,12},{10,... | collective-permute-start | bytes 49160 | tf_op jit(solution)/shard_map/ppermute | solution.py:319
  32.1 3.2 %collective-permute-start.11 = (f32[32,128]{1,0:T(8,128)S(1)}, f32[32,128]{1,0:T(8,128)S(1)}, u32[]{:S(2)}, u32[]{:S(2)}) collective-permute-start(f32[32,128]{1,0:T(8,128)S(1)} %multiply_add_fusion.1), channel_id=1, source_target_pairs={{0,3},{1,2},{2,1},{3,0},{4,7},{5,6},{6,5},{7,4},{8,11},{9,10},{10,... | collective-permute-start | bytes 49160 | tf_op jit(solution)/shard_map/ppermute | solution.py:319
  35.3 5.1 %collective-permute-start.16 = (f32[32,128]{1,0:T(8,128)S(1)}, f32[32,128]{1,0:T(8,128)S(1)}, u32[]{:S(2)}, u32[]{:S(2)}) collective-permute-start(f32[32,128]{1,0:T(8,128)S(1)} %multiply_add_fusion), channel_id=1, source_target_pairs={{0,25},{1,24},{2,27},{3,26},{4,29},{5,28},{6,31},{7,30},{8,17},{9,... | collective-permute-start | bytes 49160 | tf_op jit(solution)/shard_map/ppermute | solution.py:319
  38.7 4.1 %collective-permute-start.15 = (f32[32,128]{1,0:T(8,128)S(1)}, f32[32,128]{1,0:T(8,128)S(1)}, u32[]{:S(2)}, u32[]{:S(2)}) collective-permute-start(f32[32,128]{1,0:T(8,128)S(1)} %multiply_add_fusion), channel_id=1, source_target_pairs={{0,17},{1,16},{2,19},{3,18},{4,21},{5,20},{6,23},{7,22},{8,25},{9,... | collective-permute-start | bytes 49160 | tf_op jit(solution)/shard_map/ppermute | solution.py:319
  38.9 3.9 %collective-permute-start.14 = (f32[32,128]{1,0:T(8,128)S(1)}, f32[32,128]{1,0:T(8,128)S(1)}, u32[]{:S(2)}, u32[]{:S(2)}) collective-permute-start(f32[32,128]{1,0:T(8,128)S(1)} %multiply_add_fusion), channel_id=1, source_target_pairs={{0,9},{1,8},{2,11},{3,10},{4,13},{5,12},{6,15},{7,14},{8,1},{9,0},... | collective-permute-start | bytes 49160 | tf_op jit(solution)/shard_map/ppermute | solution.py:319
  48.3 1.2 %collective-permute-start.17 = (f32[32,128]{1,0:T(8,128)S(1)}, f32[32,128]{1,0:T(8,128)S(1)}, u32[]{:S(2)}, u32[]{:S(2)}) collective-permute-start(f32[32,128]{1,0:T(8,128)S(1)} %get-tuple-element.15), channel_id=1, source_target_pairs={{0,1},{1,0},{2,3},{3,2},{4,5},{5,4},{6,7},{7,6},{8,9},{9,8},{10,11... | collective-permute-start | bytes 49160 | tf_op jit(solution)/shard_map/ppermute | solution.py:319
  49.5 4.1 %collective-permute-start.20 = (f32[32,128]{1,0:T(8,128)S(1)}, f32[32,128]{1,0:T(8,128)S(1)}, u32[]{:S(2)}, u32[]{:S(2)}) collective-permute-start(f32[32,128]{1,0:T(8,128)S(1)} %add.241), channel_id=1, source_target_pairs={{0,7},{1,6},{2,5},{3,4},{4,3},{5,2},{6,1},{7,0},{8,15},{9,14},{10,... | collective-permute-start | bytes 49160 | tf_op jit(solution)/shard_map/ppermute | solution.py:319
  51.3 3.2 %collective-permute-start.19 = (f32[32,128]{1,0:T(8,128)S(1)}, f32[32,128]{1,0:T(8,128)S(1)}, u32[]{:S(2)}, u32[]{:S(2)}) collective-permute-start(f32[32,128]{1,0:T(8,128)S(1)} %add.241), channel_id=1, source_target_pairs={{0,5},{1,4},{2,7},{3,6},{4,1},{5,0},{6,3},{7,2},{8,13},{9,12},{10,... | collective-permute-start | bytes 49160 | tf_op jit(solution)/shard_map/ppermute | solution.py:319
  51.4 3.2 %collective-permute-start.18 = (f32[32,128]{1,0:T(8,128)S(1)}, f32[32,128]{1,0:T(8,128)S(1)}, u32[]{:S(2)}, u32[]{:S(2)}) collective-permute-start(f32[32,128]{1,0:T(8,128)S(1)} %add.241), channel_id=1, source_target_pairs={{0,3},{1,2},{2,1},{3,0},{4,7},{5,6},{6,5},{7,4},{8,11},{9,10},{10,... | collective-permute-start | bytes 49160 | tf_op jit(solution)/shard_map/ppermute | solution.py:319
  54.6 5.0 %collective-permute-start.23 = (f32[32,128]{1,0:T(8,128)S(1)}, f32[32,128]{1,0:T(8,128)S(1)}, u32[]{:S(2)}, u32[]{:S(2)}) collective-permute-start(f32[32,128]{1,0:T(8,128)S(1)} %add_add_fusion), channel_id=1, source_target_pairs={{0,25},{1,24},{2,27},{3,26},{4,29},{5,28},{6,31},{7,30},{8,17},{9,... | collective-permute-start | bytes 49160 | tf_op jit(solution)/shard_map/ppermute | solution.py:319
  57.6 4.1 %collective-permute-start.22 = (f32[32,128]{1,0:T(8,128)S(1)}, f32[32,128]{1,0:T(8,128)S(1)}, u32[]{:S(2)}, u32[]{:S(2)}) collective-permute-start(f32[32,128]{1,0:T(8,128)S(1)} %add_add_fusion), channel_id=1, source_target_pairs={{0,17},{1,16},{2,19},{3,18},{4,21},{5,20},{6,23},{7,22},{8,25},{9,... | collective-permute-start | bytes 49160 | tf_op jit(solution)/shard_map/ppermute | solution.py:319
  57.6 4.1 %collective-permute-start.21 = (f32[32,128]{1,0:T(8,128)S(1)}, f32[32,128]{1,0:T(8,128)S(1)}, u32[]{:S(2)}, u32[]{:S(2)}) collective-permute-start(f32[32,128]{1,0:T(8,128)S(1)} %add_add_fusion), channel_id=1, source_target_pairs={{0,9},{1,8},{2,11},{3,10},{4,13},{5,12},{6,15},{7,14},{8,1},{9,0},... | collective-permute-start | bytes 49160 | tf_op jit(solution)/shard_map/ppermute | solution.py:319
  65.9 11.5 %all-to-all-start = ((f32[32,8,128]{2,1,0:T(8,128)}), f32[32,8,128]{2,1,0:T(8,128)S(1)}, u32[]{:S(2)}, u32[]{:S(2)}) async-start(f32[32,8,128]{2,1,0:T(8,128)} %bitcast.21), calls=%async_computation | async-start | bytes 262144 | tf_op jit(solution)/shard_map/all_to_all | solution.py:335

commit v8 on v7

--- a/solution.py
+++ b/solution.py
@@ -10,7 +10,7 @@
 
 BLK = 128
 TOPC = 8
-JOINED = 16
+JOINED = 32
 LOG2E = math.log2(math.e)
 FLOOR = -1e30
 VMEM_LIMIT = 8 * 1024 * 1024

time: 78.3 us -> 78.8 us (level)
  starting transfers between devices: 25.6 us -> 30.3 us
  Pallas kernels: 20.2 us -> 16.2 us
    ppermute x24, starting transfers between devices: 22.4 us -> 26.2 us  [swap(): return lax.ppermute(value, ('grp', 'nar'), pairs)]
    pallas_call x1, Pallas kernels: 10.6 us -> 8.42 us  [shards(): call(first_kernel, [smem] + [pl.BlockSpec(memory_space=pltpu.HBM)] * 3 +...]
    pallas_call x1, Pallas kernels: 5.44 us -> 4.13 us  [shards(): call(second_kernel, [smem] + [vmem] * 4, [score_shape, rep_shape, table_s...]
    all_to_all x1, starting transfers between devices: 3.23 us -> 4.07 us  [reduce_own(): return join(list(lax.all_to_all(sent, ('grp', 'nar'), 0, 0, tiled=True)))]
  transfers between devices with their start and end apart: 25 -> 25, of which waited for: 17 -> 16; matrix products, arithmetic and copies ran while one was open for 7% -> 7% of each run, Pallas kernels for 0% -> 0%
where the time goes in v8:
time: 78.8 us; the launch traced here: 78.1 us
  starting transfers between devices  30.3 us (38%)
  waiting for transfers between devices  23.5 us (30%)
  Pallas kernels  16.2 us (21%)
  other arithmetic  3.81 us (5%)
  local copies, waits for them, and re-layouts  3.56 us (5%)
    ppermute x24, starting transfers between devices, swap(): return lax.ppermute(value, ('grp', 'nar'), pairs)  26.2 us
    ppermute x24, waiting for transfers between devices, swap(): return lax.ppermute(value, ('grp', 'nar'), pairs)  15.2 us
    pallas_call x1, Pallas kernels, shards(): call(first_kernel, [smem] + [pl.BlockSpec(memory_space=pltpu.HBM)] * 3 +...  8.42 us
    all_to_all x1, waiting for transfers between devices, reduce_own(): return join(list(lax.all_to_all(sent, ('grp', 'nar'), 0, 0, tiled=True)))  8.22 us
    pallas_call x1, Pallas kernels, shards(): call(second_kernel, [smem] + [vmem] * 4, [score_shape, rep_shape, table_s...  4.13 us
    all_to_all x1, starting transfers between devices, reduce_own(): return join(list(lax.all_to_all(sent, ('grp', 'nar'), 0, 0, tiled=True)))  4.07 us
    pallas_call x1, Pallas kernels, shards(): call(third_kernel, [smem] + [vmem] * 5, [jax.ShapeDtypeStruct((run_blocks...  3.64 us
  transfers between devices with their start and end apart: 25, of which 16 were waited for; matrix products, arithmetic and copies ran while one was open for 7% of the time, Pallas kernels for 0%

profile of v8, /device:TPU:0, one launch (start us, length us, event | category | flops | bytes accessed | tf_op | source)
XLA Modules:
  0.0 78.1 jit_solution(3981319946717481164)
XLA Ops:
  1.8 2.6 %collective-permute-start = (f32[2,8,128]{2,1,0:T(8,128)S(1)}, f32[2,8,128]{2,1,0:T(8,128)S(1)}, u32[]{:S(2)}, u32[]{:S(2)}) collective-permute-start(f32[2,8,128]{2,1,0:T(8,128)S(1)} %pad_maximum_fusion), channel_id=1, source_target_pairs={{0,3},{1,2},{2,1},{3,0},{4,7},{5,6},{6,5},{7,4},{8,11},{9,10},{10,... | collective-permute-start | bytes 24584 | tf_op jit(solution)/shard_map/ppermute | solution.py:319
  4.4 0.9 %constant_dynamic-slice_fusion = bf16[256,256]{1,0:T(8,128)(2,1)S(1)} fusion(bf16[1024,256]{1,0:T(8,128)(2,1)} %own_hbm.1, s32[]{:T(128)S(6)} %select_n.123), kind=kLoop, calls=%fused_computation.93 | loop fusion | bytes 262148 | tf_op jit(solution)/shard_map/dynamic_slice | solution.py:361
  5.5 1.0 %slice.24 = bf16[512,256]{1,0:T(8,128)(2,1)S(1)} slice(bf16[1024,256]{1,0:T(8,128)(2,1)} %own_hbm.1), slice={[256:768], [0:256]} | slice | bytes 524288 | tf_op jit(solution)/shard_map/slice | solution.py:362
  6.4 1.8 %collective-permute-start.5 = (bf16[512,256]{1,0:T(8,128)(2,1)S(1)}, bf16[512,256]{1,0:T(8,128)(2,1)S(1)}, u32[]{:S(2)}, u32[]{:S(2)}) collective-permute-start(bf16[512,256]{1,0:T(8,128)(2,1)S(1)} %slice.24), channel_id=1, source_target_pairs={{0,3},{1,2},{2,1},{3,0},{4,7},{5,6},{6,5},{7,4},{8,11},{9,10},{10,... | collective-permute-start | bytes 786440 | tf_op jit(solution)/shard_map/ppermute | solution.py:319
  9.6 1.0 %collective-permute-done.3.rest_0_ = bf16[256,256]{1,0:T(8,128)(2,1)S(1)} collective-permute-done((bf16[256,256]{1,0:T(8,128)(2,1)S(1)}, bf16[256,256]{1,0:T(8,128)(2,1)S(1)}, u32[]{:S(2)}, u32[]{:S(2)}) %collective-permute-start.3) | collective-permute-done | bytes 131104 | tf_op jit(solution)/shard_map/ppermute | solution.py:319
  10.6 1.5 %collective-permute-start.4 = (bf16[256,256]{1,0:T(8,128)(2,1)S(1)}, bf16[256,256]{1,0:T(8,128)(2,1)S(1)}, u32[]{:S(2)}, u32[]{:S(2)}) collective-permute-start(bf16[256,256]{1,0:T(8,128)(2,1)S(1)} %collective-permute-done.3.rest_0_), channel_id=1, source_target_pairs={{0,4},{1,5},{2,6},{3,7},{4,0},{5,1},{6,2},{7,3},{8,12},{9,13},{10,... | collective-permute-start | bytes 393224 | tf_op jit(solution)/shard_map/ppermute | solution.py:319
  12.2 1.2 %collective-permute-start.1 = (f32[2,8,128]{2,1,0:T(8,128)S(1)}, f32[2,8,128]{2,1,0:T(8,128)S(1)}, u32[]{:S(2)}, u32[]{:S(2)}) collective-permute-start(f32[2,8,128]{2,1,0:T(8,128)S(1)} %collective-permute-done), channel_id=1, source_target_pairs={{0,1},{1,0},{2,3},{3,2},{4,5},{5,4},{6,7},{7,6},{8,9},{9,8},{10,11... | collective-permute-start | bytes 24584 | tf_op jit(solution)/shard_map/ppermute | solution.py:319
  13.5 0.8 reshape.65
  14.4 0.7 concatenate.18.table
  15.2 1.4 %collective-permute-done.4.rest_1_ = bf16[256,256]{1,0:T(8,128)(2,1)S(1)} collective-permute-done((bf16[256,256]{1,0:T(8,128)(2,1)S(1)}, bf16[256,256]{1,0:T(8,128)(2,1)S(1)}, u32[]{:S(2)}, u32[]{:S(2)}) %collective-permute-start.4) | collective-permute-done | bytes 131104 | tf_op jit(solution)/shard_map/ppermute | solution.py:319
  18.4 8.4 %shard_map.86 = (f32[32,128,1024]{2,1,0:T(8,128)S(1)}, f32[4096,128]{1,0:T(8,128)S(1)}, f32[32,128]{1,0:T(8,128)S(1)}) custom-call(s32[328]{0:T(512)S(1)} %concatenate.18.table, bf16[4096,256]{1,0:T(8,128)(2,1)} %run_hbm.1, f32[32,128]{1,0:T(8,128)} %bitcast.87, bf16[1024,256]{1,0:T(8,128)(2,1)} %own_hbm.1, f32[40,128]{1,0:T(8,128)S(1)} %concatenate.20.pot, ...), custom_call_target="tpu_custom_call" | custom-call | tf_op jit(solution)/shard_map/pallas_call | solution.py:420
  26.8 1.3 %collective-permute-start.10 = (f32[32,128]{1,0:T(8,128)S(1)}, f32[32,128]{1,0:T(8,128)S(1)}, u32[]{:S(2)}, u32[]{:S(2)}) collective-permute-start(f32[32,128]{1,0:T(8,128)S(1)} %get-tuple-element.11), channel_id=1, source_target_pairs={{0,1},{1,0},{2,3},{3,2},{4,5},{5,4},{6,7},{7,6},{8,9},{9,8},{10,11... | collective-permute-start | bytes 49160 | tf_op jit(solution)/shard_map/ppermute | solution.py:319
  28.1 0.8 %collective-permute-done.10 = f32[32,128]{1,0:T(8,128)S(1)} collective-permute-done((f32[32,128]{1,0:T(8,128)S(1)}, f32[32,128]{1,0:T(8,128)S(1)}, u32[]{:S(2)}, u32[]{:S(2)}) %collective-permute-start.10) | collective-permute-done | bytes 16416 | tf_op jit(solution)/shard_map/ppermute | solution.py:319
  29.0 2.7 %collective-permute-start.13 = (f32[32,128]{1,0:T(8,128)S(1)}, f32[32,128]{1,0:T(8,128)S(1)}, u32[]{:S(2)}, u32[]{:S(2)}) collective-permute-start(f32[32,128]{1,0:T(8,128)S(1)} %multiply_add_fusion.1), channel_id=1, source_target_pairs={{0,7},{1,6},{2,5},{3,4},{4,3},{5,2},{6,1},{7,0},{8,15},{9,14},{10,... | collective-permute-start | bytes 49160 | tf_op jit(solution)/shard_map/ppermute | solution.py:319
  32.2 0.9 %collective-permute-done.13 = f32[32,128]{1,0:T(8,128)S(1)} collective-permute-done((f32[32,128]{1,0:T(8,128)S(1)}, f32[32,128]{1,0:T(8,128)S(1)}, u32[]{:S(2)}, u32[]{:S(2)}) %collective-permute-start.13) | collective-permute-done | bytes 16416 | tf_op jit(solution)/shard_map/ppermute | solution.py:319
  33.1 1.7 %collective-permute-done.12 = f32[32,128]{1,0:T(8,128)S(1)} collective-permute-done((f32[32,128]{1,0:T(8,128)S(1)}, f32[32,128]{1,0:T(8,128)S(1)}, u32[]{:S(2)}, u32[]{:S(2)}) %collective-permute-start.12) | collective-permute-done | bytes 16416 | tf_op jit(solution)/shard_map/ppermute | solution.py:319
  34.8 4.3 %collective-permute-start.16 = (f32[32,128]{1,0:T(8,128)S(1)}, f32[32,128]{1,0:T(8,128)S(1)}, u32[]{:S(2)}, u32[]{:S(2)}) collective-permute-start(f32[32,128]{1,0:T(8,128)S(1)} %multiply_add_fusion), channel_id=1, source_target_pairs={{0,25},{1,24},{2,27},{3,26},{4,29},{5,28},{6,31},{7,30},{8,17},{9,... | collective-permute-start | bytes 49160 | tf_op jit(solution)/shard_map/ppermute | solution.py:319
  39.7 0.8 %collective-permute-done.16 = f32[32,128]{1,0:T(8,128)S(1)} collective-permute-done((f32[32,128]{1,0:T(8,128)S(1)}, f32[32,128]{1,0:T(8,128)S(1)}, u32[]{:S(2)}, u32[]{:S(2)}) %collective-permute-start.16) | collective-permute-done | bytes 16416 | tf_op jit(solution)/shard_map/ppermute | solution.py:319
  40.6 2.6 %collective-permute-done.15 = f32[32,128]{1,0:T(8,128)S(1)} collective-permute-done((f32[32,128]{1,0:T(8,128)S(1)}, f32[32,128]{1,0:T(8,128)S(1)}, u32[]{:S(2)}, u32[]{:S(2)}) %collective-permute-start.15) | collective-permute-done | bytes 16416 | tf_op jit(solution)/shard_map/ppermute | solution.py:319
  43.3 4.1 %shard_map.87 = (f32[32,128,1024]{2,1,0:T(8,128)S(1)}, f32[4096,128]{1,0:T(8,128)S(1)}, f32[32,128]{1,0:T(8,128)S(1)}) custom-call(s32[328]{0:T(512)S(1)} %concatenate.18.table, f32[32,128,1024]{2,1,0:T(8,128)S(1)} %get-tuple-element.10.scores, f32[40,128]{1,0:T(8,128)S(1)} %concatenate.22.pot, ...), custom_call_target="tpu_custom_call", output_to_operand_aliasing={{0}: (1, {})} | custom-call | tf_op jit(solution)/shard_map/pallas_call | solution.py:444
  47.4 0.9 %collective-permute-start.17 = (f32[32,128]{1,0:T(8,128)S(1)}, f32[32,128]{1,0:T(8,128)S(1)}, u32[]{:S(2)}, u32[]{:S(2)}) collective-permute-start(f32[32,128]{1,0:T(8,128)S(1)} %get-tuple-element.15), channel_id=1, source_target_pairs={{0,1},{1,0},{2,3},{3,2},{4,5},{5,4},{6,7},{7,6},{8,9},{9,8},{10,11... | collective-permute-start | bytes 49160 | tf_op jit(solution)/shard_map/ppermute | solution.py:319
  48.3 0.8 %collective-permute-done.17 = f32[32,128]{1,0:T(8,128)S(1)} collective-permute-done((f32[32,128]{1,0:T(8,128)S(1)}, f32[32,128]{1,0:T(8,128)S(1)}, u32[]{:S(2)}, u32[]{:S(2)}) %collective-permute-start.17) | collective-permute-done | bytes 16416 | tf_op jit(solution)/shard_map/ppermute | solution.py:319
  49.2 3.0 %collective-permute-start.20 = (f32[32,128]{1,0:T(8,128)S(1)}, f32[32,128]{1,0:T(8,128)S(1)}, u32[]{:S(2)}, u32[]{:S(2)}) collective-permute-start(f32[32,128]{1,0:T(8,128)S(1)} %add.241), channel_id=1, source_target_pairs={{0,7},{1,6},{2,5},{3,4},{4,3},{5,2},{6,1},{7,0},{8,15},{9,14},{10,... | collective-permute-start | bytes 49160 | tf_op jit(solution)/shard_map/ppermute | solution.py:319
  52.7 0.9 %collective-permute-done.20 = f32[32,128]{1,0:T(8,128)S(1)} collective-permute-done((f32[32,128]{1,0:T(8,128)S(1)}, f32[32,128]{1,0:T(8,128)S(1)}, u32[]{:S(2)}, u32[]{:S(2)}) %collective-permute-start.20) | collective-permute-done | bytes 16416 | tf_op jit(solution)/shard_map/ppermute | solution.py:319
  53.6 1.7 %collective-permute-done.19 = f32[32,128]{1,0:T(8,128)S(1)} collective-permute-done((f32[32,128]{1,0:T(8,128)S(1)}, f32[32,128]{1,0:T(8,128)S(1)}, u32[]{:S(2)}, u32[]{:S(2)}) %collective-permute-start.19) | collective-permute-done | bytes 16416 | tf_op jit(solution)/shard_map/ppermute | solution.py:319
  55.6 1.8 %collective-permute-start.23 = (f32[32,128]{1,0:T(8,128)S(1)}, f32[32,128]{1,0:T(8,128)S(1)}, u32[]{:S(2)}, u32[]{:S(2)}) collective-permute-start(f32[32,128]{1,0:T(8,128)S(1)} %add_add_fusion), channel_id=1, source_target_pairs={{0,25},{1,24},{2,27},{3,26},{4,29},{5,28},{6,31},{7,30},{8,17},{9,... | collective-permute-start | bytes 49160 | tf_op jit(solution)/shard_map/ppermute | solution.py:319
  57.4 2.4 %collective-permute-start.21 = (f32[32,128]{1,0:T(8,128)S(1)}, f32[32,128]{1,0:T(8,128)S(1)}, u32[]{:S(2)}, u32[]{:S(2)}) collective-permute-start(f32[32,128]{1,0:T(8,128)S(1)} %add_add_fusion), channel_id=1, source_target_pairs={{0,9},{1,8},{2,11},{3,10},{4,13},{5,12},{6,15},{7,14},{8,1},{9,0},... | collective-permute-start | bytes 49160 | tf_op jit(solution)/shard_map/ppermute | solution.py:319
  59.7 0.9 %collective-permute-done.23 = f32[32,128]{1,0:T(8,128)S(1)} collective-permute-done((f32[32,128]{1,0:T(8,128)S(1)}, f32[32,128]{1,0:T(8,128)S(1)}, u32[]{:S(2)}, u32[]{:S(2)}) %collective-permute-start.23) | collective-permute-done | bytes 16416 | tf_op jit(solution)/shard_map/ppermute | solution.py:319
  60.6 0.9 %collective-permute-done.22 = f32[32,128]{1,0:T(8,128)S(1)} collective-permute-done((f32[32,128]{1,0:T(8,128)S(1)}, f32[32,128]{1,0:T(8,128)S(1)}, u32[]{:S(2)}, u32[]{:S(2)}) %collective-permute-start.22) | collective-permute-done | bytes 16416 | tf_op jit(solution)/shard_map/ppermute | solution.py:319
  61.6 3.6 %shard_map.88 = (f32[32,128]{1,0:T(8,128)}, f32[8,32,128]{2,1,0:T(8,128)}) custom-call(s32[328]{0:T(512)S(1)} %concatenate.18.table, f32[32,128,1024]{2,1,0:T(8,128)S(1)} %get-tuple-element.13.weights, f32[4096,128]{1,0:T(8,128)S(1)} %get-tuple-element.14.peaks, f32[40,128]{1,0:T(8,128)S(1)} %concatenate.23.gain, ...), custom_call_target="tpu_custom_call" | custom-call | tf_op jit(solution)/shard_map/pallas_call | solution.py:451
  65.2 4.1 %all-to-all-start = ((f32[32,8,128]{2,1,0:T(8,128)}), f32[32,8,128]{2,1,0:T(8,128)S(1)}, u32[]{:S(2)}, u32[]{:S(2)}) async-start(f32[32,8,128]{2,1,0:T(8,128)} %bitcast.21), calls=%async_computation | async-start | bytes 262144 | tf_op jit(solution)/shard_map/all_to_all | solution.py:335
  69.3 8.2 %all-to-all-done = f32[32,8,128]{2,1,0:T(8,128)S(1)} async-done(((f32[32,8,128]{2,1,0:T(8,128)}), f32[32,8,128]{2,1,0:T(8,128)S(1)}, u32[]{:S(2)}, u32[]{:S(2)}) %all-to-all-start) | async-done | bytes 131104 | tf_op jit(solution)/shard_map/all_to_all | solution.py:335
  (48 shorter events, 7.7 us)
Async XLA Ops:
  1.3 13.8 %collective-permute-start.2 = (f32[2,8,128]{2,1,0:T(8,128)S(1)}, f32[2,8,128]{2,1,0:T(8,128)S(1)}, u32[]{:S(2)}, u32[]{:S(2)}) collective-permute-start(f32[2,8,128]{2,1,0:T(8,128)S(1)} %pad_maximum_fusion), channel_id=1, source_target_pairs={{0,1},{1,0},{2,3},{3,2},{4,5},{5,4},{6,7},{7,6},{8,9},{9,8},{10,11... | collective-permute-start | bytes 24584 | tf_op jit(solution)/shard_map/ppermute | solution.py:319
  1.8 10.4 %collective-permute-start = (f32[2,8,128]{2,1,0:T(8,128)S(1)}, f32[2,8,128]{2,1,0:T(8,128)S(1)}, u32[]{:S(2)}, u32[]{:S(2)}) collective-permute-start(f32[2,8,128]{2,1,0:T(8,128)S(1)} %pad_maximum_fusion), channel_id=1, source_target_pairs={{0,3},{1,2},{2,1},{3,0},{4,7},{5,6},{6,5},{7,4},{8,11},{9,10},{10,... | collective-permute-start | bytes 24584 | tf_op jit(solution)/shard_map/ppermute | solution.py:319
  4.4 13.9 %collective-permute-start.6 = (bf16[1024,256]{1,0:T(8,128)(2,1)}, bf16[1024,256]{1,0:T(8,128)(2,1)S(1)}, u32[]{:S(2)}, u32[]{:S(2)}) collective-permute-start(bf16[1024,256]{1,0:T(8,128)(2,1)} %own_hbm.1), channel_id=1, source_target_pairs={{0,1},{1,0},{2,3},{3,2},{4,5},{5,4},{6,7},{7,6},{8,9},{9,8},{10,11... | collective-permute-start | bytes 1572872 | tf_op jit(solution)/shard_map/ppermute | solution.py:319
  5.3 5.2 %collective-permute-start.3 = (bf16[256,256]{1,0:T(8,128)(2,1)S(1)}, bf16[256,256]{1,0:T(8,128)(2,1)S(1)}, u32[]{:S(2)}, u32[]{:S(2)}) collective-permute-start(bf16[256,256]{1,0:T(8,128)(2,1)S(1)} %constant_dynamic-slice_fusion), channel_id=1, source_target_pairs={{0,3},{1,2},{2,1},{3,0},{4,7},{5,6},{6,5},{7,4},{8,11},{9,10},{10,... | collective-permute-start | bytes 393224 | tf_op jit(solution)/shard_map/ppermute | solution.py:319
  6.4 10.3 %collective-permute-start.5 = (bf16[512,256]{1,0:T(8,128)(2,1)S(1)}, bf16[512,256]{1,0:T(8,128)(2,1)S(1)}, u32[]{:S(2)}, u32[]{:S(2)}) collective-permute-start(bf16[512,256]{1,0:T(8,128)(2,1)S(1)} %slice.24), channel_id=1, source_target_pairs={{0,3},{1,2},{2,1},{3,0},{4,7},{5,6},{6,5},{7,4},{8,11},{9,10},{10,... | collective-permute-start | bytes 786440 | tf_op jit(solution)/shard_map/ppermute | solution.py:319
  10.6 6.0 %collective-permute-start.4 = (bf16[256,256]{1,0:T(8,128)(2,1)S(1)}, bf16[256,256]{1,0:T(8,128)(2,1)S(1)}, u32[]{:S(2)}, u32[]{:S(2)}) collective-permute-start(bf16[256,256]{1,0:T(8,128)(2,1)S(1)} %collective-permute-done.3.rest_0_), channel_id=1, source_target_pairs={{0,4},{1,5},{2,6},{3,7},{4,0},{5,1},{6,2},{7,3},{8,12},{9,13},{10,... | collective-permute-start | bytes 393224 | tf_op jit(solution)/shard_map/ppermute | solution.py:319
  12.2 4.9 %collective-permute-start.1 = (f32[2,8,128]{2,1,0:T(8,128)S(1)}, f32[2,8,128]{2,1,0:T(8,128)S(1)}, u32[]{:S(2)}, u32[]{:S(2)}) collective-permute-start(f32[2,8,128]{2,1,0:T(8,128)S(1)} %collective-permute-done), channel_id=1, source_target_pairs={{0,1},{1,0},{2,3},{3,2},{4,5},{5,4},{6,7},{7,6},{8,9},{9,8},{10,11... | collective-permute-start | bytes 24584 | tf_op jit(solution)/shard_map/ppermute | solution.py:319
  15.1 2.7 %collective-permute-start.7 = (bf16[256,256]{1,0:T(8,128)(2,1)S(1)}, bf16[256,256]{1,0:T(8,128)(2,1)S(1)}, u32[]{:S(2)}, u32[]{:S(2)}) collective-permute-start(bf16[256,256]{1,0:T(8,128)(2,1)S(1)} %collective-permute-done.3.rest_0_), channel_id=1, source_target_pairs={{0,1},{1,0},{2,3},{3,2},{4,5},{5,4},{6,7},{7,6},{8,9},{9,8},{10,11... | collective-permute-start | bytes 393224 | tf_op jit(solution)/shard_map/ppermute | solution.py:319
  16.6 1.3 %collective-permute-start.8 = (bf16[256,256]{1,0:T(8,128)(2,1)S(1)}, bf16[256,256]{1,0:T(8,128)(2,1)S(1)}, u32[]{:S(2)}, u32[]{:S(2)}) collective-permute-start(bf16[256,256]{1,0:T(8,128)(2,1)S(1)} %collective-permute-done.4.rest_1_), channel_id=1, source_target_pairs={{0,1},{1,0},{2,3},{3,2},{4,5},{5,4},{6,7},{7,6},{8,9},{9,8},{10,11... | collective-permute-start | bytes 393224 | tf_op jit(solution)/shard_map/ppermute | solution.py:319
  16.8 1.5 %collective-permute-start.9 = (bf16[512,256]{1,0:T(8,128)(2,1)S(1)}, bf16[512,256]{1,0:T(8,128)(2,1)S(1)}, u32[]{:S(2)}, u32[]{:S(2)}) collective-permute-start(bf16[512,256]{1,0:T(8,128)(2,1)S(1)} %collective-permute-done.5.rest_2_), channel_id=1, source_target_pairs={{0,1},{1,0},{2,3},{3,2},{4,5},{5,4},{6,7},{7,6},{8,9},{9,8},{10,11... | collective-permute-start | bytes 786440 | tf_op jit(solution)/shard_map/ppermute | solution.py:319
  18.4 21.3 %copy-start = (f32[1024]{0:T(1024)S(1)}, f32[1024]{0:T(1024)}, u32[]{:S(2)}) copy-start(f32[1024]{0:T(1024)} %param.12) | copy-start | bytes 12292
  26.8 2.1 %collective-permute-start.10 = (f32[32,128]{1,0:T(8,128)S(1)}, f32[32,128]{1,0:T(8,128)S(1)}, u32[]{:S(2)}, u32[]{:S(2)}) collective-permute-start(f32[32,128]{1,0:T(8,128)S(1)} %get-tuple-element.11), channel_id=1, source_target_pairs={{0,1},{1,0},{2,3},{3,2},{4,5},{5,4},{6,7},{7,6},{8,9},{9,8},{10,11... | collective-permute-start | bytes 49160 | tf_op jit(solution)/shard_map/ppermute | solution.py:319
  29.0 4.1 %collective-permute-start.13 = (f32[32,128]{1,0:T(8,128)S(1)}, f32[32,128]{1,0:T(8,128)S(1)}, u32[]{:S(2)}, u32[]{:S(2)}) collective-permute-start(f32[32,128]{1,0:T(8,128)S(1)} %multiply_add_fusion.1), channel_id=1, source_target_pairs={{0,7},{1,6},{2,5},{3,4},{4,3},{5,2},{6,1},{7,0},{8,15},{9,14},{10,... | collective-permute-start | bytes 49160 | tf_op jit(solution)/shard_map/ppermute | solution.py:319
  31.6 3.2 %collective-permute-start.12 = (f32[32,128]{1,0:T(8,128)S(1)}, f32[32,128]{1,0:T(8,128)S(1)}, u32[]{:S(2)}, u32[]{:S(2)}) collective-permute-start(f32[32,128]{1,0:T(8,128)S(1)} %multiply_add_fusion.1), channel_id=1, source_target_pairs={{0,5},{1,4},{2,7},{3,6},{4,1},{5,0},{6,3},{7,2},{8,13},{9,12},{10,... | collective-permute-start | bytes 49160 | tf_op jit(solution)/shard_map/ppermute | solution.py:319
  31.6 3.2 %collective-permute-start.11 = (f32[32,128]{1,0:T(8,128)S(1)}, f32[32,128]{1,0:T(8,128)S(1)}, u32[]{:S(2)}, u32[]{:S(2)}) collective-permute-start(f32[32,128]{1,0:T(8,128)S(1)} %multiply_add_fusion.1), channel_id=1, source_target_pairs={{0,3},{1,2},{2,1},{3,0},{4,7},{5,6},{6,5},{7,4},{8,11},{9,10},{10,... | collective-permute-start | bytes 49160 | tf_op jit(solution)/shard_map/ppermute | solution.py:319
  34.8 5.8 %collective-permute-start.16 = (f32[32,128]{1,0:T(8,128)S(1)}, f32[32,128]{1,0:T(8,128)S(1)}, u32[]{:S(2)}, u32[]{:S(2)}) collective-permute-start(f32[32,128]{1,0:T(8,128)S(1)} %multiply_add_fusion), channel_id=1, source_target_pairs={{0,25},{1,24},{2,27},{3,26},{4,29},{5,28},{6,31},{7,30},{8,17},{9,... | collective-permute-start | bytes 49160 | tf_op jit(solution)/shard_map/ppermute | solution.py:319
  39.1 4.1 %collective-permute-start.15 = (f32[32,128]{1,0:T(8,128)S(1)}, f32[32,128]{1,0:T(8,128)S(1)}, u32[]{:S(2)}, u32[]{:S(2)}) collective-permute-start(f32[32,128]{1,0:T(8,128)S(1)} %multiply_add_fusion), channel_id=1, source_target_pairs={{0,17},{1,16},{2,19},{3,18},{4,21},{5,20},{6,23},{7,22},{8,25},{9,... | collective-permute-start | bytes 49160 | tf_op jit(solution)/shard_map/ppermute | solution.py:319
  39.1 4.1 %collective-permute-start.14 = (f32[32,128]{1,0:T(8,128)S(1)}, f32[32,128]{1,0:T(8,128)S(1)}, u32[]{:S(2)}, u32[]{:S(2)}) collective-permute-start(f32[32,128]{1,0:T(8,128)S(1)} %multiply_add_fusion), channel_id=1, source_target_pairs={{0,9},{1,8},{2,11},{3,10},{4,13},{5,12},{6,15},{7,14},{8,1},{9,0},... | collective-permute-start | bytes 49160 | tf_op jit(solution)/shard_map/ppermute | solution.py:319
  47.4 1.8 %collective-permute-start.17 = (f32[32,128]{1,0:T(8,128)S(1)}, f32[32,128]{1,0:T(8,128)S(1)}, u32[]{:S(2)}, u32[]{:S(2)}) collective-permute-start(f32[32,128]{1,0:T(8,128)S(1)} %get-tuple-element.15), channel_id=1, source_target_pairs={{0,1},{1,0},{2,3},{3,2},{4,5},{5,4},{6,7},{7,6},{8,9},{9,8},{10,11... | collective-permute-start | bytes 49160 | tf_op jit(solution)/shard_map/ppermute | solution.py:319
  49.2 4.4 %collective-permute-start.20 = (f32[32,128]{1,0:T(8,128)S(1)}, f32[32,128]{1,0:T(8,128)S(1)}, u32[]{:S(2)}, u32[]{:S(2)}) collective-permute-start(f32[32,128]{1,0:T(8,128)S(1)} %add.241), channel_id=1, source_target_pairs={{0,7},{1,6},{2,5},{3,4},{4,3},{5,2},{6,1},{7,0},{8,15},{9,14},{10,... | collective-permute-start | bytes 49160 | tf_op jit(solution)/shard_map/ppermute | solution.py:319
  52.2 3.2 %collective-permute-start.19 = (f32[32,128]{1,0:T(8,128)S(1)}, f32[32,128]{1,0:T(8,128)S(1)}, u32[]{:S(2)}, u32[]{:S(2)}) collective-permute-start(f32[32,128]{1,0:T(8,128)S(1)} %add.241), channel_id=1, source_target_pairs={{0,5},{1,4},{2,7},{3,6},{4,1},{5,0},{6,3},{7,2},{8,13},{9,12},{10,... | collective-permute-start | bytes 49160 | tf_op jit(solution)/shard_map/ppermute | solution.py:319
  52.4 3.2 %collective-permute-start.18 = (f32[32,128]{1,0:T(8,128)S(1)}, f32[32,128]{1,0:T(8,128)S(1)}, u32[]{:S(2)}, u32[]{:S(2)}) collective-permute-start(f32[32,128]{1,0:T(8,128)S(1)} %add.241), channel_id=1, source_target_pairs={{0,3},{1,2},{2,1},{3,0},{4,7},{5,6},{6,5},{7,4},{8,11},{9,10},{10,... | collective-permute-start | bytes 49160 | tf_op jit(solution)/shard_map/ppermute | solution.py:319
  55.6 5.0 %collective-permute-start.23 = (f32[32,128]{1,0:T(8,128)S(1)}, f32[32,128]{1,0:T(8,128)S(1)}, u32[]{:S(2)}, u32[]{:S(2)}) collective-permute-start(f32[32,128]{1,0:T(8,128)S(1)} %add_add_fusion), channel_id=1, source_target_pairs={{0,25},{1,24},{2,27},{3,26},{4,29},{5,28},{6,31},{7,30},{8,17},{9,... | collective-permute-start | bytes 49160 | tf_op jit(solution)/shard_map/ppermute | solution.py:319
  57.4 4.2 %collective-permute-start.22 = (f32[32,128]{1,0:T(8,128)S(1)}, f32[32,128]{1,0:T(8,128)S(1)}, u32[]{:S(2)}, u32[]{:S(2)}) collective-permute-start(f32[32,128]{1,0:T(8,128)S(1)} %add_add_fusion), channel_id=1, source_target_pairs={{0,17},{1,16},{2,19},{3,18},{4,21},{5,20},{6,23},{7,22},{8,25},{9,... | collective-permute-start | bytes 49160 | tf_op jit(solution)/shard_map/ppermute | solution.py:319
  57.4 4.2 %collective-permute-start.21 = (f32[32,128]{1,0:T(8,128)S(1)}, f32[32,128]{1,0:T(8,128)S(1)}, u32[]{:S(2)}, u32[]{:S(2)}) collective-permute-start(f32[32,128]{1,0:T(8,128)S(1)} %add_add_fusion), channel_id=1, source_target_pairs={{0,9},{1,8},{2,11},{3,10},{4,13},{5,12},{6,15},{7,14},{8,1},{9,0},... | collective-permute-start | bytes 49160 | tf_op jit(solution)/shard_map/ppermute | solution.py:319
  65.2 12.3 %all-to-all-start = ((f32[32,8,128]{2,1,0:T(8,128)}), f32[32,8,128]{2,1,0:T(8,128)S(1)}, u32[]{:S(2)}, u32[]{:S(2)}) async-start(f32[32,8,128]{2,1,0:T(8,128)} %bitcast.21), calls=%async_computation | async-start | bytes 262144 | tf_op jit(solution)/shard_map/all_to_all | solution.py:335
